TPU v7x, 128 devices: a whole 4x4x4 slice. The times are simulated.
128 devices in a mesh: wide: 32 (over x, z, core), mp: 4 (over y).
Axes of the slice: x: 4, y: 4, z: 4, core: 2. Of those that a mesh axis runs over, the one named last changes fastest.
Arguments:
- points: bfloat16 [131072, 512], P('wide', 'mp'), may hold values from -16 to 16
- mask: int32 [131072], P('wide'), may hold values 0 or 1
- perm: int32 [131072], P('wide'), may hold values from 0 to 131071, as said below
- w_qkv: bfloat16 [3, 512, 512], P(None, None, 'mp'), may hold values from -8 to 8
- w_out: bfloat16 [512, 512], P('mp'), may hold values from -0.25 to 0.25
- w_gate_up: bfloat16 [2, 512, 2048], P(None, None, 'mp'), may hold values from -0.25 to 0.25
- w_down: bfloat16 [2048, 512], P('mp'), may hold values from -0.125 to 0.125
- w_coarse: bfloat16 [2, 3, 512, 512], P(None, None, None, 'mp'), may hold values from -8 to 8
- w_coarse_out: bfloat16 [2, 512, 512], P(None, 'mp'), may hold values from -1.5 to 1.5
Outputs:
- refreshed: float32 [131072, 512], P('wide', 'mp')
Inputs may be any that keep to these rules, and one draw needn't show every extreme that they name: perm is a permutation of the 131072 rows; the 4096 rows of one index of wide send at most 256 rows to the block of any one index, and exactly 256 to some index in every draw.
All inputs are finite; a program needn't handle non-finite values. No bound on the sum of `mask` on one device may be relied on, other than what follows from the above.
Results may differ from a plain program's by a relative error of at most 0.039.
Values may be sent and summed in bfloat16 or wider, within the bound.
A program may use at most 128 MiB of HBM per device.

v0:
```python
import jax
import jax.numpy as jnp
from jax import lax
from jax.sharding import PartitionSpec as P

BALL = 256
HEAD_DIM = 64


def swapped(value, axis, stride):
    return lax.ppermute(value, axis, [(i, i ^ 1 << stride) for i in range(lax.axis_size(axis))])


def rms_norm(values):
    values = values.astype(jnp.float32)
    return values * lax.rsqrt(jnp.mean(values * values, -1, keepdims=True) + 1e-06)


def attend(queries, key_rows, value_rows, allowed):
    count_q = queries.shape[0]
    count_k = key_rows.shape[0]
    q_heads = queries.reshape(count_q, -1, HEAD_DIM)
    k_heads = key_rows.reshape(count_k, -1, HEAD_DIM)
    v_heads = value_rows.reshape(count_k, -1, HEAD_DIM)
    scores = jnp.einsum(
        "qhe,khe->hqk", q_heads, k_heads, preferred_element_type=jnp.float32
    ) * HEAD_DIM ** (-0.5)
    scores = jnp.where(allowed[None], scores, -1e30)
    scores = scores - jnp.max(scores, -1, keepdims=True)
    expo = jnp.exp(scores)
    weights = (expo / jnp.sum(expo, -1, keepdims=True)).astype(jnp.bfloat16)
    mixed_heads = jnp.einsum("hqk,khe->qhe", weights, v_heads, preferred_element_type=jnp.float32)
    return mixed_heads.astype(jnp.bfloat16).reshape(count_q, -1)


def pool_rows(state_rows, row_mask, factor):
    count_rows = state_rows.shape[0] // factor
    weighted = state_rows.reshape(count_rows, factor, -1) * row_mask.reshape(
        count_rows, factor, 1
    ).astype(jnp.float32)
    counted = jnp.sum(row_mask.reshape(count_rows, factor), 1)
    pooled = jnp.sum(weighted, 1) / jnp.maximum(counted, 1).astype(jnp.float32)[:, None]
    return (rms_norm(pooled).astype(jnp.bfloat16), (counted > 0).astype(jnp.int32))


def spread(lifted, factor):
    count_rows, columns = lifted.shape
    return jnp.broadcast_to(lifted[:, None, :], (count_rows, factor, columns)).reshape(
        count_rows * factor, columns
    )


def on_device(points, mask, perm, w_qkv, w_out, w_gate_up, w_down, w_coarse, w_coarse_out):
    rows_dev, width_local = points.shape
    shards = lax.axis_size("wide")
    capacity = 2 * rows_dev // shards
    buffer_size = shards * capacity
    target = perm // rows_dev
    landing = perm % rows_dev
    onehot = (target[:, None] == jnp.arange(shards, dtype=jnp.int32)[None, :]).astype(jnp.int32)
    before = jnp.cumsum(onehot, 0) - onehot
    bucket = target * capacity + jnp.sum(before * onehot, 1)
    send_index = (
        jnp.full((buffer_size,), rows_dev, jnp.int32)
        .at[bucket]
        .set(landing)
        .reshape(shards, capacity)
    )
    send_mask = jnp.zeros((buffer_size,), jnp.int32).at[bucket].set(mask).reshape(shards, capacity)
    column = lax.axis_index("mp") * width_local
    carried = lax.all_gather(points, "mp", axis=1, tiled=True)
    carried_cols = carried.shape[1]
    send_rows = (
        jnp.zeros((buffer_size, carried_cols), carried.dtype)
        .at[bucket]
        .set(carried)
        .reshape(shards, capacity, carried_cols)
    )
    got_rows, got_index, got_mask = (
        lax.all_to_all(send_rows, "wide", split_axis=0, concat_axis=0, tiled=True),
        lax.all_to_all(send_index, "wide", split_axis=0, concat_axis=0, tiled=True),
        lax.all_to_all(send_mask, "wide", split_axis=0, concat_axis=0, tiled=True),
    )
    flat_index = got_index.reshape(buffer_size)
    owned_rows = (
        jnp.zeros((rows_dev, carried_cols), carried.dtype)
        .at[flat_index]
        .set(got_rows.reshape(buffer_size, carried_cols), mode="drop")
    )
    owned_mask = (
        jnp.zeros((rows_dev,), jnp.int32)
        .at[flat_index]
        .set(got_mask.reshape(buffer_size), mode="drop")
    )
    normed = rms_norm(owned_rows).astype(jnp.bfloat16)
    projected = jnp.einsum("pd,tdc->tpc", normed, w_qkv, preferred_element_type=jnp.float32).astype(
        jnp.bfloat16
    )
    ball_count = rows_dev // BALL
    shaped = projected.reshape(3, ball_count, BALL, width_local)
    ball_rows = jnp.arange(BALL, dtype=jnp.int32)
    allowed = (owned_mask.reshape(ball_count, 1, BALL) > 0) | (
        ball_rows[:, None] == ball_rows[None, :]
    )[None]
    mixed_heads = jax.vmap(attend)(shaped[0], shaped[1], shaped[2], allowed).reshape(
        rows_dev, width_local
    )
    head_terms = jnp.dot(mixed_heads, w_out, preferred_element_type=jnp.float32)
    head_total = lax.psum(head_terms.astype(jnp.bfloat16), "mp").astype(jnp.float32)
    state_rows = owned_rows.astype(jnp.float32) + head_total
    own_state = lax.dynamic_slice_in_dim(state_rows, column, width_local, 1)
    level_one, keep_one = pool_rows(state_rows, owned_mask, 4)
    level_two, keep_two = pool_rows(state_rows, owned_mask, 8)
    qkv_one = jnp.einsum(
        "pd,tdc->tpc", level_one, w_coarse[0], preferred_element_type=jnp.float32
    ).astype(jnp.bfloat16)
    qkv_two = jnp.einsum(
        "pd,tdc->tpc", level_two, w_coarse[1], preferred_element_type=jnp.float32
    ).astype(jnp.bfloat16)
    mate_keys_one, mate_values_one, mate_keep_one, mate_keys_two, mate_values_two, mate_keep_two = (
        swapped((qkv_one[1], qkv_one[2], keep_one, qkv_two[1], qkv_two[2], keep_two), "wide", 0)
    )
    pair_keys = jnp.concatenate([qkv_two[1], mate_keys_two], 0)
    pair_values = jnp.concatenate([qkv_two[2], mate_values_two], 0)
    pair_keep = jnp.concatenate([keep_two, mate_keep_two], 0)
    far_keys, far_values, far_keep = swapped((pair_keys, pair_values, pair_keep), "wide", 1)
    rows_one = rows_dev // 4
    rows_two = rows_dev // 8
    keys_one = jnp.concatenate([qkv_one[1], mate_keys_one], 0)
    values_one = jnp.concatenate([qkv_one[2], mate_values_one], 0)
    flags_one = jnp.concatenate([keep_one, mate_keep_one], 0)
    allowed_one = (flags_one > 0)[None, :] | (
        jnp.arange(2 * rows_one, dtype=jnp.int32)[None, :]
        == jnp.arange(rows_one, dtype=jnp.int32)[:, None]
    )
    out_one = attend(qkv_one[0], keys_one, values_one, allowed_one)
    keys_two = jnp.concatenate([pair_keys, far_keys], 0)
    values_two = jnp.concatenate([pair_values, far_values], 0)
    flags_two = jnp.concatenate([pair_keep, far_keep], 0)
    allowed_two = (flags_two > 0)[None, :] | (
        jnp.arange(4 * rows_two, dtype=jnp.int32)[None, :]
        == jnp.arange(rows_two, dtype=jnp.int32)[:, None]
    )
    out_two = attend(qkv_two[0], keys_two, values_two, allowed_two)
    lift_one = jnp.dot(out_one, w_coarse_out[0], preferred_element_type=jnp.float32)
    lift_two = jnp.dot(out_two, w_coarse_out[1], preferred_element_type=jnp.float32)
    normed_state = rms_norm(state_rows).astype(jnp.bfloat16)
    gate_up = jnp.einsum("pd,tdf->tpf", normed_state, w_gate_up, preferred_element_type=jnp.float32)
    activated = (jax.nn.silu(gate_up[0]) * gate_up[1]).astype(jnp.bfloat16)
    terms_all = (
        jnp.dot(activated, w_down, preferred_element_type=jnp.float32)
        + spread(lift_one, 4)
        + spread(lift_two, 8)
    )
    update = lax.psum_scatter(
        terms_all.astype(jnp.bfloat16), "mp", scatter_dimension=1, tiled=True
    ).astype(jnp.float32)
    result = own_state + update
    back_rows = jnp.take(result, flat_index, axis=0, mode="fill", fill_value=0).reshape(
        shards, capacity, width_local
    )
    returned = lax.all_to_all(
        back_rows.astype(jnp.bfloat16), "wide", split_axis=0, concat_axis=0, tiled=True
    ).astype(back_rows.dtype)
    return returned.reshape(buffer_size, width_local)[bucket]


def solution(mesh):
    placed = (
        P("wide", "mp"),
        P("wide"),
        P("wide"),
        P(None, None, "mp"),
        P("mp", None),
        P(None, None, "mp"),
        P("mp", None),
        P(None, None, None, "mp"),
        P(None, "mp", None),
    )
    return jax.shard_map(
        on_device, mesh=mesh, in_specs=placed, out_specs=P("wide", "mp"), check_vma=False
    )
```

profile of v0, /device:TPU:1, one launch (start us, length us, event | category | flops | bytes accessed | tf_op | source)
XLA Modules:
  0.0 636.9 jit_solution(13883061653342103385)
XLA Ops:
  8.1 9.2 %reduce-window.6 = s32[32,32,128]{2,1,0:T(8,128)S(1)} reduce-window(s32[32,32,128]{2,1,0:T(8,128)S(1)} %fusion.69, s32[]{:T(128)} %constant.35.clone.1), window={size=1x1x128 pad=0_0x0_0x127_0}, to_apply=%region_0.1 | reduce-window | flops 16646144 | bytes 1048580 | tf_op jit(solution)/shard_map/reduce-window
  19.5 16.1 %scatter_custom_fusion = s32[8192]{0:T(1024)} fusion(s32[4096]{0:T(1024)S(1)} %get-tuple-element.6, s32[4096]{0:T(1024)S(1)} %get-tuple-element.28, s32[]{:T(128)} %constant.31.clone.1), kind=kCustom, calls=%fused_computation.137 | custom fusion | bytes 32772 | tf_op jit(solution)/shard_map/scatter | solution.py:66
  35.6 9.4 %all-to-all-start = ((s32[32,1,256]{2,1,0:T(1,128)}), s32[32,1,256]{2,1,0:T(1,128)S(1)}, u32[]{:S(2)}, u32[]{:S(2)}) async-start(s32[32,1,256]{2,1,0:T(1,128)} %bitcast.2), calls=%async_computation | async-start | bytes 65536 | tf_op jit(solution)/shard_map/all_to_all | solution.py:81
  45.0 16.3 %scatter_custom_fusion.3 = s32[8192]{0:T(1024)} fusion(s32[4096]{0:T(1024)S(1)} %get-tuple-element.6, s32[4096]{0:T(1024)} %param.10, s32[]{:T(128)} %constant.35.clone.1), kind=kCustom, calls=%fused_computation.133 | custom fusion | bytes 33280 | tf_op jit(solution)/shard_map/scatter | solution.py:69
  61.3 7.4 %all-to-all-start.2 = ((s32[32,1,256]{2,1,0:T(1,128)}), s32[32,1,256]{2,1,0:T(1,128)S(1)}, u32[]{:S(2)}, u32[]{:S(2)}) async-start(s32[32,1,256]{2,1,0:T(1,128)} %bitcast.9), calls=%async_computation.2 | async-start | bytes 65536 | tf_op jit(solution)/shard_map/all_to_all | solution.py:82
  68.7 23.5 %scatter_custom_fusion.1 = bf16[8192,512]{1,0:T(8,128)(2,1)} fusion(s32[4096]{0:T(1024)S(1)} %get-tuple-element.6, bf16[4096,512]{1,0:T(8,128)(2,1)} %all-gather.2.cloned.1.call-done, bf16[]{:T(256)} %constant.46.clone.1), kind=kCustom, calls=%fused_computation.58 | custom fusion | bytes 8389120 | tf_op jit(solution)/shard_map/scatter | solution.py:76
  92.1 7.4 %all-to-all-start.1 = ((bf16[32,256,512]{2,1,0:T(8,128)(2,1)}), bf16[32,256,512]{2,1,0:T(8,128)(2,1)}, u32[]{:S(2)}, u32[]{:S(2)}) async-start(bf16[32,256,512]{2,1,0:T(8,128)(2,1)} %bitcast.134), calls=%async_computation.1 | async-start | bytes 16777216 | tf_op jit(solution)/shard_map/all_to_all | solution.py:80
  100.0 30.5 %scatter_custom_fusion.4 = s32[4096]{0:T(1024)S(1)} fusion(s32[8192]{0:T(1024)S(1)} %bitcast.152, s32[8192]{0:T(1024)S(1)} %bitcast.161, s32[]{:T(128)} %constant.35.clone.1), kind=kCustom, calls=%fused_computation.144 | custom fusion | bytes 16388 | tf_op jit(solution)/shard_map/scatter | solution.py:93
  130.5 2.0 broadcast_or_fusion
  132.5 75.6 %all-to-all-done.1 = bf16[32,256,512]{2,1,0:T(8,128)(2,1)} async-done(((bf16[32,256,512]{2,1,0:T(8,128)(2,1)}), bf16[32,256,512]{2,1,0:T(8,128)(2,1)}, u32[]{:S(2)}, u32[]{:S(2)}) %all-to-all-start.1) | async-done | bytes 8388640 | tf_op jit(solution)/shard_map/all_to_all | solution.py:80
  208.1 38.5 %scatter_custom_fusion.2 = bf16[4096,512]{1,0:T(8,128)(2,1)} fusion(s32[8192]{0:T(1024)S(1)} %bitcast.153, bf16[8192,512]{1,0:T(8,128)(2,1)} %bitcast.6, bf16[]{:T(256)} %constant.46.clone.1), kind=kCustom, calls=%fused_computation.73 | custom fusion | bytes 4194816 | tf_op jit(solution)/shard_map/scatter | solution.py:88
  246.6 3.1 fusion.4
  249.7 4.6 fusion.17
  255.5 5.0 reshape.403
  260.5 1.8 reshape.402
  262.3 1.8 reshape.401
  264.1 3.5 fusion.36
  267.6 4.6 fusion.109
  272.2 5.0 fusion.47
  278.3 3.2 convolution_convert_fusion
  281.5 9.9 %reduce-scatter.4.cloned.1.call-start = ((), (), s32[]{:S(2)}) async-start(), calls=%async_computation.7 | async-start | bytes 5242880
  294.3 5.5 collective-permute-start.5
  301.0 12.1 %collective-permute-start.6 = (s32[1024]{0:T(1024)S(1)}, s32[1024]{0:T(1024)S(1)}, u32[]{:S(2)}, u32[]{:S(2)}) collective-permute-start(s32[1024]{0:T(1024)S(1)} %pad_add_fusion), channel_id=1, source_target_pairs={{0,8},{4,12},{8,0},{12,4},{16,24},{20,28},{24,16},{28,20},{32,40},... | collective-permute-start | bytes 12296 | tf_op jit(solution)/shard_map/ppermute | solution.py:11
  314.4 1.5 fusion.32
  315.9 73.8 %all-reduce.2.cloned.1.call-done = bf16[4096,512]{1,0:T(8,128)(2,1)} async-done(((bf16[4096,512]{1,0:T(8,128)(2,1)}), bf16[4096,512]{1,0:T(8,128)(2,1)}) %all-reduce.2.cloned.1.call-update) | async-done | bytes 4194320 | tf_op jit(solution)/shard_map/psum | solution.py:109
  389.7 8.0 %multiply_reduce_fusion.1 = (f32[4096]{0:T(1024)S(1)}, f32[4096,512]{1,0:T(8,128)}) fusion(bf16[4096,512]{1,0:T(8,128)(2,1)} %all-reduce.2.cloned.1.call-done, bf16[4096,512]{1,0:T(8,128)(2,1)} %scatter_custom_fusion.2), kind=kLoop, calls=%fused_computation.36 | loop fusion | flops 10481664 | bytes 16793600 | tf_op jit(solution)/shard_map/reduce_sum | solution.py:16
  397.7 9.8 %reshape.323 = f32[1024,4,512]{2,1,0:T(4,128)} reshape(f32[4096,512]{1,0:T(8,128)} %get-tuple-element.8) | data formatting | bytes 16777216 | tf_op jit(solution)/shard_map/reshape | solution.py:38
  407.5 8.0 %multiply_reduce_fusion = f32[1024,512]{1,0:T(8,128)S(1)} fusion(f32[1024,4,512]{2,1,0:T(4,128)} %reshape.323, f32[1024,4]{1,0:T(8,128)} %get-tuple-element.19), kind=kLoop, calls=%fused_computation.34 | loop fusion | flops 3670016 | bytes 10502144 | tf_op jit(solution)/shard_map/reduce_sum | solution.py:42
  415.9 1.6 fusion.52
  419.4 3.2 fusion.9
  424.9 8.2 %convolution_bitcast_fusion = f32[2,4096,512]{2,1,0:T(8,128)} fusion(bf16[2,512,512]{2,1,0:T(8,128)(2,1)S(1)} %copy-done, f32[4096]{0:T(1024)S(1)} %add_rsqrt_fusion, bf16[4096,512]{1,0:T(8,128)(2,1)S(1)} %copy-done.2, bf16[4096,512]{1,0:T(8,128)(2,1)S(1)} %copy-done.3), kind=kOutput, calls=%fused_computation.17 | convolution fusion | flops 4305453056 | bytes 26230784 | tf_op jit(solution)/shard_map/pd,tdf->tpf/dot_general | solution.py:148
  433.9 1.3 collective-permute-start.8
  437.0 9.9 %fusion.110 = (f32[2,1024]{1,0:T(2,128)S(1)}, f32[2,1024,2048]{2,1,0:T(8,128)}) fusion(pred[1024,2048]{1,0:T(8,128)(4,1)S(1)} %fusion.12, bf16[1024,2,64]{0,2,1:T(8,128)(2,1)} %bitcast.150, bf16[1024,2,64]{0,2,1:T(8,128)(2,1)} %bitcast.162, bf16[1024,2,64]{0,2,1:T(8,128)(2,1)S(1)} %bitcast.149), kind=kOutput, calls=%fused_computation.178 | convolution fusion | flops 554698752 | bytes 19668992 | tf_op jit(solution)/shard_map/sub | solution.py:29
  447.0 8.6 %fusion.50 = bf16[2,64,1024]{2,1,0:T(8,128)(2,1)S(1)} fusion(f32[2,1024,2048]{2,1,0:T(8,128)} %get-tuple-element.33, f32[2,1024]{1,0:T(2,128)S(1)} %get-tuple-element.32, bf16[1024,2,64]{0,2,1:T(8,128)(2,1)} %bitcast.23, bf16[1024,2,64]{0,2,1:T(8,128)(2,1)S(1)} %bitcast.148), kind=kOutput, calls=%fused_computation.79 | convolution fusion | flops 546439168 | bytes 17571840 | tf_op jit(solution)/shard_map/hqk,khe->qhe/dot_general | solution.py:32
  456.1 4.6 broadcast_in_dim.61
  460.7 10.1 %reshape.326 = f32[4096,512]{1,0:T(8,128)} reshape(f32[1024,4,512]{2,1,0:T(4,128)} %broadcast_in_dim.61) | data formatting | bytes 16777216 | tf_op jit(solution)/shard_map/reshape | solution.py:48
  470.9 7.2 %fusion.111 = (f32[2,512]{1,0:T(2,128)S(1)}, f32[2,512,2048]{2,1,0:T(8,128)}) fusion(pred[512,2048]{1,0:T(8,128)(4,1)S(1)} %copy-done.5, bf16[512,2,64]{0,2,1:T(8,128)(2,1)S(1)} %bitcast.159, bf16[1024,2,64]{0,2,1:T(8,128)(2,1)} %bitcast.45, bf16[512,2,64]{0,2,1:T(8,128)(2,1)S(1)} %bitcast.156, bf16[512,2,64]{0,2,1:T(8,128)(2,1)S(1)} %bitcast.158), kind=kOutput, calls=%fused_computation.179 | convolution fusion | flops 278398976 | bytes 10096640 | tf_op jit(solution)/shard_map/sub | solution.py:29
  478.1 5.1 fusion.51
  484.0 9.0 %fusion.8 = bf16[4096,512]{1,0:T(8,128)(2,1)} fusion(f32[4096,512]{1,0:T(8,128)S(1)} %copy-done.4, bf16[512,512]{1,0:T(8,128)(2,1)S(1)} %copy-done.22, f32[512,512]{1,0:T(8,128)S(1)} %fusion.72, f32[2,4096,512]{2,1,0:T(8,128)} %convolution_bitcast_fusion), kind=kOutput, calls=%fused_computation.25 | convolution fusion | flops 2166358016 | bytes 30932992 | tf_op jit(solution)/shard_map/dot_general | solution.py:151
  493.0 6.4 %copy.43 = bf16[4096,512]{0,1:T(8,128)(2,1)} copy(bf16[4096,512]{1,0:T(8,128)(2,1)} %fusion.8) | data formatting | bytes 8388608
  499.4 47.2 %reduce-scatter.4.cloned.1.call-done = bf16[128,4096]{1,0:T(8,128)(2,1)} async-done(((bf16[512,4096]{1,0:T(8,128)(2,1)}), bf16[128,4096]{1,0:T(8,128)(2,1)}) %reduce-scatter.4.cloned.1.call-update) | async-done | bytes 1048592
  546.6 1.6 copy.44
  548.3 1.8 convert_add_fusion.1
  550.1 24.0 %gather_fusion = bf16[8192,128]{1,0:T(8,128)(2,1)S(1)} fusion(bf16[4096,128]{1,0:T(8,128)(2,1)S(1)} %convert_add_fusion.1, s32[8192]{0:T(1024)S(1)} %broadcast_clamp_fusion), kind=kCustom, calls=%fused_computation | custom fusion | bytes 4227072 | tf_op jit(solution)/shard_map/jit(_take)/gather | solution.py:159
  574.1 1.4 select_convert_fusion
  575.6 35.6 %all_to_all.28 = bf16[32,256,128]{2,1,0:T(8,128)(2,1)S(1)} all-to-all(bf16[32,256,128]{2,1,0:T(8,128)(2,1)S(1)} %select_convert_fusion), channel_id=1, replica_groups=mesh['wide'=32,'mp'=4] {'wide'}, dimensions={0} | all-to-all | bytes 4194304 | tf_op jit(solution)/shard_map/all_to_all | solution.py:162
  611.1 2.3 bitcast_convert_fusion
  613.4 16.5 %gather_fusion.1 = f32[4096,128]{1,0:T(8,128)} fusion(f32[8192,128]{1,0:T(8,128)} %bitcast_convert_fusion, s32[4096]{0:T(1024)S(1)} %copy-done.21), kind=kCustom, calls=%fused_computation.1 | custom fusion | bytes 4210688 | tf_op jit(solution)/shard_map/gather | solution.py:165
  (119 shorter events, 20.1 us)
Async XLA Ops:
  6.5 418.4 %copy-start = (bf16[2,512,512]{2,1,0:T(8,128)(2,1)S(1)}, bf16[2,512,512]{2,1,0:T(8,128)(2,1)}, u32[]{:S(2)}) copy-start(bf16[2,512,512]{2,1,0:T(8,128)(2,1)} %param.14) | copy-start | bytes 3145732
  6.5 62.1 %all-gather.2.cloned.1.call-start = ((), (), s32[]{:S(2)}) async-start(), calls=%async_computation.5 | async-start | bytes 5242880 | tf_op jit(solution)/shard_map/all_gather | solution.py:71
  35.6 25.7 %all-to-all-start = ((s32[32,1,256]{2,1,0:T(1,128)}), s32[32,1,256]{2,1,0:T(1,128)S(1)}, u32[]{:S(2)}, u32[]{:S(2)}) async-start(s32[32,1,256]{2,1,0:T(1,128)} %bitcast.2), calls=%async_computation | async-start | bytes 65536 | tf_op jit(solution)/shard_map/all_to_all | solution.py:81
  61.3 30.9 %all-to-all-start.2 = ((s32[32,1,256]{2,1,0:T(1,128)}), s32[32,1,256]{2,1,0:T(1,128)S(1)}, u32[]{:S(2)}, u32[]{:S(2)}) async-start(s32[32,1,256]{2,1,0:T(1,128)} %bitcast.9), calls=%async_computation.2 | async-start | bytes 65536 | tf_op jit(solution)/shard_map/all_to_all | solution.py:82
  92.1 116.0 %all-to-all-start.1 = ((bf16[32,256,512]{2,1,0:T(8,128)(2,1)}), bf16[32,256,512]{2,1,0:T(8,128)(2,1)}, u32[]{:S(2)}, u32[]{:S(2)}) async-start(bf16[32,256,512]{2,1,0:T(8,128)(2,1)} %bitcast.134), calls=%async_computation.1 | async-start | bytes 16777216 | tf_op jit(solution)/shard_map/all_to_all | solution.py:80
  99.6 150.2 %copy-start.23 = (bf16[3,512,128]{2,1,0:T(8,128)(2,1)S(1)}, bf16[3,512,128]{2,1,0:T(8,128)(2,1)}, u32[]{:S(2)}) copy-start(bf16[3,512,128]{2,1,0:T(8,128)(2,1)} %param.12) | copy-start | bytes 1179652
  99.6 290.1 %all-reduce.2.cloned.1.call-start = ((), (), s32[]{:S(2)}) async-start(), calls=%async_computation.6 | async-start | bytes 8388608 | tf_op jit(solution)/shard_map/psum | solution.py:109
  262.3 5.3 copy-start.6
  272.2 6.1 copy-start.13
  277.2 14.3 %copy-start.7 = (bf16[2,3,512,128]{3,2,1,0:T(8,128)(2,1)S(1)}, bf16[2,3,512,128]{3,2,1,0:T(8,128)(2,1)}, u32[]{:S(2)}) copy-start(bf16[2,3,512,128]{3,2,1,0:T(8,128)(2,1)} %param.16) | copy-start | bytes 2359300
  281.5 265.1 %reduce-scatter.4.cloned.1.call-start = ((), (), s32[]{:S(2)}) async-start(), calls=%async_computation.7 | async-start | bytes 5242880
  294.3 6.6 %collective-permute-start.5 = (s32[512]{0:T(512)S(1)}, s32[512]{0:T(512)S(1)}, u32[]{:S(2)}, u32[]{:S(2)}) collective-permute-start(s32[512]{0:T(512)S(1)} %compare_convert_fusion.1), channel_id=1, source_target_pairs={{0,4},{4,0},{8,12},{12,8},{16,20},{20,16},{24,28},{28,24},{32,36},... | collective-permute-start | bytes 6152 | tf_op jit(solution)/shard_map/ppermute | solution.py:11
  300.8 12.2 %collective-permute-start.1 = (s32[1024]{0:T(1024)S(1)}, s32[1024]{0:T(1024)S(1)}, u32[]{:S(2)}, u32[]{:S(2)}) collective-permute-start(s32[1024]{0:T(1024)S(1)} %compare_convert_fusion), channel_id=1, source_target_pairs={{0,4},{4,0},{8,12},{12,8},{16,20},{20,16},{24,28},{28,24},{32,36},... | collective-permute-start | bytes 12296 | tf_op jit(solution)/shard_map/ppermute | solution.py:11
  301.0 13.5 %collective-permute-start.6 = (s32[1024]{0:T(1024)S(1)}, s32[1024]{0:T(1024)S(1)}, u32[]{:S(2)}, u32[]{:S(2)}) collective-permute-start(s32[1024]{0:T(1024)S(1)} %pad_add_fusion), channel_id=1, source_target_pairs={{0,8},{4,12},{8,0},{12,4},{16,24},{20,28},{24,16},{28,20},{32,40},... | collective-permute-start | bytes 12296 | tf_op jit(solution)/shard_map/ppermute | solution.py:11
  407.5 8.4 %copy-start.9 = (bf16[1,3,512,128]{2,3,1,0:T(8,128)(2,1)S(1)}, bf16[1,3,512,128]{2,3,1,0:T(8,128)(2,1)}, u32[]{:S(2)}) copy-start(bf16[1,3,512,128]{2,3,1,0:T(8,128)(2,1)} %copy.46) | copy-start | bytes 1179652
  415.5 3.8 copy-start.2
  415.5 3.8 copy-start.3
  417.5 5.3 copy-start.8
  418.7 17.6 %collective-permute-start.2 = (bf16[1024,128]{0,1:T(8,128)(2,1)S(1)}, bf16[1024,128]{0,1:T(8,128)(2,1)S(1)}, u32[]{:S(2)}, u32[]{:S(2)}) collective-permute-start(bf16[1024,128]{0,1:T(8,128)(2,1)S(1)} %get-tuple-element.16), channel_id=1, source_target_pairs={{0,4},{4,0},{8,12},{12,8},{16,20},{20,16},{24,28},{28,24},{32,36},... | collective-permute-start | bytes 786440 | tf_op jit(solution)/shard_map/ppermute | solution.py:11
  419.3 27.6 %collective-permute-start = (bf16[1024,128]{0,1:T(8,128)(2,1)}, bf16[1024,128]{0,1:T(8,128)(2,1)}, u32[]{:S(2)}, u32[]{:S(2)}) collective-permute-start(bf16[1024,128]{0,1:T(8,128)(2,1)} %get-tuple-element.15), channel_id=1, source_target_pairs={{0,4},{4,0},{8,12},{12,8},{16,20},{20,16},{24,28},{28,24},{32,36},... | collective-permute-start | bytes 786440 | tf_op jit(solution)/shard_map/ppermute | solution.py:11
  424.2 8.9 %collective-permute-start.7 = (bf16[512,128]{0,1:T(8,128)(2,1)S(1)}, bf16[512,128]{0,1:T(8,128)(2,1)S(1)}, u32[]{:S(2)}, u32[]{:S(2)}) collective-permute-start(bf16[512,128]{0,1:T(8,128)(2,1)S(1)} %get-tuple-element.23), channel_id=1, source_target_pairs={{0,4},{4,0},{8,12},{12,8},{16,20},{20,16},{24,28},{28,24},{32,36},... | collective-permute-start | bytes 393224 | tf_op jit(solution)/shard_map/ppermute | solution.py:11
  424.9 10.2 %collective-permute-start.3 = (bf16[512,128]{0,1:T(8,128)(2,1)S(1)}, bf16[512,128]{0,1:T(8,128)(2,1)S(1)}, u32[]{:S(2)}, u32[]{:S(2)}) collective-permute-start(bf16[512,128]{0,1:T(8,128)(2,1)S(1)} %get-tuple-element.22), channel_id=1, source_target_pairs={{0,4},{4,0},{8,12},{12,8},{16,20},{20,16},{24,28},{28,24},{32,36},... | collective-permute-start | bytes 393224 | tf_op jit(solution)/shard_map/ppermute | solution.py:11
  424.9 12.1 %copy-start.12 = (bf16[1,1024,128]{1,2,0:T(8,128)(2,1)S(1)}, bf16[1,1024,128]{1,2,0:T(8,128)(2,1)}, u32[]{:S(2)}) copy-start(bf16[1,1024,128]{1,2,0:T(8,128)(2,1)} %get-tuple-element.17) | copy-start | bytes 786436
  433.1 3.2 copy-start.16
  433.9 37.0 %collective-permute-start.8 = (bf16[1024,128]{0,1:T(8,128)(2,1)}, bf16[1024,128]{0,1:T(8,128)(2,1)}, u32[]{:S(2)}, u32[]{:S(2)}) collective-permute-start(bf16[1024,128]{0,1:T(8,128)(2,1)} %pad_maximum_fusion.9), channel_id=1, source_target_pairs={{0,8},{4,12},{8,0},{12,4},{16,24},{20,28},{24,16},{28,20},{32,40},... | collective-permute-start | bytes 786440 | tf_op jit(solution)/shard_map/ppermute | solution.py:11
  435.1 1.1 copy-start.14
  435.9 42.2 %collective-permute-start.4 = (bf16[1024,128]{0,1:T(8,128)(2,1)}, bf16[1024,128]{0,1:T(8,128)(2,1)}, u32[]{:S(2)}, u32[]{:S(2)}) collective-permute-start(bf16[1024,128]{0,1:T(8,128)(2,1)} %pad_maximum_fusion.8), channel_id=1, source_target_pairs={{0,8},{4,12},{8,0},{12,4},{16,24},{20,28},{24,16},{28,20},{32,40},... | collective-permute-start | bytes 786440 | tf_op jit(solution)/shard_map/ppermute | solution.py:11
  436.3 0.7 copy-start.24
  437.0 10.0 %copy-start.11 = (bf16[1,1024,128]{1,2,0:T(8,128)(2,1)S(1)}, bf16[1,1024,128]{1,2,0:T(8,128)(2,1)}, u32[]{:S(2)}) copy-start(bf16[1,1024,128]{1,2,0:T(8,128)(2,1)} %get-tuple-element.14) | copy-start | bytes 786436
  446.9 8.7 %copy-start.10 = (bf16[2,128,512]{2,1,0:T(8,128)(2,1)S(1)}, bf16[2,128,512]{2,1,0:T(8,128)(2,1)}, u32[]{:S(2)}) copy-start(bf16[2,128,512]{2,1,0:T(8,128)(2,1)} %param.17) | copy-start | bytes 786436
  460.7 10.1 %copy-start.5 = (pred[512,2048]{1,0:T(8,128)(4,1)S(1)}, pred[512,2048]{1,0:T(8,128)(4,1)}, u32[]{:S(2)}) copy-start(pred[512,2048]{1,0:T(8,128)(4,1)} %fusion.32) | copy-start | bytes 3145732
  460.7 10.1 %copy-start.17 = (bf16[512,128]{0,1:T(8,128)(2,1)S(1)}, bf16[512,128]{0,1:T(8,128)(2,1)}, u32[]{:S(2)}) copy-start(bf16[512,128]{0,1:T(8,128)(2,1)} %copy-done.16) | copy-start | bytes 393220
  460.7 10.1 %copy-start.19 = (bf16[1,512,128]{1,2,0:T(8,128)(2,1)S(1)}, bf16[1,512,128]{1,2,0:T(8,128)(2,1)}, u32[]{:S(2)}) copy-start(bf16[1,512,128]{1,2,0:T(8,128)(2,1)} %get-tuple-element.24) | copy-start | bytes 393220
  460.7 10.1 %copy-start.20 = (bf16[1,512,128]{1,2,0:T(8,128)(2,1)S(1)}, bf16[1,512,128]{1,2,0:T(8,128)(2,1)}, u32[]{:S(2)}) copy-start(bf16[1,512,128]{1,2,0:T(8,128)(2,1)} %get-tuple-element.25) | copy-start | bytes 393220
  470.8 7.2 %copy-start.15 = (bf16[512,128]{0,1:T(8,128)(2,1)S(1)}, bf16[512,128]{0,1:T(8,128)(2,1)}, u32[]{:S(2)}) copy-start(bf16[512,128]{0,1:T(8,128)(2,1)} %copy-done.14) | copy-start | bytes 393220
  470.8 7.2 %copy-start.18 = (bf16[1,512,128]{1,2,0:T(8,128)(2,1)S(1)}, bf16[1,512,128]{1,2,0:T(8,128)(2,1)}, u32[]{:S(2)}) copy-start(bf16[1,512,128]{1,2,0:T(8,128)(2,1)} %get-tuple-element.21) | copy-start | bytes 393220
  478.1 5.8 copy-start.4
  478.1 5.9 copy-start.22
  574.1 39.3 %copy-start.21 = (s32[4096]{0:T(1024)S(1)}, s32[4096]{0:T(1024)}, u32[]{:S(2)}) copy-start(s32[4096]{0:T(1024)} %get-tuple-element.5) | copy-start | bytes 49156
  613.4 16.5 %copy-start.1 = (bf16[2,512,512]{2,1,0:T(8,128)(2,1)S(1)}, bf16[2,512,512]{2,1,0:T(8,128)(2,1)}, u32[]{:S(2)}) copy-start(bf16[2,512,512]{2,1,0:T(8,128)(2,1)} %param.14) | copy-start | bytes 3145732
Sparse Core Ops, SparseCore 0:
  9.0 54.3 all-gather.1
  281.7 108.0 all-reduce.1
  499.5 47.0 reduce-scatter.3
where the time goes:
time: 646 us; the launch traced here: 637 us
  local copies, waits for them, and re-layouts  215 us (33%)
  waiting for transfers between devices  198 us (31%)
  matrix products  67.2 us (10%)
  starting transfers between devices  55.2 us (9%)
  other arithmetic  51.9 us (8%)
  blocking collectives  35.6 us (6%)
  between operations  14.1 us (2%)
    all_to_all x1, waiting for transfers between devices, on_device(): lax.all_to_all(send_rows, 'wide', split_axis=0, concat_axis=0, tiled=True)  75.6 us
    psum x1, waiting for transfers between devices, on_device(): lax.psum(head_terms.astype(jnp.bfloat16), 'mp').astype(jnp.float32)  73.8 us
    unnamed x4, waiting for transfers between devices  48 us
    scatter x1, local copies, waits for them, and re-layouts, on_device(): owned_rows = jnp.zeros((rows_dev, carried_cols), carried.dtype).at[flat_i...  38.5 us
    all_to_all x1, blocking collectives, on_device(): lax.all_to_all(back_rows.astype(jnp.bfloat16), 'wide', split_axis=0, conc...  35.6 us
    scatter x1, local copies, waits for them, and re-layouts, on_device(): owned_mask = jnp.zeros((rows_dev,), jnp.int32).at[flat_index].set(got_mas...  30.5 us
    gather x1, local copies, waits for them, and re-layouts, on_device(): jnp.take(result, flat_index, axis=0, mode='fill', fill_value=0)  24 us
    scatter x1, local copies, waits for them, and re-layouts, on_device(): send_rows = jnp.zeros((buffer_size, carried_cols), carried.dtype).at[buck...  23.5 us
  transfers between devices with their start and end apart: 15, of which 4 were waited for; matrix products, arithmetic and copies ran while one was open for 25% of the time, Pallas kernels for 0%

commit v1 on v0

v1 whole, which is shorter than its diff:
```python
import functools

import jax
import jax.numpy as jnp
from jax import lax
from jax.experimental import pallas as pl
from jax.experimental.pallas import tpu as pltpu
from jax.sharding import PartitionSpec as P

BALL = 256
WIDE = 32
MP = 4
ROWS = 4096
CAP = 256
SLOTS = WIDE * CAP
QUARTER = ROWS // MP
WIDTH = 512
LOCAL = WIDTH // MP
HIDDEN = 2048
ONE = QUARTER // 4
TWO = QUARTER // 8
COARSE = ONE + TWO
F32 = jnp.float32
BF16 = jnp.bfloat16
I32 = jnp.int32
MESH = pl.DeviceIdType.MESH
ANY = pl.BlockSpec(memory_space=pl.ANY)
VMEM = pl.BlockSpec(memory_space=pltpu.VMEM)
SMEM = pl.BlockSpec(memory_space=pltpu.SMEM)
LIMIT = 56 * 1024 * 1024


def shape(dims, kind):
    return jax.ShapeDtypeStruct(dims, kind)


def params(collective=None):
    if collective is None:
        return pltpu.CompilerParams(vmem_limit_bytes=LIMIT)
    return pltpu.CompilerParams(
        vmem_limit_bytes=LIMIT, collective_id=collective, has_side_effects=True
    )


def dot(a, b):
    return jnp.dot(a, b, preferred_element_type=F32)


def dot_t(a, b):
    return lax.dot_general(a, b, (((1,), (1,)), ((), ())), preferred_element_type=F32)


def norm(values):
    return values * lax.rsqrt(jnp.mean(values * values, -1, keepdims=True) + 1e-06)


def rank_kernel(perm_ref, mask_ref, slot_ref, code_ref):
    perm = perm_ref[...]
    target = perm >> 12
    code_ref[...] = (perm & (ROWS - 1)) * 2 + mask_ref[...]
    rows = lax.broadcasted_iota(I32, (256, 256), 0)
    cols = lax.broadcasted_iota(I32, (256, 256), 1)
    upper = jnp.where(rows < cols, 1.0, 0.0).astype(BF16)
    which = lax.broadcasted_iota(I32, (WIDE, 256), 0)
    carry = jnp.zeros((WIDE, 1), F32)
    for c in range(ROWS // 256):
        hot = jnp.where(which == target[c : c + 1, :], 1.0, 0.0)
        before = dot(hot.astype(BF16), upper) + carry
        rank = jnp.sum(hot * before, 0, keepdims=True)
        slot_ref[c : c + 1, :] = target[c : c + 1, :] * CAP + rank.astype(I32)
        carry = carry + jnp.sum(hot, 1, keepdims=True)


def widen(src, dst, rows):
    @pl.loop(0, rows // 256)
    def _(i):
        at = pl.ds(pl.multiple_of(i * 256, 256), 256)
        dst[at, :] = src[at, :].astype(dst.dtype)


UNROLL = 16


def pack_kernel(slot_ref, code_ref, points_ref, none_ref, rows_ref, codes_ref, wide, packed):
    pltpu.sync_copy(none_ref, codes_ref)
    widen(points_ref, wide, ROWS)

    @pl.loop(0, SLOTS // 256)
    def _(i):
        packed[pl.ds(pl.multiple_of(i * 256, 256), 256), :] = jnp.zeros((256, LOCAL), F32)

    @pl.loop(0, ROWS // UNROLL)
    def _(i):
        base = i * UNROLL
        slots = [slot_ref[base + u] for u in range(UNROLL)]
        lines = [wide[pl.ds(base + u, 1), :] for u in range(UNROLL)]
        for u in range(UNROLL):
            packed[pl.ds(slots[u], 1), :] = lines[u]
        codes = [code_ref[base + u] for u in range(UNROLL)]
        for u in range(UNROLL):
            codes_ref[slots[u]] = codes[u]

    widen(packed, rows_ref, SLOTS)


def unpack_kernel(code_ref, got_ref, rows_ref, mask_ref, wide, owned):
    widen(got_ref, wide, SLOTS)

    @pl.loop(0, SLOTS // UNROLL)
    def _(i):
        base = i * UNROLL
        codes = [code_ref[base + u] for u in range(UNROLL)]
        lines = [wide[pl.ds(base + u, 1), :] for u in range(UNROLL)]
        for u in range(UNROLL):
            owned[pl.ds(codes[u] >> 1, 1), :] = lines[u]
        for u in range(UNROLL):
            mask_ref[codes[u] >> 1] = codes[u] & 1

    widen(owned, rows_ref, ROWS)


def repack_kernel(code_ref, rows_ref, out_ref, wide, packed):
    widen(rows_ref, wide, ROWS)

    @pl.loop(0, SLOTS // UNROLL)
    def _(i):
        base = i * UNROLL
        lines = [wide[pl.ds(code_ref[base + u] >> 1, 1), :] for u in range(UNROLL)]
        for u in range(UNROLL):
            packed[pl.ds(base + u, 1), :] = lines[u]

    widen(packed, out_ref, SLOTS)


def finish_kernel(slot_ref, got_ref, out_ref, wide):
    widen(got_ref, wide, SLOTS)

    @pl.loop(0, ROWS // UNROLL)
    def _(i):
        base = i * UNROLL
        lines = [wide[pl.ds(slot_ref[base + u], 1), :] for u in range(UNROLL)]
        for u in range(UNROLL):
            out_ref[pl.ds(base + u, 1), :] = lines[u]


def greet(axis, size):
    me = lax.axis_index(axis)
    barrier = pltpu.get_barrier_semaphore()

    @pl.loop(1, size)
    def _(k):
        pl.semaphore_signal(
            barrier, inc=1, device_id={axis: lax.rem(me + k, size)}, device_id_type=MESH
        )

    pl.semaphore_wait(barrier, size - 1)
    return me


def remote(src, dst, send, recv, device):
    return pltpu.make_async_remote_copy(
        src_ref=src, dst_ref=dst, send_sem=send, recv_sem=recv, device_id=device, device_id_type=MESH
    )


def shuffle_kernel(count, *refs):
    ins, outs = refs[:count], refs[count : 2 * count]
    send, recv, own = refs[2 * count :]
    me = greet("wide", WIDE)

    def copy(k, j):
        peer = lax.rem(me + k, WIDE)
        return remote(
            ins[j].at[peer], outs[j].at[me], send.at[k, j], recv.at[k, j], {"wide": peer}
        )

    @pl.loop(1, WIDE)
    def _(k):
        for j in range(count):
            copy(k, j).start()

    for j in range(count):
        mine = pltpu.make_async_copy(ins[j].at[me], outs[j].at[me], own.at[j])
        mine.start()
        mine.wait()

    @pl.loop(1, WIDE)
    def _(k):
        for j in range(count):
            copy(k, j).wait()


def shuffle(arrays, collective):
    count = len(arrays)
    return pl.pallas_call(
        functools.partial(shuffle_kernel, count),
        out_shape=[shape(a.shape, a.dtype) for a in arrays],
        in_specs=[ANY] * count,
        out_specs=[ANY] * count,
        scratch_shapes=[
            pltpu.SemaphoreType.DMA((WIDE, count)),
            pltpu.SemaphoreType.DMA((WIDE, count)),
            pltpu.SemaphoreType.DMA((count,)),
        ],
        compiler_params=params(collective),
    )(*arrays)


def swap_kernel(pick, place, src, dst, send, recv, own):
    me = greet("mp", MP)

    def copy(k):
        peer = lax.rem(me + k, MP)
        return remote(pick(src, peer), place(dst, me), send.at[k], recv.at[k], {"mp": peer})

    for k in (2, 1, 3):
        copy(k).start()
    mine = pltpu.make_async_copy(pick(src, me), place(dst, me), own)
    mine.start()
    mine.wait()
    for k in (1, 3, 2):
        copy(k).wait()


def swap(array, out, pick, place, collective):
    return pl.pallas_call(
        functools.partial(swap_kernel, pick, place),
        out_shape=out,
        in_specs=[ANY],
        out_specs=ANY,
        scratch_shapes=[
            pltpu.SemaphoreType.DMA((MP,)),
            pltpu.SemaphoreType.DMA((MP,)),
            pltpu.SemaphoreType.DMA,
        ],
        compiler_params=params(collective),
    )(array)


def columns(ref, which):
    return ref.at[:, pl.ds(pl.multiple_of(which * LOCAL, LOCAL), LOCAL)]


def block(ref, which):
    return ref.at[which]


def whole(ref, which):
    return ref


def attend_pair(queries, parts, low):
    mixed = []
    for head in range(2):
        mine = low if head == 0 else jnp.logical_not(low)
        q = jnp.where(mine, queries, jnp.zeros_like(queries))
        scores = [jnp.where(allowed, dot_t(q, keys), -1e30) for keys, _, allowed in parts]
        top = functools.reduce(jnp.maximum, [jnp.max(s, -1, keepdims=True) for s in scores])
        expo = [jnp.exp(s - top) for s in scores]
        total = sum(jnp.sum(e, -1, keepdims=True) for e in expo)
        out = sum(dot(e.astype(BF16), values) for e, (_, values, _) in zip(expo, parts))
        mixed.append(out / total)
    return jnp.where(low, mixed[0], mixed[1])


def fine_kernel(x_ref, mask_ref, qkv_ref, out_ref, state_ref, coarse_ref):
    x = x_ref[...].astype(F32)
    normed = norm(x).astype(BF16)
    q = (dot(normed, qkv_ref[0]) * 0.125).astype(BF16)
    k = dot(normed, qkv_ref[1]).astype(BF16)
    v = dot(normed, qkv_ref[2]).astype(BF16)
    rows = lax.broadcasted_iota(I32, (BALL, BALL), 0)
    cols = lax.broadcasted_iota(I32, (BALL, BALL), 1)
    real = mask_ref[0] > 0
    allowed = jnp.logical_or(real, rows == cols)
    low = lax.broadcasted_iota(I32, (BALL, 128), 1) < 64
    mixed = []
    for g in range(MP):
        at = slice(g * 128, (g + 1) * 128)
        mixed.append(attend_pair(q[:, at], [(k[:, at], v[:, at], allowed)], low).astype(BF16))
    state = x + dot(jnp.concatenate(mixed, 1), out_ref[...])
    state_ref[...] = state
    high = state.astype(BF16)
    rest = (state - high.astype(F32)).astype(BF16)
    for f, begin in ((4, 0), (8, BALL // 4)):
        count_rows = BALL // f
        r = lax.broadcasted_iota(I32, (count_rows, BALL), 0)
        c = lax.broadcasted_iota(I32, (count_rows, BALL), 1)
        hot = jnp.where(jnp.logical_and(r == c // f, real), 1.0, 0.0)
        counted = jnp.sum(hot, 1, keepdims=True)
        hot = hot.astype(BF16)
        pooled = (dot(hot, high) + dot(hot, rest)) / jnp.maximum(counted, 1.0)
        coarse_ref[0, begin : begin + count_rows, :] = norm(pooled).astype(BF16)


def fine(x, mask, w_qkv, w_out):
    balls = QUARTER // BALL
    return pl.pallas_call(
        fine_kernel,
        grid=(balls,),
        out_shape=[shape((QUARTER, WIDTH), F32), shape((balls, 96, WIDTH), BF16)],
        in_specs=[
            pl.BlockSpec((BALL, WIDTH), lambda i: (i, 0)),
            pl.BlockSpec((1, 1, BALL), lambda i: (i, 0, 0)),
            pl.BlockSpec((3, WIDTH, WIDTH), lambda i: (0, 0, 0)),
            pl.BlockSpec((WIDTH, WIDTH), lambda i: (0, 0)),
        ],
        out_specs=[
            pl.BlockSpec((BALL, WIDTH), lambda i: (i, 0)),
            pl.BlockSpec((1, 96, WIDTH), lambda i: (i, 0, 0)),
        ],
        compiler_params=params(),
    )(x, mask, w_qkv, w_out)


def forward_kernel(state_ref, gate_ref, up_ref, down_ref, out_ref):
    state = state_ref[...]
    normed = norm(state).astype(BF16)
    total = state
    for c in range(MP):
        gate = dot(normed, gate_ref[c])
        up = dot(normed, up_ref[c])
        activated = (gate / (1.0 + jnp.exp(-gate)) * up).astype(BF16)
        total = total + dot(activated, down_ref[c])
    out_ref[...] = total


def forward(state, gate_up, down):
    tiles = QUARTER // BALL
    return pl.pallas_call(
        forward_kernel,
        grid=(tiles,),
        out_shape=shape((QUARTER, WIDTH), F32),
        in_specs=[
            pl.BlockSpec((BALL, WIDTH), lambda i: (i, 0)),
            pl.BlockSpec((MP, None, WIDTH, WIDTH), lambda i: (0, 0, 0, 0)),
            pl.BlockSpec((MP, None, WIDTH, WIDTH), lambda i: (0, 1, 0, 0)),
            pl.BlockSpec((MP, WIDTH, WIDTH), lambda i: (0, 0, 0)),
        ],
        out_specs=pl.BlockSpec((BALL, WIDTH), lambda i: (i, 0)),
        compiler_params=params(),
    )(state, gate_up, gate_up, down)


def project_kernel(rows_ref, w_ref, one_ref, two_ref):
    for ball in range(QUARTER // BALL):
        rows = rows_ref[0, ball]
        for t in range(3):
            scale = 0.125 if t == 0 else 1.0
            one_ref[t, ball * 64 : (ball + 1) * 64, :] = (
                dot(rows[:64], w_ref[0, t]) * scale
            ).astype(BF16)
            two_ref[t, ball * 32 : (ball + 1) * 32, :] = (
                dot(rows[64:], w_ref[1, t]) * scale
            ).astype(BF16)


def project(rows, w_coarse):
    return pl.pallas_call(
        project_kernel,
        grid=(MP,),
        out_shape=[shape((3, 4 * ONE, LOCAL), BF16), shape((3, 4 * TWO, LOCAL), BF16)],
        in_specs=[
            pl.BlockSpec((1, 4, 96, WIDTH), lambda i: (i, 0, 0, 0)),
            pl.BlockSpec((2, 3, WIDTH, LOCAL), lambda i: (0, 0, 0, 0)),
        ],
        out_specs=[
            pl.BlockSpec((3, ONE, LOCAL), lambda i: (0, i, 0)),
            pl.BlockSpec((3, TWO, LOCAL), lambda i: (0, i, 0)),
        ],
        compiler_params=params(),
    )(rows, w_coarse)


def relatives(me):
    low = lax.rem(me, 2)
    high = lax.rem(me // 2, 2)
    first = me + 1 - 2 * low
    second = me + 2 - 4 * high
    third = first + 2 - 4 * high
    return (first, second, third)


def exchange_kernel(one, two, keep, mate_one, mate_two, mate_keep, send, recv):
    me = lax.axis_index("wide")
    others = relatives(me)
    barrier = pltpu.get_barrier_semaphore()
    for other in others:
        pl.semaphore_signal(barrier, inc=1, device_id={"wide": other}, device_id_type=MESH)
    pl.semaphore_wait(barrier, 3)
    copies = []
    for j in (1, 2, 0):
        to = {"wide": others[j]}
        copies.append(remote(two.at[1:], mate_two.at[j], send.at[j, 0], recv.at[j, 0], to))
        copies.append(remote(keep, mate_keep.at[j], send.at[j, 1], recv.at[j, 1], to))
    copies.append(
        remote(one.at[1:], mate_one, send.at[3, 0], recv.at[3, 0], {"wide": others[0]})
    )
    for copy in copies:
        copy.start()
    for copy in copies:
        copy.wait()


def exchange(one, two, keep, collective):
    return pl.pallas_call(
        exchange_kernel,
        out_shape=[
            shape((2, 4 * ONE, LOCAL), BF16),
            shape((3, 2, 4 * TWO, LOCAL), BF16),
            shape((3,) + keep.shape, I32),
        ],
        in_specs=[ANY] * 3,
        out_specs=[ANY] * 3,
        scratch_shapes=[pltpu.SemaphoreType.DMA((4, 2)), pltpu.SemaphoreType.DMA((4, 2))],
        compiler_params=params(collective),
    )(one, two, keep)


def coarse_kernel(one, two, mate_one, mate_two, keep, mate_keep, out):
    tile = 256
    low = lax.broadcasted_iota(I32, (tile, 128), 1) < 64
    flags = [keep[...]] + [mate_keep[j] for j in range(3)]

    def own(begin, real, length):
        rows = lax.broadcasted_iota(I32, (tile, length), 0) + begin
        cols = lax.broadcasted_iota(I32, (tile, length), 1)
        return jnp.logical_or(real, rows == cols)

    for t in range(4):
        begin = t * tile
        real = [flags[j][:, : 4 * ONE] > 0 for j in range(2)]
        parts = [
            (one[1], one[2], own(begin, real[0], 4 * ONE)),
            (mate_one[0], mate_one[1], real[1]),
        ]
        mixed = attend_pair(one[0, begin : begin + tile, :], parts, low)
        out[t, 0:256, :] = mixed.astype(BF16)
    for t in range(2):
        begin = t * tile
        real = [flags[j][:, 4 * ONE :] > 0 for j in range(4)]
        parts = [(two[1], two[2], own(begin, real[0], 4 * TWO))]
        for j in range(3):
            parts.append((mate_two[j, 0], mate_two[j, 1], real[j + 1]))
        mixed = attend_pair(two[0, begin : begin + tile, :], parts, low).astype(BF16)
        out[2 * t, 256:384, :] = mixed[:128]
        out[2 * t + 1, 256:384, :] = mixed[128:]


def coarse(one, two, mate_one, mate_two, keep, mate_keep):
    return pl.pallas_call(
        coarse_kernel,
        out_shape=shape((MP, COARSE, LOCAL), BF16),
        in_specs=[VMEM] * 6,
        out_specs=VMEM,
        compiler_params=params(),
    )(one, two, mate_one, mate_two, keep, mate_keep)


def lift_kernel(state_ref, mixed_ref, w_ref, out_ref):
    one = dot(mixed_ref[0:ONE, :], w_ref[0]).astype(BF16)
    two = dot(mixed_ref[ONE:COARSE, :], w_ref[1]).astype(BF16)
    for t in range(QUARTER // BALL):
        both = jnp.concatenate([one[t * 64 : (t + 1) * 64], two[t * 32 : (t + 1) * 32]], 0)
        r = lax.broadcasted_iota(I32, (BALL, 96), 0)
        c = lax.broadcasted_iota(I32, (BALL, 96), 1)
        hot = jnp.logical_or(
            jnp.logical_and(c < 64, r // 4 == c), jnp.logical_and(c >= 64, r // 8 == c - 64)
        )
        spread = dot(jnp.where(hot, 1.0, 0.0).astype(BF16), both)
        at = slice(t * BALL, (t + 1) * BALL)
        out_ref[at, :] = (state_ref[at, :] + spread).astype(BF16)


def lift(state, mixed, w_coarse_out):
    return pl.pallas_call(
        lift_kernel,
        out_shape=shape((QUARTER, WIDTH), BF16),
        in_specs=[VMEM] * 3,
        out_specs=VMEM,
        compiler_params=params(),
    )(state, mixed, w_coarse_out)


def on_device(points, mask, perm, w_qkv, w_out, w_gate_up, w_down, w_coarse, w_coarse_out):
    full_qkv = lax.all_gather(w_qkv, "mp", axis=2, tiled=True)
    full_out = lax.all_gather(w_out, "mp", axis=0, tiled=True)
    full_gate_up = lax.all_gather(w_gate_up, "mp", axis=0)
    full_down = lax.all_gather(w_down, "mp", axis=0)
    full_coarse_out = lax.all_gather(w_coarse_out, "mp", axis=1, tiled=True)

    slot, code = pl.pallas_call(
        rank_kernel,
        out_shape=[shape((16, 256), I32)] * 2,
        in_specs=[VMEM] * 2,
        out_specs=[VMEM] * 2,
        compiler_params=params(),
    )(perm.reshape(16, 256), mask.reshape(16, 256))
    slot = slot.reshape(ROWS)
    code = code.reshape(ROWS)
    rows, codes = pl.pallas_call(
        pack_kernel,
        out_shape=[shape((SLOTS, LOCAL), BF16), shape((SLOTS,), I32)],
        in_specs=[SMEM, SMEM, VMEM, ANY],
        out_specs=[VMEM, SMEM],
        scratch_shapes=[pltpu.VMEM((ROWS, LOCAL), F32), pltpu.VMEM((SLOTS, LOCAL), F32)],
        compiler_params=params(),
    )(slot, code, points, jnp.full((SLOTS,), 2 * ROWS, I32))
    got, got_code = shuffle(
        [rows.reshape(WIDE, CAP, LOCAL), codes.reshape(WIDE, 2, 128)], 1
    )
    got_code = got_code.reshape(SLOTS)
    owned, owned_mask = pl.pallas_call(
        unpack_kernel,
        out_shape=[shape((ROWS, LOCAL), BF16), shape((ROWS + 128,), I32)],
        in_specs=[SMEM, VMEM],
        out_specs=[VMEM, SMEM],
        scratch_shapes=[pltpu.VMEM((SLOTS, LOCAL), F32), pltpu.VMEM((ROWS + 8, LOCAL), F32)],
        compiler_params=params(),
    )(got_code, got.reshape(SLOTS, LOCAL))
    owned_mask = owned_mask[:ROWS]
    keep_one = (jnp.sum(owned_mask.reshape(ROWS // 4, 4), 1) > 0).astype(I32)
    keep_two = (jnp.sum(owned_mask.reshape(ROWS // 8, 8), 1) > 0).astype(I32)
    keep = jnp.concatenate([keep_one, keep_two]).reshape(1, 12 * 128)
    quarter_mask = lax.dynamic_slice_in_dim(
        owned_mask.reshape(MP, QUARTER), lax.axis_index("mp"), 1, 0
    ).reshape(QUARTER // BALL, 1, BALL)
    x = swap(
        owned.reshape(MP, QUARTER, LOCAL), shape((QUARTER, WIDTH), BF16), block, columns, 2
    )
    state, pooled = fine(x, quarter_mask, full_qkv, full_out)
    all_pooled = swap(pooled, shape((MP,) + pooled.shape, BF16), whole, block, 3)
    one, two = project(all_pooled, w_coarse)
    mate_one, mate_two, mate_keep = exchange(one, two, keep, 4)
    fed = forward(state, full_gate_up, full_down)
    mixed = coarse(one, two, mate_one, mate_two, keep, mate_keep)
    all_mixed = swap(mixed, shape((COARSE, WIDTH), BF16), block, columns, 5)
    result = lift(fed, all_mixed, full_coarse_out)
    updated = swap(result, shape((MP, QUARTER, LOCAL), BF16), columns, block, 6)
    back = pl.pallas_call(
        repack_kernel,
        out_shape=shape((SLOTS, LOCAL), BF16),
        in_specs=[SMEM, VMEM],
        out_specs=VMEM,
        scratch_shapes=[pltpu.VMEM((ROWS + 8, LOCAL), F32), pltpu.VMEM((SLOTS, LOCAL), F32)],
        compiler_params=params(),
    )(got_code, updated.reshape(ROWS, LOCAL))
    (returned,) = shuffle([back.reshape(WIDE, CAP, LOCAL)], 7)
    return pl.pallas_call(
        finish_kernel,
        out_shape=shape((ROWS, LOCAL), F32),
        in_specs=[SMEM, VMEM],
        out_specs=VMEM,
        scratch_shapes=[pltpu.VMEM((SLOTS, LOCAL), F32)],
        compiler_params=params(),
    )(slot, returned.reshape(SLOTS, LOCAL))


def solution(mesh):
    placed = (
        P("wide", "mp"),
        P("wide"),
        P("wide"),
        P(None, None, "mp"),
        P("mp", None),
        P(None, None, "mp"),
        P("mp", None),
        P(None, None, None, "mp"),
        P(None, "mp", None),
    )
    return jax.shard_map(
        on_device, mesh=mesh, in_specs=placed, out_specs=P("wide", "mp"), check_vma=False
    )
```

time: 646 us -> 323 us (0.50); the launches traced: 637 us -> 321 us
  Pallas kernels: 0 us -> 283 us
  local copies, waits for them, and re-layouts: 215 us -> 7.14 us
  waiting for transfers between devices: 198 us -> 2.65 us
  matrix products: 67.2 us -> 0 us
  starting transfers between devices: 55.2 us -> 0.12 us
  other arithmetic: 51.9 us -> 0.37 us
  blocking collectives: 35.6 us -> 14.2 us
    pallas_call x0 -> x17, Pallas kernels: none -> 283 us  [the longest x2 87.2 us: shuffle(): pl.pallas_call(functools.partial(shuffle_kernel, count), out_shape=[shape...]
    scatter x5 -> x0, local copies, waits for them, and re-layouts: 125 us -> none  [the longest x1 38.5 us: on_device(): owned_rows = jnp.zeros((rows_dev, carried_cols), carried.dtype).at[flat_i...]
    all_to_all x3 -> x0, waiting for transfers between devices: 75.6 us -> none  [the longest x1 75.6 us: on_device(): lax.all_to_all(send_rows, 'wide', split_axis=0, concat_axis=0, tiled=True)]
    psum x1 -> x0, waiting for transfers between devices: 73.8 us -> none  [on_device(): lax.psum(head_terms.astype(jnp.bfloat16), 'mp').astype(jnp.float32)]
    dot_general x10 -> x0, matrix products: 48 us -> none  [the longest x3 18.7 us: attend(): jnp.einsum('hqk,khe->qhe', weights, v_heads, preferred_element_type=jnp.f...]
    unnamed x4, waiting for transfers between devices: 48 us -> 2.61 us
    gather x2 -> x0, local copies, waits for them, and re-layouts: 40.5 us -> none  [the longest x1 24 us: on_device(): jnp.take(result, flat_index, axis=0, mode='fill', fill_value=0)]
    all_to_all x1 -> x0, blocking collectives: 35.6 us -> none  [on_device(): lax.all_to_all(back_rows.astype(jnp.bfloat16), 'wide', split_axis=0, conc...]
  transfers between devices with their start and end apart: 15 -> 4, of which waited for: 4 -> 0; matrix products, arithmetic and copies ran while one was open for 25% -> 2% of each run, Pallas kernels for 0% -> 62%
where the time goes in v1:
time: 323 us; the launch traced here: 321 us
  Pallas kernels  283 us (88%)
  blocking collectives  14.2 us (4%)
  between operations  13.3 us (4%)
  local copies, waits for them, and re-layouts  7.14 us (2%)
    pallas_call x2, Pallas kernels, shuffle(): pl.pallas_call(functools.partial(shuffle_kernel, count), out_shape=[shape...  87.2 us
    pallas_call x4, Pallas kernels, swap(): pl.pallas_call(functools.partial(swap_kernel, pick, place), out_shape=out...  78.4 us
    pallas_call x1, Pallas kernels, on_device(): pl.pallas_call(unpack_kernel, out_shape=[shape((ROWS, LOCAL), BF16), shap...  20.6 us
    pallas_call x1, Pallas kernels, exchange(): pl.pallas_call(exchange_kernel, out_shape=[shape((2, 4 * ONE, LOCAL), BF1...  16.2 us
    pallas_call x1, Pallas kernels, on_device(): pl.pallas_call(repack_kernel, out_shape=shape((SLOTS, LOCAL), BF16), in_s...  14.4 us
    all_gather x1, blocking collectives, on_device(): full_out = lax.all_gather(w_out, 'mp', axis=0, tiled=True)  14.2 us
    pallas_call x1, Pallas kernels, forward(): pl.pallas_call(forward_kernel, grid=(tiles,), out_shape=shape((QUARTER, W...  13 us
    pallas_call x1, Pallas kernels, coarse(): pl.pallas_call(coarse_kernel, out_shape=shape((MP, COARSE, LOCAL), BF16),...  12.6 us
  transfers between devices with their start and end apart: 4, of which 0 were waited for; matrix products, arithmetic and copies ran while one was open for 2% of the time, Pallas kernels for 62%

profile of v1, /device:TPU:1, one launch (start us, length us, event | category | flops | bytes accessed | tf_op | source)
XLA Modules:
  0.0 320.5 jit_solution(8345070728446468286)
XLA Ops:
  6.5 0.0 copy-start.1
  6.5 0.0 copy-start.2
  6.5 0.0 all-gather.7.cloned.1.call-start
  6.5 0.7 all-gather.7.cloned.1.call-update
  7.3 0.0 all-gather.13.cloned.1.call-start
  7.3 0.7 all-gather.13.cloned.1.call-update
  8.0 0.0 all-gather.11.cloned.1.call-start
  8.1 0.7 all-gather.11.cloned.1.call-update
  8.7 0.0 all-gather.9.cloned.1.call-start
  8.8 0.5 all-gather.9.cloned.1.call-update
  9.3 0.0 copy-done.1
  9.3 0.6 reshape.69.perm_ref
  9.9 0.0 copy-done.2
  9.9 0.6 reshape.70.mask_ref
  10.6 1.8 shard_map.91
  12.4 1.3 copy.10
  13.7 1.3 copy.11
  15.0 0.6 broadcast_in_dim.3.none_ref
  15.6 11.9 %shard_map.92 = (bf16[8192,128]{1,0:T(8,128)(2,1)}, s32[8192]{0:T(1024)}) custom-call(s32[4096]{0:T(1024)} %bitcast.24, s32[4096]{0:T(1024)} %bitcast.28, bf16[4096,128]{1,0:T(8,128)(2,1)} %points_ref.1, s32[8192]{0:T(1024)} %broadcast_in_dim.3.none_ref), custom_call_target="tpu_custom_call" | custom-call | tf_op jit(solution)/shard_map/pallas_call | solution.py:501
  27.6 44.7 %shard_map.93 = (bf16[32,256,128]{2,1,0:T(8,128)(2,1)}, s32[32,2,128]{2,1,0:T(2,128)}) custom-call(bf16[32,256,128]{2,1,0:T(8,128)(2,1)} %bitcast.21, s32[32,2,128]{2,1,0:T(2,128)} %bitcast.29), custom_call_target="tpu_custom_call" | custom-call | tf_op jit(solution)/shard_map/pallas_call | solution.py:195
  72.3 20.6 %shard_map.94 = (bf16[4096,128]{1,0:T(8,128)(2,1)}, s32[4224]{0:T(1024)}) custom-call(s32[8192]{0:T(1024)} %bitcast.26, bf16[8192,128]{1,0:T(8,128)(2,1)} %bitcast.22), custom_call_target="tpu_custom_call" | custom-call | tf_op jit(solution)/shard_map/pallas_call | solution.py:513
  93.0 0.0 copy-start
  93.0 0.8 slice.19
  93.7 0.5 reshape.80
  94.3 0.2 reshape.81
  94.4 26.9 %shard_map.95.x_ref = bf16[1024,512]{1,0:T(8,128)(2,1)} custom-call(bf16[4,1024,128]{2,1,0:T(8,128)(2,1)} %bitcast.23), custom_call_target="tpu_custom_call" | custom-call | tf_op jit(solution)/shard_map/pallas_call | solution.py:226
  121.4 0.2 reduce_sum.18
  121.6 0.1 reduce_sum.19
  121.7 0.6 reshape.88.keep
  122.3 0.6 constant_dynamic-slice_fusion
  122.9 0.0 copy-done
  122.9 14.2 %all_gather.22.out_ref = bf16[512,512]{1,0:T(8,128)(2,1)} all-gather(bf16[128,512]{1,0:T(8,128)(2,1)S(1)} %copy-done), channel_id=1, replica_groups=mesh['wide'=32,'mp'=4] {'mp'}, dimensions={0}, use_global_device_ids=true | all-gather | bytes 655360 | tf_op jit(solution)/shard_map/all_gather | solution.py:487
  137.1 0.0 all-gather.7.cloned.1.call-done.qkv_ref
  137.1 10.0 %shard_map.96 = (f32[1024,512]{1,0:T(8,128)}, bf16[4,96,512]{2,1,0:T(8,128)(2,1)}) custom-call(bf16[1024,512]{1,0:T(8,128)(2,1)} %shard_map.95.x_ref, s32[4,1,256]{2,1,0:T(1,128)} %bitcast.30, bf16[3,512,512]{2,1,0:T(8,128)(2,1)} %all-gather.7.cloned.1.call-done.qkv_ref, bf16[512,512]{1,0:T(8,128)(2,1)} %all_gather.22.out_ref), custom_call_target="tpu_custom_call" | custom-call | tf_op jit(solution)/shard_map/pallas_call | solution.py:298
  147.1 27.5 %shard_map.98.rows_ref = bf16[4,4,96,512]{3,2,1,0:T(8,128)(2,1)} custom-call(bf16[4,96,512]{2,1,0:T(8,128)(2,1)} %get-tuple-element.29.src), custom_call_target="tpu_custom_call" | custom-call | tf_op jit(solution)/shard_map/pallas_call | solution.py:226
  174.6 5.1 %shard_map.99 = (bf16[3,1024,128]{2,1,0:T(8,128)(2,1)}, bf16[3,512,128]{2,1,0:T(8,128)(2,1)}) custom-call(bf16[4,4,96,512]{3,2,1,0:T(8,128)(2,1)} %shard_map.98.rows_ref, bf16[2,3,512,128]{3,2,1,0:T(8,128)(2,1)} %w_ref.1), custom_call_target="tpu_custom_call" | custom-call | tf_op jit(solution)/shard_map/pallas_call | solution.py:359
  179.7 16.2 %shard_map.100 = (bf16[2,1024,128]{2,1,0:T(8,128)(2,1)}, bf16[3,2,512,128]{3,2,1,0:T(8,128)(2,1)}, s32[3,1,1536]{2,1,0:T(1,128)}) custom-call(bf16[3,1024,128]{2,1,0:T(8,128)(2,1)} %get-tuple-element.30.one, bf16[3,512,128]{2,1,0:T(8,128)(2,1)} %get-tuple-element.31.two, s32[1,1536]{1,0:T(1,128)} %reshape.88.keep), custom_call_target="tpu_custom_call" | custom-call | tf_op jit(solution)/shard_map/pallas_call | solution.py:406
  195.9 12.6 %shard_map.101.src = bf16[4,384,128]{2,1,0:T(8,128)(2,1)} custom-call(bf16[3,1024,128]{2,1,0:T(8,128)(2,1)} %get-tuple-element.30.one, bf16[3,512,128]{2,1,0:T(8,128)(2,1)} %get-tuple-element.31.two, bf16[2,1024,128]{2,1,0:T(8,128)(2,1)} %get-tuple-element.32.mate_one, bf16[3,2,512,128]{3,2,1,0:T(8,128)(2,1)} %get-tuple-element.33.mate_two, ...), custom_call_target="tpu_custom_call" | custom-call | tf_op jit(solution)/shard_map/pallas_call | solution.py:451
  208.5 8.8 %shard_map.102.mixed_ref = bf16[384,512]{1,0:T(8,128)(2,1)} custom-call(bf16[4,384,128]{2,1,0:T(8,128)(2,1)} %shard_map.101.src), custom_call_target="tpu_custom_call" | custom-call | tf_op jit(solution)/shard_map/pallas_call | solution.py:226
  217.3 0.0 all-gather.13.cloned.1.call-done
  217.4 0.0 all-gather.11.cloned.1.call-done
  217.4 13.0 %shard_map.97.state_ref = f32[1024,512]{1,0:T(8,128)} custom-call(f32[1024,512]{1,0:T(8,128)} %get-tuple-element.28.state_ref, bf16[4,2,512,512]{3,2,1,0:T(8,128)(2,1)} %bitcast.15, bf16[4,2,512,512]{3,2,1,0:T(8,128)(2,1)} %bitcast.16, bf16[4,512,512]{2,1,0:T(8,128)(2,1)} %bitcast.20), custom_call_target="tpu_custom_call" | custom-call | tf_op jit(solution)/shard_map/pallas_call | solution.py:330
  230.4 0.0 all-gather.9.cloned.1.call-done.w_ref
  230.4 3.7 %shard_map.103.src = bf16[1024,512]{1,0:T(8,128)(2,1)} custom-call(f32[1024,512]{1,0:T(8,128)} %shard_map.97.state_ref, bf16[384,512]{1,0:T(8,128)(2,1)} %shard_map.102.mixed_ref, bf16[2,512,512]{2,1,0:T(8,128)(2,1)} %all-gather.9.cloned.1.call-done.w_ref), custom_call_target="tpu_custom_call" | custom-call | tf_op jit(solution)/shard_map/pallas_call | solution.py:476
  234.1 15.2 %shard_map.104 = bf16[4,1024,128]{2,1,0:T(8,128)(2,1)} custom-call(bf16[1024,512]{1,0:T(8,128)(2,1)} %shard_map.103.src), custom_call_target="tpu_custom_call" | custom-call | tf_op jit(solution)/shard_map/pallas_call | solution.py:226
  249.3 14.4 %shard_map.105 = bf16[8192,128]{1,0:T(8,128)(2,1)} custom-call(s32[8192]{0:T(1024)} %bitcast.27, bf16[4096,128]{1,0:T(8,128)(2,1)} %bitcast.19), custom_call_target="tpu_custom_call" | custom-call | tf_op jit(solution)/shard_map/pallas_call | solution.py:540
  263.7 42.5 %shard_map.106 = bf16[32,256,128]{2,1,0:T(8,128)(2,1)} custom-call(bf16[32,256,128]{2,1,0:T(8,128)(2,1)} %bitcast.17), custom_call_target="tpu_custom_call" | custom-call | tf_op jit(solution)/shard_map/pallas_call | solution.py:195
  306.2 7.8 %shard_map.107 = f32[4096,128]{1,0:T(8,128)} custom-call(s32[4096]{0:T(1024)} %bitcast.25, bf16[8192,128]{1,0:T(8,128)(2,1)} %bitcast.18), custom_call_target="tpu_custom_call" | custom-call | tf_op jit(solution)/shard_map/pallas_call | solution.py:549
  (4 shorter events, 0.0 us)
Async XLA Ops:
  6.5 2.8 copy-start.1
  6.5 3.4 %copy-start.2 = (s32[4096]{0:T(1024)S(1)}, s32[4096]{0:T(1024)}, u32[]{:S(2)}) copy-start(s32[4096]{0:T(1024)} %param.10) | copy-start | bytes 49156
  6.5 130.6 %all-gather.7.cloned.1.call-start = ((), (), s32[]{:S(2)}) async-start(), calls=%async_computation | async-start | bytes 1966080 | tf_op jit(solution)/shard_map/all_gather | solution.py:486
  7.3 210.1 %all-gather.13.cloned.1.call-start = ((), (), s32[]{:S(2)}) async-start(), calls=%async_computation.3 | async-start | bytes 2621440 | tf_op jit(solution)/shard_map/all_gather | solution.py:489
  8.0 209.4 %all-gather.11.cloned.1.call-start = ((), (), s32[]{:S(2)}) async-start(), calls=%async_computation.2 | async-start | bytes 5242880 | tf_op jit(solution)/shard_map/all_gather | solution.py:488
  8.7 221.7 %all-gather.9.cloned.1.call-start = ((), (), s32[]{:S(2)}) async-start(), calls=%async_computation.1 | async-start | bytes 1310720 | tf_op jit(solution)/shard_map/all_gather | solution.py:490
  93.0 30.0 %copy-start = (bf16[128,512]{1,0:T(8,128)(2,1)S(1)}, bf16[128,512]{1,0:T(8,128)(2,1)}, u32[]{:S(2)}) copy-start(bf16[128,512]{1,0:T(8,128)(2,1)} %param.13) | copy-start | bytes 393220
Sparse Core Ops, SparseCore 0:
  9.0 32.5 all-gather.6
  43.2 32.6 all-gather.12
  77.6 63.7 all-gather.10
  142.9 33.9 all-gather.8

commit v2 on v1

--- a/solution.py
+++ b/solution.py
@@ -54,10 +54,22 @@
     return values * lax.rsqrt(jnp.mean(values * values, -1, keepdims=True) + 1e-06)
 
 
-def rank_kernel(perm_ref, mask_ref, slot_ref, code_ref):
+UNROLL = 16
+NONE = 2 * ROWS
+
+
+def index_kernel(
+    perm_ref, mask_ref, blank_ref, slot_ref, source_ref, codes_ref, slots, codes, slot_s, code_s, sems
+):
+    blanks = [
+        pltpu.make_async_copy(blank_ref.at[0], source_ref, sems.at[0]),
+        pltpu.make_async_copy(blank_ref.at[1], codes_ref, sems.at[1]),
+    ]
+    for copy in blanks:
+        copy.start()
     perm = perm_ref[...]
     target = perm >> 12
-    code_ref[...] = (perm & (ROWS - 1)) * 2 + mask_ref[...]
+    codes[...] = (perm & (ROWS - 1)) * 2 + mask_ref[...]
     rows = lax.broadcasted_iota(I32, (256, 256), 0)
     cols = lax.broadcasted_iota(I32, (256, 256), 1)
     upper = jnp.where(rows < cols, 1.0, 0.0).astype(BF16)
@@ -67,8 +79,45 @@
         hot = jnp.where(which == target[c : c + 1, :], 1.0, 0.0)
         before = dot(hot.astype(BF16), upper) + carry
         rank = jnp.sum(hot * before, 0, keepdims=True)
-        slot_ref[c : c + 1, :] = target[c : c + 1, :] * CAP + rank.astype(I32)
+        slots[c : c + 1, :] = target[c : c + 1, :] * CAP + rank.astype(I32)
         carry = carry + jnp.sum(hot, 1, keepdims=True)
+    slot_ref[...] = slots[...]
+    moves = [
+        pltpu.make_async_copy(slots, slot_s, sems.at[2]),
+        pltpu.make_async_copy(codes, code_s, sems.at[3]),
+    ]
+    for copy in moves:
+        copy.start()
+    for copy in blanks + moves:
+        copy.wait()
+    for c in range(ROWS // 256):
+
+        @pl.loop(0, 256 // UNROLL)
+        def _(i):
+            base = i * UNROLL
+            at = [slot_s[c, base + u] for u in range(UNROLL)]
+            code = [code_s[c, base + u] for u in range(UNROLL)]
+            for u in range(UNROLL):
+                source_ref[at[u]] = c * 256 + base + u
+                codes_ref[at[u]] = code[u]
+
+
+def index(perm, mask):
+    blank = jnp.broadcast_to(jnp.array([[0], [NONE]], I32), (2, SLOTS))
+    return pl.pallas_call(
+        index_kernel,
+        out_shape=[shape((16, 256), I32), shape((SLOTS,), I32), shape((SLOTS,), I32)],
+        in_specs=[VMEM, VMEM, ANY],
+        out_specs=[VMEM, SMEM, SMEM],
+        scratch_shapes=[
+            pltpu.VMEM((16, 256), I32),
+            pltpu.VMEM((16, 256), I32),
+            pltpu.SMEM((16, 256), I32),
+            pltpu.SMEM((16, 256), I32),
+            pltpu.SemaphoreType.DMA((4,)),
+        ],
+        compiler_params=params(),
+    )(perm.reshape(16, 256), mask.reshape(16, 256), blank)
 
 
 def widen(src, dst, rows):
@@ -78,58 +127,23 @@
         dst[at, :] = src[at, :].astype(dst.dtype)
 
 
-UNROLL = 16
-
-
-def pack_kernel(slot_ref, code_ref, points_ref, none_ref, rows_ref, codes_ref, wide, packed):
-    pltpu.sync_copy(none_ref, codes_ref)
-    widen(points_ref, wide, ROWS)
-
-    @pl.loop(0, SLOTS // 256)
-    def _(i):
-        packed[pl.ds(pl.multiple_of(i * 256, 256), 256), :] = jnp.zeros((256, LOCAL), F32)
-
-    @pl.loop(0, ROWS // UNROLL)
-    def _(i):
-        base = i * UNROLL
-        slots = [slot_ref[base + u] for u in range(UNROLL)]
-        lines = [wide[pl.ds(base + u, 1), :] for u in range(UNROLL)]
-        for u in range(UNROLL):
-            packed[pl.ds(slots[u], 1), :] = lines[u]
-        codes = [code_ref[base + u] for u in range(UNROLL)]
-        for u in range(UNROLL):
-            codes_ref[slots[u]] = codes[u]
-
-    widen(packed, rows_ref, SLOTS)
-
-
 def unpack_kernel(code_ref, got_ref, rows_ref, mask_ref, wide, owned):
     widen(got_ref, wide, SLOTS)
 
     @pl.loop(0, SLOTS // UNROLL)
     def _(i):
         base = i * UNROLL
-        codes = [code_ref[base + u] for u in range(UNROLL)]
-        lines = [wide[pl.ds(base + u, 1), :] for u in range(UNROLL)]
-        for u in range(UNROLL):
-            owned[pl.ds(codes[u] >> 1, 1), :] = lines[u]
-        for u in range(UNROLL):
-            mask_ref[codes[u] >> 1] = codes[u] & 1
+
+        @pl.when(code_ref[base] < NONE)
+        def _():
+            codes = [code_ref[base + u] for u in range(UNROLL)]
+            lines = [wide[pl.ds(base + u, 1), :] for u in range(UNROLL)]
+            for u in range(UNROLL):
+                owned[pl.ds(codes[u] >> 1, 1), :] = lines[u]
+            for u in range(UNROLL):
+                mask_ref[codes[u] >> 1] = codes[u] & 1
 
     widen(owned, rows_ref, ROWS)
-
-
-def repack_kernel(code_ref, rows_ref, out_ref, wide, packed):
-    widen(rows_ref, wide, ROWS)
-
-    @pl.loop(0, SLOTS // UNROLL)
-    def _(i):
-        base = i * UNROLL
-        lines = [wide[pl.ds(code_ref[base + u] >> 1, 1), :] for u in range(UNROLL)]
-        for u in range(UNROLL):
-            packed[pl.ds(base + u, 1), :] = lines[u]
-
-    widen(packed, out_ref, SLOTS)
 
 
 def finish_kernel(slot_ref, got_ref, out_ref, wide):
@@ -163,47 +177,286 @@
     )
 
 
-def shuffle_kernel(count, *refs):
-    ins, outs = refs[:count], refs[count : 2 * count]
-    send, recv, own = refs[2 * count :]
-    me = greet("wide", WIDE)
-
-    def copy(k, j):
+def gather_bucket(line, lookup, wide, staged, packed, peer):
+    @pl.loop(0, CAP // UNROLL)
+    def _(i):
+        begin = i * UNROLL
+        lines = [wide[pl.ds(lookup(peer * CAP + begin + u), 1), :] for u in range(UNROLL)]
+        for u in range(UNROLL):
+            staged[line, pl.ds(begin + u, 1), :] = lines[u]
+
+    packed[peer] = staged[line].astype(BF16)
+
+
+def send_kernel(
+    source_ref, points_ref, codes_ref, qkv_ref, out_ref, gate_up_ref, down_ref, lift_ref,
+    got_ref, got_codes_ref, all_qkv, all_out, all_gate_up, all_down, all_lift,
+    wide, staged, packed, send, recv, own, w_send, w_recv, w_own,
+):
+    me = lax.axis_index("wide")
+    mp = lax.axis_index("mp")
+    core = lax.rem(me, 2)
+    partner = me + 1 - 2 * core
+    after, ahead = lax.rem(mp + 1, MP), lax.rem(mp + 2, MP)
+    behind = lax.rem(mp + 3, MP)
+    barrier = pltpu.get_barrier_semaphore()
+
+    @pl.loop(1, WIDE)
+    def _(k):
+        pl.semaphore_signal(
+            barrier, inc=1, device_id={"wide": lax.rem(me + k, WIDE)}, device_id_type=MESH
+        )
+
+    for other in (after, behind):
+        pl.semaphore_signal(barrier, inc=1, device_id={"mp": other}, device_id_type=MESH)
+    widen(points_ref, wide, ROWS)
+
+    def part(first, count):
+        def rows(ref, quarter):
+            return pl.ds(pl.multiple_of(first * quarter, 16), count * quarter)
+
+        def cut(j, ref, shard):
+            if j == 0:
+                return ref.at[rows(ref, 384), pl.ds(pl.multiple_of(shard * 128, 128), 128)]
+            quarter = (0, 32, 256, 128, 64)[j]
+            return ref.at[shard, rows(ref, quarter), :]
+
+        def own_cut(j, ref):
+            quarter = (384, 32, 256, 128, 64)[j]
+            return ref.at[rows(ref, quarter), :]
+
+        return cut, own_cut
+
+    half, own_half = part(2 * core, 2)
+    first, _ = part(2 * core, 1)
+    second, _ = part(2 * core + 1, 1)
+    every, own_every = part(0, 4)
+    shards = [qkv_ref, out_ref, gate_up_ref, down_ref, lift_ref]
+    full = [all_qkv, all_out, all_gate_up, all_down, all_lift]
+    count = len(shards)
+
+    def weight(j, kind, cut, src, shard, device):
+        return remote(
+            src, cut(j, full[j], shard), w_send.at[j, kind], w_recv.at[j, kind], device
+        )
+
+    def weight_copies(j):
+        ref = full[j]
+        mine = own_half(j, shards[j])
+        return [
+            weight(j, 0, half, mine, mp, {"mp": after}),
+            weight(j, 1, half, mine, mp, {"mp": behind}),
+            weight(j, 2, first, first(j, ref, behind), behind, {"mp": after}),
+            weight(j, 3, second, second(j, ref, after), after, {"mp": behind}),
+            weight(j, 4, half, half(j, ref, behind), behind, {"wide": partner}),
+            weight(j, 5, half, half(j, ref, after), after, {"wide": partner}),
+            weight(j, 6, first, first(j, ref, ahead), ahead, {"wide": partner}),
+            weight(j, 7, second, second(j, ref, ahead), ahead, {"wide": partner}),
+        ]
+
+    weights = [weight_copies(j) for j in range(count)]
+
+    def rows_copy(k):
         peer = lax.rem(me + k, WIDE)
         return remote(
-            ins[j].at[peer], outs[j].at[me], send.at[k, j], recv.at[k, j], {"wide": peer}
-        )
+            packed.at[peer], got_ref.at[me], send.at[k, 0], recv.at[k, 0], {"wide": peer}
+        )
+
+    def codes_copy(k):
+        peer = lax.rem(me + k, WIDE)
+        return remote(
+            codes_ref.at[peer], got_codes_ref.at[me], send.at[k, 1], recv.at[k, 1], {"wide": peer}
+        )
+
+    pl.semaphore_wait(barrier, WIDE + 1)
+    for j in range(count):
+        weights[j][0].start()
+        weights[j][1].start()
 
     @pl.loop(1, WIDE)
     def _(k):
-        for j in range(count):
-            copy(k, j).start()
-
+        gather_bucket(0, lambda s: source_ref[s], wide, staged, packed, lax.rem(me + k, WIDE))
+        rows_copy(k).start()
+        codes_copy(k).start()
+
+    gather_bucket(0, lambda s: source_ref[s], wide, staged, packed, me)
+    mine = [
+        pltpu.make_async_copy(packed.at[me], got_ref.at[me], own.at[0]),
+        pltpu.make_async_copy(codes_ref.at[me], got_codes_ref.at[me], own.at[1]),
+    ]
     for j in range(count):
-        mine = pltpu.make_async_copy(ins[j].at[me], outs[j].at[me], own.at[j])
-        mine.start()
-        mine.wait()
+        mine.append(
+            pltpu.make_async_copy(own_every(j, shards[j]), every(j, full[j], mp), w_own.at[j])
+        )
+    for copy in mine:
+        copy.start()
+    for j in range(count):
+        weights[j][0].wait_recv()
+        weights[j][2].start()
+        weights[j][4].start()
+        weights[j][1].wait_recv()
+        weights[j][3].start()
+        weights[j][5].start()
+    for j in range(count):
+        weights[j][2].wait_recv()
+        weights[j][6].start()
+        weights[j][3].wait_recv()
+        weights[j][7].start()
+    for copy in mine:
+        copy.wait()
 
     @pl.loop(1, WIDE)
     def _(k):
-        for j in range(count):
-            copy(k, j).wait()
-
-
-def shuffle(arrays, collective):
-    count = len(arrays)
-    return pl.pallas_call(
-        functools.partial(shuffle_kernel, count),
-        out_shape=[shape(a.shape, a.dtype) for a in arrays],
-        in_specs=[ANY] * count,
-        out_specs=[ANY] * count,
+        rows_copy(k).wait()
+        codes_copy(k).wait()
+
+    for j in range(count):
+        for kind in range(4):
+            weights[j][kind].wait_send()
+        for kind in range(4, 8):
+            weights[j][kind].wait()
+
+
+def send_rows(source, points, codes, weights, collective):
+    return pl.pallas_call(
+        send_kernel,
+        out_shape=[
+            shape((WIDE, CAP, LOCAL), BF16),
+            shape((WIDE, 2, 128), I32),
+            shape((3 * WIDTH, WIDTH), BF16),
+            shape((MP, LOCAL, WIDTH), BF16),
+            shape((MP, 2 * WIDTH, WIDTH), BF16),
+            shape((MP, WIDTH, WIDTH), BF16),
+            shape((MP, 2 * LOCAL, WIDTH), BF16),
+        ],
+        in_specs=[SMEM, VMEM] + [ANY] * 6,
+        out_specs=[ANY] * 7,
         scratch_shapes=[
-            pltpu.SemaphoreType.DMA((WIDE, count)),
-            pltpu.SemaphoreType.DMA((WIDE, count)),
-            pltpu.SemaphoreType.DMA((count,)),
+            pltpu.VMEM((ROWS, LOCAL), F32),
+            pltpu.VMEM((1, CAP, LOCAL), F32),
+            pltpu.VMEM((WIDE, CAP, LOCAL), BF16),
+            pltpu.SemaphoreType.DMA((WIDE, 2)),
+            pltpu.SemaphoreType.DMA((WIDE, 2)),
+            pltpu.SemaphoreType.DMA((2,)),
+            pltpu.SemaphoreType.DMA((5, 8)),
+            pltpu.SemaphoreType.DMA((5, 8)),
+            pltpu.SemaphoreType.DMA((5,)),
         ],
         compiler_params=params(collective),
-    )(*arrays)
+    )(source, points, codes, *weights)
+
+
+def return_kernel(
+    code_ref, state_ref, mixed_ref, w_ref, got_ref,
+    tiles, turned, wide, staged, packed, send, recv, own, m_send, m_recv, m_own,
+):
+    me = lax.axis_index("wide")
+    mp = lax.axis_index("mp")
+    barrier = pltpu.get_barrier_semaphore()
+
+    @pl.loop(1, WIDE)
+    def _(k):
+        pl.semaphore_signal(
+            barrier, inc=1, device_id={"wide": lax.rem(me + k, WIDE)}, device_id_type=MESH
+        )
+
+    for k in range(1, MP):
+        pl.semaphore_signal(
+            barrier, inc=1, device_id={"mp": lax.rem(mp + k, MP)}, device_id_type=MESH
+        )
+
+    lifted = []
+    for level, rows in ((0, slice(0, ONE)), (1, slice(ONE, COARSE))):
+        total = jnp.zeros((rows.stop - rows.start, WIDTH), F32)
+        for g in range(MP):
+            total = total + dot(
+                mixed_ref[rows, g * LOCAL : (g + 1) * LOCAL],
+                w_ref[g, level * LOCAL : (level + 1) * LOCAL, :],
+            )
+        lifted.append(total.astype(BF16))
+    one, two = lifted
+    r = lax.broadcasted_iota(I32, (BALL, 96), 0)
+    c = lax.broadcasted_iota(I32, (BALL, 96), 1)
+    hot = jnp.logical_or(
+        jnp.logical_and(c < 64, r // 4 == c), jnp.logical_and(c >= 64, r // 8 == c - 64)
+    )
+    hot = jnp.where(hot, 1.0, 0.0).astype(BF16)
+
+    def turn(k, t):
+        peer = lax.rem(mp + k, MP)
+        begin = pl.multiple_of(mp * QUARTER + t * BALL, BALL)
+        return remote(
+            tiles.at[pl.ds(t * BALL, BALL), pl.ds(pl.multiple_of(peer * LOCAL, LOCAL), LOCAL)],
+            turned.at[pl.ds(begin, BALL), :],
+            m_send.at[k, t],
+            m_recv.at[k, t],
+            {"mp": peer},
+        )
+
+    mine = []
+    for t in range(QUARTER // BALL):
+        both = jnp.concatenate([one[t * 64 : (t + 1) * 64], two[t * 32 : (t + 1) * 32]], 0)
+        at = slice(t * BALL, (t + 1) * BALL)
+        tiles[at, :] = (state_ref[at, :] + dot(hot, both)).astype(BF16)
+        if t == 0:
+            pl.semaphore_wait(barrier, WIDE - 1 + MP - 1)
+        for k in (2, 1, 3):
+            turn(k, t).start()
+        mine.append(
+            pltpu.make_async_copy(
+                tiles.at[at, pl.ds(pl.multiple_of(mp * LOCAL, LOCAL), LOCAL)],
+                turned.at[pl.ds(pl.multiple_of(mp * QUARTER + t * BALL, BALL), BALL), :],
+                m_own.at[t],
+            )
+        )
+        mine[-1].start()
+    for t in range(QUARTER // BALL):
+        mine[t].wait()
+        for k in (1, 3, 2):
+            turn(k, t).wait()
+    widen(turned, wide, ROWS)
+    wide[ROWS : ROWS + 8, :] = jnp.zeros((8, LOCAL), F32)
+
+    def rows_copy(k):
+        peer = lax.rem(me + k, WIDE)
+        return remote(packed.at[peer], got_ref.at[me], send.at[k], recv.at[k], {"wide": peer})
+
+    @pl.loop(1, WIDE)
+    def _(k):
+        gather_bucket(0, lambda s: code_ref[s] >> 1, wide, staged, packed, lax.rem(me + k, WIDE))
+        rows_copy(k).start()
+
+    gather_bucket(0, lambda s: code_ref[s] >> 1, wide, staged, packed, me)
+    last = pltpu.make_async_copy(packed.at[me], got_ref.at[me], own)
+    last.start()
+    last.wait()
+
+    @pl.loop(1, WIDE)
+    def _(k):
+        rows_copy(k).wait()
+
+
+def return_rows(codes, state, mixed, w_lift, collective):
+    return pl.pallas_call(
+        return_kernel,
+        out_shape=shape((WIDE, CAP, LOCAL), BF16),
+        in_specs=[SMEM, VMEM, VMEM, VMEM],
+        out_specs=ANY,
+        scratch_shapes=[
+            pltpu.VMEM((QUARTER, WIDTH), BF16),
+            pltpu.VMEM((ROWS, LOCAL), BF16),
+            pltpu.VMEM((ROWS + 8, LOCAL), F32),
+            pltpu.VMEM((1, CAP, LOCAL), F32),
+            pltpu.VMEM((WIDE, CAP, LOCAL), BF16),
+            pltpu.SemaphoreType.DMA((WIDE,)),
+            pltpu.SemaphoreType.DMA((WIDE,)),
+            pltpu.SemaphoreType.DMA,
+            pltpu.SemaphoreType.DMA((MP, 4)),
+            pltpu.SemaphoreType.DMA((MP, 4)),
+            pltpu.SemaphoreType.DMA((4,)),
+        ],
+        compiler_params=params(collective),
+    )(codes, state, mixed, w_lift)
 
 
 def swap_kernel(pick, place, src, dst, send, recv, own):
@@ -457,58 +710,24 @@
     )(one, two, mate_one, mate_two, keep, mate_keep)
 
 
-def lift_kernel(state_ref, mixed_ref, w_ref, out_ref):
-    one = dot(mixed_ref[0:ONE, :], w_ref[0]).astype(BF16)
-    two = dot(mixed_ref[ONE:COARSE, :], w_ref[1]).astype(BF16)
-    for t in range(QUARTER // BALL):
-        both = jnp.concatenate([one[t * 64 : (t + 1) * 64], two[t * 32 : (t + 1) * 32]], 0)
-        r = lax.broadcasted_iota(I32, (BALL, 96), 0)
-        c = lax.broadcasted_iota(I32, (BALL, 96), 1)
-        hot = jnp.logical_or(
-            jnp.logical_and(c < 64, r // 4 == c), jnp.logical_and(c >= 64, r // 8 == c - 64)
-        )
-        spread = dot(jnp.where(hot, 1.0, 0.0).astype(BF16), both)
-        at = slice(t * BALL, (t + 1) * BALL)
-        out_ref[at, :] = (state_ref[at, :] + spread).astype(BF16)
-
-
-def lift(state, mixed, w_coarse_out):
-    return pl.pallas_call(
-        lift_kernel,
-        out_shape=shape((QUARTER, WIDTH), BF16),
-        in_specs=[VMEM] * 3,
-        out_specs=VMEM,
-        compiler_params=params(),
-    )(state, mixed, w_coarse_out)
-
-
 def on_device(points, mask, perm, w_qkv, w_out, w_gate_up, w_down, w_coarse, w_coarse_out):
-    full_qkv = lax.all_gather(w_qkv, "mp", axis=2, tiled=True)
-    full_out = lax.all_gather(w_out, "mp", axis=0, tiled=True)
-    full_gate_up = lax.all_gather(w_gate_up, "mp", axis=0)
-    full_down = lax.all_gather(w_down, "mp", axis=0)
-    full_coarse_out = lax.all_gather(w_coarse_out, "mp", axis=1, tiled=True)
-
-    slot, code = pl.pallas_call(
-        rank_kernel,
-        out_shape=[shape((16, 256), I32)] * 2,
-        in_specs=[VMEM] * 2,
-        out_specs=[VMEM] * 2,
-        compiler_params=params(),
-    )(perm.reshape(16, 256), mask.reshape(16, 256))
-    slot = slot.reshape(ROWS)
-    code = code.reshape(ROWS)
-    rows, codes = pl.pallas_call(
-        pack_kernel,
-        out_shape=[shape((SLOTS, LOCAL), BF16), shape((SLOTS,), I32)],
-        in_specs=[SMEM, SMEM, VMEM, ANY],
-        out_specs=[VMEM, SMEM],
-        scratch_shapes=[pltpu.VMEM((ROWS, LOCAL), F32), pltpu.VMEM((SLOTS, LOCAL), F32)],
-        compiler_params=params(),
-    )(slot, code, points, jnp.full((SLOTS,), 2 * ROWS, I32))
-    got, got_code = shuffle(
-        [rows.reshape(WIDE, CAP, LOCAL), codes.reshape(WIDE, 2, 128)], 1
+    slot, source, codes = index(perm, mask)
+    got, got_code, full_qkv, full_out, full_gate_up, full_down, full_lift = send_rows(
+        source,
+        points,
+        codes.reshape(WIDE, 2, 128),
+        [
+            w_qkv.reshape(3 * WIDTH, LOCAL),
+            w_out,
+            w_gate_up.reshape(2 * WIDTH, WIDTH),
+            w_down,
+            w_coarse_out.reshape(2 * LOCAL, WIDTH),
+        ],
+        1,
     )
+    full_qkv = full_qkv.reshape(3, WIDTH, WIDTH)
+    full_out = full_out.reshape(WIDTH, WIDTH)
+    full_gate_up = full_gate_up.reshape(MP, 2, WIDTH, WIDTH)
     got_code = got_code.reshape(SLOTS)
     owned, owned_mask = pl.pallas_call(
         unpack_kernel,
@@ -535,17 +754,7 @@
     fed = forward(state, full_gate_up, full_down)
     mixed = coarse(one, two, mate_one, mate_two, keep, mate_keep)
     all_mixed = swap(mixed, shape((COARSE, WIDTH), BF16), block, columns, 5)
-    result = lift(fed, all_mixed, full_coarse_out)
-    updated = swap(result, shape((MP, QUARTER, LOCAL), BF16), columns, block, 6)
-    back = pl.pallas_call(
-        repack_kernel,
-        out_shape=shape((SLOTS, LOCAL), BF16),
-        in_specs=[SMEM, VMEM],
-        out_specs=VMEM,
-        scratch_shapes=[pltpu.VMEM((ROWS + 8, LOCAL), F32), pltpu.VMEM((SLOTS, LOCAL), F32)],
-        compiler_params=params(),
-    )(got_code, updated.reshape(ROWS, LOCAL))
-    (returned,) = shuffle([back.reshape(WIDE, CAP, LOCAL)], 7)
+    returned = return_rows(got_code, fed, all_mixed, full_lift, 6)
     return pl.pallas_call(
         finish_kernel,
         out_shape=shape((ROWS, LOCAL), F32),
@@ -553,7 +762,7 @@
         out_specs=VMEM,
         scratch_shapes=[pltpu.VMEM((SLOTS, LOCAL), F32)],
         compiler_params=params(),
-    )(slot, returned.reshape(SLOTS, LOCAL))
+    )(slot.reshape(ROWS), returned.reshape(SLOTS, LOCAL))
 
 
 def solution(mesh):

time: 323 us -> 305 us (0.944)
  blocking collectives: 14.2 us -> 0 us
  between operations: 13.3 us -> 0.14 us
  Pallas kernels: 283 us -> 294 us
    pallas_call x6 -> x3, Pallas kernels: 119 us -> 167 us  [the longest x1 94 us: send_rows(): pl.pallas_call(send_kernel, out_shape=[shape((WIDE, CAP, LOCAL), BF16), s...]
    pallas_call x4 -> x3, Pallas kernels: 78.4 us -> 45.8 us  [swap(): pl.pallas_call(functools.partial(swap_kernel, pick, place), out_shape=out...]
    all_gather x1 -> x0, blocking collectives: 14.2 us -> none  [on_device(): full_out = lax.all_gather(w_out, 'mp', axis=0, tiled=True)]
  transfers between devices with their start and end apart: 4 -> 0, of which waited for: 0 -> 0; matrix products, arithmetic and copies ran while one was open for 2% -> 0% of each run, Pallas kernels for 62% -> 0%
where the time goes in v2:
time: 305 us; the launch traced here: 302 us
  Pallas kernels  294 us (96%)
  local copies, waits for them, and re-layouts  6.57 us (2%)
    pallas_call x1, Pallas kernels, send_rows(): pl.pallas_call(send_kernel, out_shape=[shape((WIDE, CAP, LOCAL), BF16), s...  94 us
    pallas_call x1, Pallas kernels, return_rows(): pl.pallas_call(return_kernel, out_shape=shape((WIDE, CAP, LOCAL), BF16),...  49.7 us
    pallas_call x3, Pallas kernels, swap(): pl.pallas_call(functools.partial(swap_kernel, pick, place), out_shape=out...  45.8 us
    pallas_call x1, Pallas kernels, index(): pl.pallas_call(index_kernel, out_shape=[shape((16, 256), I32), shape((SLO...  23.6 us
    pallas_call x1, Pallas kernels, on_device(): pl.pallas_call(unpack_kernel, out_shape=[shape((ROWS, LOCAL), BF16), shap...  17.8 us
    pallas_call x1, Pallas kernels, exchange(): pl.pallas_call(exchange_kernel, out_shape=[shape((2, 4 * ONE, LOCAL), BF1...  15.4 us
    pallas_call x1, Pallas kernels, forward(): pl.pallas_call(forward_kernel, grid=(tiles,), out_shape=shape((QUARTER, W...  12.8 us
    pallas_call x1, Pallas kernels, coarse(): pl.pallas_call(coarse_kernel, out_shape=shape((MP, COARSE, LOCAL), BF16),...  12.6 us

profile of v2, /device:TPU:1, one launch (start us, length us, event | category | flops | bytes accessed | tf_op | source)
XLA Modules:
  0.0 301.5 jit_solution(10277652235404766450)
XLA Ops:
  0.0 1.3 reshape.76.mask_ref
  1.3 1.3 reshape.75.perm_ref
  2.6 0.7 broadcast_in_dim.8.blank_ref
  3.4 23.6 %shard_map.100 = (s32[16,256]{1,0:T(8,128)}, s32[8192]{0:T(1024)}, s32[8192]{0:T(1024)}) custom-call(s32[16,256]{1,0:T(8,128)} %reshape.75.perm_ref, s32[16,256]{1,0:T(8,128)} %reshape.76.mask_ref, s32[2,8192]{1,0:T(2,128)} %broadcast_in_dim.8.blank_ref), custom_call_target="tpu_custom_call" | custom-call | tf_op jit(solution)/shard_map/pallas_call | solution.py:107
  27.0 1.3 copy.11
  28.3 94.0 %shard_map.101 = (bf16[32,256,128]{2,1,0:T(8,128)(2,1)}, s32[32,2,128]{2,1,0:T(2,128)}, bf16[1536,512]{1,0:T(8,128)(2,1)}, bf16[4,128,512]{2,1,0:T(8,128)(2,1)},...) custom-call(s32[8192]{0:T(1024)} %get-tuple-element.25.source_ref, ...), custom_call_target="tpu_custom_call" | custom-call | tf_op jit(solution)/shard_map/pallas_call | solution.py:321
  122.3 17.8 %shard_map.102 = (bf16[4096,128]{1,0:T(8,128)(2,1)}, s32[4224]{0:T(1024)}) custom-call(s32[8192]{0:T(1024)} %bitcast.24, bf16[8192,128]{1,0:T(8,128)(2,1)} %bitcast.17), custom_call_target="tpu_custom_call" | custom-call | tf_op jit(solution)/shard_map/pallas_call | solution.py:732
  140.1 0.0 copy-start
  140.1 16.3 %shard_map.103.x_ref = bf16[1024,512]{1,0:T(8,128)(2,1)} custom-call(bf16[4,1024,128]{2,1,0:T(8,128)(2,1)} %bitcast.20), custom_call_target="tpu_custom_call" | custom-call | tf_op jit(solution)/shard_map/pallas_call | solution.py:479
  156.5 0.0 copy-done
  156.5 0.6 constant_dynamic-slice_fusion
  157.1 10.0 %shard_map.104 = (f32[1024,512]{1,0:T(8,128)}, bf16[4,96,512]{2,1,0:T(8,128)(2,1)}) custom-call(bf16[1024,512]{1,0:T(8,128)(2,1)} %shard_map.103.x_ref, s32[4,1,256]{2,1,0:T(1,128)} %bitcast.28, bf16[3,512,512]{2,1,0:T(8,128)(2,1)} %bitcast.18, bf16[512,512]{1,0:T(8,128)(2,1)} %bitcast.21), custom_call_target="tpu_custom_call" | custom-call | tf_op jit(solution)/shard_map/pallas_call | solution.py:551
  167.1 12.8 %shard_map.105.state_ref = f32[1024,512]{1,0:T(8,128)} custom-call(f32[1024,512]{1,0:T(8,128)} %get-tuple-element.33.state_ref, bf16[4,2,512,512]{3,2,1,0:T(8,128)(2,1)} %bitcast.14, bf16[4,2,512,512]{3,2,1,0:T(8,128)(2,1)} %bitcast.15, bf16[4,512,512]{2,1,0:T(8,128)(2,1)} %get-tuple-element.35.down_ref), custom_call_target="tpu_custom_call" | custom-call | tf_op jit(solution)/shard_map/pallas_call | solution.py:583
  179.8 0.2 reshape.91
  180.0 0.1 reduce_sum.19
  180.2 0.5 reshape.90
  180.7 0.2 reduce_sum.18
  180.9 0.6 reshape.96.keep
  181.5 20.5 %shard_map.106.rows_ref = bf16[4,4,96,512]{3,2,1,0:T(8,128)(2,1)} custom-call(bf16[4,96,512]{2,1,0:T(8,128)(2,1)} %get-tuple-element.36.src), custom_call_target="tpu_custom_call" | custom-call | tf_op jit(solution)/shard_map/pallas_call | solution.py:479
  202.1 5.0 %shard_map.107 = (bf16[3,1024,128]{2,1,0:T(8,128)(2,1)}, bf16[3,512,128]{2,1,0:T(8,128)(2,1)}) custom-call(bf16[4,4,96,512]{3,2,1,0:T(8,128)(2,1)} %shard_map.106.rows_ref, bf16[2,3,512,128]{3,2,1,0:T(8,128)(2,1)} %w_ref.1), custom_call_target="tpu_custom_call" | custom-call | tf_op jit(solution)/shard_map/pallas_call | solution.py:612
  207.1 15.4 %shard_map.108 = (bf16[2,1024,128]{2,1,0:T(8,128)(2,1)}, bf16[3,2,512,128]{3,2,1,0:T(8,128)(2,1)}, s32[3,1,1536]{2,1,0:T(1,128)}) custom-call(bf16[3,1024,128]{2,1,0:T(8,128)(2,1)} %get-tuple-element.37.one, bf16[3,512,128]{2,1,0:T(8,128)(2,1)} %get-tuple-element.38.two, s32[1,1536]{1,0:T(1,128)} %reshape.96.keep), custom_call_target="tpu_custom_call" | custom-call | tf_op jit(solution)/shard_map/pallas_call | solution.py:659
  222.5 12.6 %shard_map.109.src = bf16[4,384,128]{2,1,0:T(8,128)(2,1)} custom-call(bf16[3,1024,128]{2,1,0:T(8,128)(2,1)} %get-tuple-element.37.one, bf16[3,512,128]{2,1,0:T(8,128)(2,1)} %get-tuple-element.38.two, bf16[2,1024,128]{2,1,0:T(8,128)(2,1)} %get-tuple-element.39.mate_one, bf16[3,2,512,128]{3,2,1,0:T(8,128)(2,1)} %get-tuple-element.40.mate_two, ...), custom_call_target="tpu_custom_call" | custom-call | tf_op jit(solution)/shard_map/pallas_call | solution.py:704
  235.1 8.9 %shard_map.110.mixed_ref = bf16[384,512]{1,0:T(8,128)(2,1)} custom-call(bf16[4,384,128]{2,1,0:T(8,128)(2,1)} %shard_map.109.src), custom_call_target="tpu_custom_call" | custom-call | tf_op jit(solution)/shard_map/pallas_call | solution.py:479
  244.0 49.7 %shard_map.111 = bf16[32,256,128]{2,1,0:T(8,128)(2,1)} custom-call(s32[8192]{0:T(1024)} %bitcast.25, f32[1024,512]{1,0:T(8,128)} %shard_map.105.state_ref, bf16[384,512]{1,0:T(8,128)(2,1)} %shard_map.110.mixed_ref, bf16[4,256,512]{2,1,0:T(8,128)(2,1)} %get-tuple-element.42.w_ref), custom_call_target="tpu_custom_call" | custom-call | tf_op jit(solution)/shard_map/pallas_call | solution.py:440
  293.7 7.8 %shard_map.112 = f32[4096,128]{1,0:T(8,128)} custom-call(s32[4096]{0:T(1024)} %bitcast.26, bf16[8192,128]{1,0:T(8,128)(2,1)} %bitcast.16), custom_call_target="tpu_custom_call" | custom-call | tf_op jit(solution)/shard_map/pallas_call | solution.py:758
  (6 shorter events, 0.0 us)
Async XLA Ops:
  140.1 16.3 %copy-start = (s32[4224]{0:T(1024)S(1)}, s32[4224]{0:T(1024)}, u32[]{:S(2)}) copy-start(s32[4224]{0:T(1024)} %get-tuple-element.30) | copy-start | bytes 50692

commit v3 on v2

--- a/solution.py
+++ b/solution.py
@@ -58,66 +58,79 @@
 NONE = 2 * ROWS
 
 
-def index_kernel(
-    perm_ref, mask_ref, blank_ref, slot_ref, source_ref, codes_ref, slots, codes, slot_s, code_s, sems
-):
-    blanks = [
-        pltpu.make_async_copy(blank_ref.at[0], source_ref, sems.at[0]),
-        pltpu.make_async_copy(blank_ref.at[1], codes_ref, sems.at[1]),
-    ]
-    for copy in blanks:
-        copy.start()
+def index_kernel(perm_ref, mask_ref, slot_ref, source_ref, codes_ref):
     perm = perm_ref[...]
     target = perm >> 12
-    codes[...] = (perm & (ROWS - 1)) * 2 + mask_ref[...]
+    code = (perm & (ROWS - 1)) * 2 + mask_ref[...]
     rows = lax.broadcasted_iota(I32, (256, 256), 0)
     cols = lax.broadcasted_iota(I32, (256, 256), 1)
     upper = jnp.where(rows < cols, 1.0, 0.0).astype(BF16)
     which = lax.broadcasted_iota(I32, (WIDE, 256), 0)
+    lane = lax.broadcasted_iota(I32, (1, 256), 1).astype(F32)
     carry = jnp.zeros((WIDE, 1), F32)
+    found = jnp.zeros((5 * WIDE, CAP), F32)
     for c in range(ROWS // 256):
-        hot = jnp.where(which == target[c : c + 1, :], 1.0, 0.0)
+        row = slice(c, c + 1)
+        hot = jnp.where(which == target[row, :], 1.0, 0.0)
         before = dot(hot.astype(BF16), upper) + carry
-        rank = jnp.sum(hot * before, 0, keepdims=True)
-        slots[c : c + 1, :] = target[c : c + 1, :] * CAP + rank.astype(I32)
+        rank = jnp.sum(hot * before, 0, keepdims=True).astype(I32)
+        slot_ref[row, :] = target[row, :] * CAP + rank
         carry = carry + jnp.sum(hot, 1, keepdims=True)
-    slot_ref[...] = slots[...]
-    moves = [
-        pltpu.make_async_copy(slots, slot_s, sems.at[2]),
-        pltpu.make_async_copy(codes, code_s, sems.at[3]),
-    ]
-    for copy in moves:
-        copy.start()
-    for copy in blanks + moves:
-        copy.wait()
-    for c in range(ROWS // 256):
-
-        @pl.loop(0, 256 // UNROLL)
-        def _(i):
-            base = i * UNROLL
-            at = [slot_s[c, base + u] for u in range(UNROLL)]
-            code = [code_s[c, base + u] for u in range(UNROLL)]
-            for u in range(UNROLL):
-                source_ref[at[u]] = c * 256 + base + u
-                codes_ref[at[u]] = code[u]
+        placed = jnp.where(rows == rank, 1.0, 0.0).astype(BF16)
+        high = (code[row, :] >> 6).astype(F32)
+        low = (code[row, :] & 63).astype(F32)
+        values = jnp.concatenate([hot * lane, hot * float(c), hot * high, hot * low, hot], 0)
+        found = found + dot_t(values.astype(BF16), placed)
+    source = found[:WIDE] + found[WIDE : 2 * WIDE] * 256.0
+    source_ref[...] = source.astype(I32)
+    codes = found[2 * WIDE : 3 * WIDE] * 64.0 + found[3 * WIDE : 4 * WIDE]
+    codes_ref[...] = jnp.where(found[4 * WIDE :] > 0.5, codes.astype(I32), NONE)
 
 
 def index(perm, mask):
-    blank = jnp.broadcast_to(jnp.array([[0], [NONE]], I32), (2, SLOTS))
     return pl.pallas_call(
         index_kernel,
-        out_shape=[shape((16, 256), I32), shape((SLOTS,), I32), shape((SLOTS,), I32)],
-        in_specs=[VMEM, VMEM, ANY],
-        out_specs=[VMEM, SMEM, SMEM],
-        scratch_shapes=[
-            pltpu.VMEM((16, 256), I32),
-            pltpu.VMEM((16, 256), I32),
-            pltpu.SMEM((16, 256), I32),
-            pltpu.SMEM((16, 256), I32),
-            pltpu.SemaphoreType.DMA((4,)),
-        ],
+        out_shape=[shape((16, 256), I32), shape((WIDE, CAP), I32), shape((WIDE, CAP), I32)],
+        in_specs=[VMEM] * 2,
+        out_specs=[VMEM] * 3,
         compiler_params=params(),
-    )(perm.reshape(16, 256), mask.reshape(16, 256), blank)
+    )(perm.reshape(16, 256), mask.reshape(16, 256))
+
+
+def inverse_kernel(codes_ref, slot_ref, mask_ref, keep_ref):
+    balls = ROWS // BALL
+    rows = lax.broadcasted_iota(I32, (256, 256), 0)
+    which = lax.broadcasted_iota(I32, (balls, 256), 0)
+    lane = lax.broadcasted_iota(I32, (1, 256), 1).astype(F32)
+    found = jnp.zeros((3 * balls, 256), F32)
+    for c in range(WIDE):
+        code = codes_ref[c : c + 1, :]
+        landing = code >> 1
+        hot = jnp.where(which == (landing >> 8), 1.0, 0.0)
+        placed = jnp.where(rows == (landing & 255), 1.0, 0.0).astype(BF16)
+        real = (code & 1).astype(F32)
+        values = jnp.concatenate([hot * lane, hot * float(c), hot * real], 0)
+        found = found + dot_t(values.astype(BF16), placed)
+    slot_ref[...] = (found[:balls] + found[balls : 2 * balls] * 256.0).astype(I32)
+    mask = found[2 * balls :]
+    mask_ref[...] = mask.astype(I32)
+    r = lax.broadcasted_iota(I32, (256, 96), 0)
+    c = lax.broadcasted_iota(I32, (256, 96), 1)
+    hot = jnp.logical_or(
+        jnp.logical_and(c < 64, r // 4 == c), jnp.logical_and(c >= 64, r // 8 == c - 64)
+    )
+    counts = dot(mask.astype(BF16), jnp.where(hot, 1.0, 0.0).astype(BF16))
+    keep_ref[...] = jnp.where(counts > 0.5, 1, 0)
+
+
+def inverse(codes):
+    return pl.pallas_call(
+        inverse_kernel,
+        out_shape=[shape((16, 256), I32), shape((16, 256), I32), shape((16, 96), I32)],
+        in_specs=[VMEM],
+        out_specs=[VMEM] * 3,
+        compiler_params=params(),
+    )(codes)
 
 
 def widen(src, dst, rows):
@@ -125,25 +138,6 @@
     def _(i):
         at = pl.ds(pl.multiple_of(i * 256, 256), 256)
         dst[at, :] = src[at, :].astype(dst.dtype)
-
-
-def unpack_kernel(code_ref, got_ref, rows_ref, mask_ref, wide, owned):
-    widen(got_ref, wide, SLOTS)
-
-    @pl.loop(0, SLOTS // UNROLL)
-    def _(i):
-        base = i * UNROLL
-
-        @pl.when(code_ref[base] < NONE)
-        def _():
-            codes = [code_ref[base + u] for u in range(UNROLL)]
-            lines = [wide[pl.ds(base + u, 1), :] for u in range(UNROLL)]
-            for u in range(UNROLL):
-                owned[pl.ds(codes[u] >> 1, 1), :] = lines[u]
-            for u in range(UNROLL):
-                mask_ref[codes[u] >> 1] = codes[u] & 1
-
-    widen(owned, rows_ref, ROWS)
 
 
 def finish_kernel(slot_ref, got_ref, out_ref, wide):
@@ -329,7 +323,7 @@
             shape((MP, WIDTH, WIDTH), BF16),
             shape((MP, 2 * LOCAL, WIDTH), BF16),
         ],
-        in_specs=[SMEM, VMEM] + [ANY] * 6,
+        in_specs=[SMEM, VMEM, ANY] + [VMEM] * 5,
         out_specs=[ANY] * 7,
         scratch_shapes=[
             pltpu.VMEM((ROWS, LOCAL), F32),
@@ -516,15 +510,14 @@
     return jnp.where(low, mixed[0], mixed[1])
 
 
-def fine_kernel(x_ref, mask_ref, qkv_ref, out_ref, state_ref, coarse_ref):
-    x = x_ref[...].astype(F32)
+def fine_ball(x, real, qkv_ref, out_ref):
+    x = x.astype(F32)
     normed = norm(x).astype(BF16)
     q = (dot(normed, qkv_ref[0]) * 0.125).astype(BF16)
     k = dot(normed, qkv_ref[1]).astype(BF16)
     v = dot(normed, qkv_ref[2]).astype(BF16)
     rows = lax.broadcasted_iota(I32, (BALL, BALL), 0)
     cols = lax.broadcasted_iota(I32, (BALL, BALL), 1)
-    real = mask_ref[0] > 0
     allowed = jnp.logical_or(real, rows == cols)
     low = lax.broadcasted_iota(I32, (BALL, 128), 1) < 64
     mixed = []
@@ -532,10 +525,10 @@
         at = slice(g * 128, (g + 1) * 128)
         mixed.append(attend_pair(q[:, at], [(k[:, at], v[:, at], allowed)], low).astype(BF16))
     state = x + dot(jnp.concatenate(mixed, 1), out_ref[...])
-    state_ref[...] = state
     high = state.astype(BF16)
     rest = (state - high.astype(F32)).astype(BF16)
-    for f, begin in ((4, 0), (8, BALL // 4)):
+    coarse = []
+    for f in (4, 8):
         count_rows = BALL // f
         r = lax.broadcasted_iota(I32, (count_rows, BALL), 0)
         c = lax.broadcasted_iota(I32, (count_rows, BALL), 1)
@@ -543,56 +536,136 @@
         counted = jnp.sum(hot, 1, keepdims=True)
         hot = hot.astype(BF16)
         pooled = (dot(hot, high) + dot(hot, rest)) / jnp.maximum(counted, 1.0)
-        coarse_ref[0, begin : begin + count_rows, :] = norm(pooled).astype(BF16)
-
-
-def fine(x, mask, w_qkv, w_out):
-    balls = QUARTER // BALL
+        coarse.append(norm(pooled).astype(BF16))
+    return state, coarse
+
+
+BALLS = QUARTER // BALL
+
+
+def fine_kernel(
+    slot_ref, got_ref, mask_ref, qkv_hbm, out_hbm, gate_up_hbm, down_hbm, fed_ref, coarse_ref,
+    wide, staged, packed, x, state, pooled, qkv_ref, out_ref, gate_up_ref, down_ref,
+    send, recv, own, c_send, c_recv, c_own, loads,
+):
+    mp = lax.axis_index("mp")
+    barrier = pltpu.get_barrier_semaphore()
+    for k in range(1, MP):
+        pl.semaphore_signal(
+            barrier, inc=1, device_id={"mp": lax.rem(mp + k, MP)}, device_id_type=MESH
+        )
+    load = [
+        pltpu.make_async_copy(qkv_hbm, qkv_ref, loads.at[0]),
+        pltpu.make_async_copy(out_hbm, out_ref, loads.at[1]),
+        pltpu.make_async_copy(gate_up_hbm, gate_up_ref, loads.at[2]),
+        pltpu.make_async_copy(down_hbm, down_ref, loads.at[3]),
+    ]
+    for copy in load:
+        copy.start()
+    widen(got_ref, wide, SLOTS)
+    pl.semaphore_wait(barrier, MP - 1)
+
+    def place(t):
+        return x.at[
+            pl.ds(pl.multiple_of(t * BALL, BALL), BALL),
+            pl.ds(pl.multiple_of(mp * LOCAL, LOCAL), LOCAL),
+        ]
+
+    def turn(k, t):
+        peer = lax.rem(mp + k, MP)
+        return remote(
+            packed.at[peer * BALLS + t], place(t), send.at[k, t], recv.at[k, t], {"mp": peer}
+        )
+
+    def keep(t):
+        return pltpu.make_async_copy(packed.at[mp * BALLS + t], place(t), own.at[t])
+
+    @pl.loop(0, BALLS)
+    def _(t):
+        for k in (2, 1, 3):
+            peer = lax.rem(mp + k, MP)
+            gather_bucket(0, lambda s: slot_ref[s], wide, staged, packed, peer * BALLS + t)
+            turn(k, t).start()
+        gather_bucket(0, lambda s: slot_ref[s], wide, staged, packed, mp * BALLS + t)
+        keep(t).start()
+
+    load[0].wait()
+    load[1].wait()
+
+    def share(k, t):
+        peer = lax.rem(mp + k, MP)
+        return remote(
+            pooled.at[t], coarse_ref.at[mp, t], c_send.at[k, t], c_recv.at[k, t], {"mp": peer}
+        )
+
+    def hold(t):
+        return pltpu.make_async_copy(pooled.at[t], coarse_ref.at[mp, t], c_own.at[t])
+
+    @pl.loop(0, BALLS)
+    def _(t):
+        for k in (1, 3, 2):
+            turn(k, t).wait_recv()
+        keep(t).wait()
+        at = pl.ds(pl.multiple_of(t * BALL, BALL), BALL)
+        real = mask_ref[pl.ds(mp * BALLS + t, 1), :] > 0
+        rows, coarse = fine_ball(x[at, :], real, qkv_ref, out_ref)
+        state[at, :] = rows
+        pooled[t, 0:64, :] = coarse[0]
+        pooled[t, 64:96, :] = coarse[1]
+        for k in (2, 1, 3):
+            share(k, t).start()
+        hold(t).start()
+
+    load[2].wait()
+    load[3].wait()
+
+    @pl.loop(0, BALLS)
+    def _(t):
+        at = pl.ds(pl.multiple_of(t * BALL, BALL), BALL)
+        fed_ref[at, :] = forward_tile(state[at, :], gate_up_ref, down_ref)
+
+    @pl.loop(0, BALLS)
+    def _(t):
+        hold(t).wait()
+        for k in (1, 3, 2):
+            turn(k, t).wait_send()
+            share(k, t).wait()
+
+
+def fine(slots, got, mask, w_qkv, w_out, w_gate_up, w_down, collective):
+    dma = pltpu.SemaphoreType.DMA
     return pl.pallas_call(
         fine_kernel,
-        grid=(balls,),
-        out_shape=[shape((QUARTER, WIDTH), F32), shape((balls, 96, WIDTH), BF16)],
-        in_specs=[
-            pl.BlockSpec((BALL, WIDTH), lambda i: (i, 0)),
-            pl.BlockSpec((1, 1, BALL), lambda i: (i, 0, 0)),
-            pl.BlockSpec((3, WIDTH, WIDTH), lambda i: (0, 0, 0)),
-            pl.BlockSpec((WIDTH, WIDTH), lambda i: (0, 0)),
+        out_shape=[shape((QUARTER, WIDTH), F32), shape((MP, BALLS, 96, WIDTH), BF16)],
+        in_specs=[SMEM, VMEM, VMEM] + [ANY] * 4,
+        out_specs=[VMEM, ANY],
+        scratch_shapes=[
+            pltpu.VMEM((SLOTS, LOCAL), F32),
+            pltpu.VMEM((1, CAP, LOCAL), F32),
+            pltpu.VMEM((MP * BALLS, BALL, LOCAL), BF16),
+            pltpu.VMEM((QUARTER, WIDTH), BF16),
+            pltpu.VMEM((QUARTER, WIDTH), F32),
+            pltpu.VMEM((BALLS, 96, WIDTH), BF16),
+            pltpu.VMEM((3, WIDTH, WIDTH), BF16),
+            pltpu.VMEM((WIDTH, WIDTH), BF16),
+            pltpu.VMEM((MP, 2, WIDTH, WIDTH), BF16),
+            pltpu.VMEM((MP, WIDTH, WIDTH), BF16),
+            dma((MP, BALLS)), dma((MP, BALLS)), dma((BALLS,)),
+            dma((MP, BALLS)), dma((MP, BALLS)), dma((BALLS,)), dma((4,)),
         ],
-        out_specs=[
-            pl.BlockSpec((BALL, WIDTH), lambda i: (i, 0)),
-            pl.BlockSpec((1, 96, WIDTH), lambda i: (i, 0, 0)),
-        ],
-        compiler_params=params(),
-    )(x, mask, w_qkv, w_out)
-
-
-def forward_kernel(state_ref, gate_ref, up_ref, down_ref, out_ref):
-    state = state_ref[...]
+        compiler_params=params(collective),
+    )(slots, got, mask, w_qkv, w_out, w_gate_up, w_down)
+
+
+def forward_tile(state, gate_up_ref, down_ref):
     normed = norm(state).astype(BF16)
     total = state
     for c in range(MP):
-        gate = dot(normed, gate_ref[c])
-        up = dot(normed, up_ref[c])
+        gate = dot(normed, gate_up_ref[c, 0])
+        up = dot(normed, gate_up_ref[c, 1])
         activated = (gate / (1.0 + jnp.exp(-gate)) * up).astype(BF16)
         total = total + dot(activated, down_ref[c])
-    out_ref[...] = total
-
-
-def forward(state, gate_up, down):
-    tiles = QUARTER // BALL
-    return pl.pallas_call(
-        forward_kernel,
-        grid=(tiles,),
-        out_shape=shape((QUARTER, WIDTH), F32),
-        in_specs=[
-            pl.BlockSpec((BALL, WIDTH), lambda i: (i, 0)),
-            pl.BlockSpec((MP, None, WIDTH, WIDTH), lambda i: (0, 0, 0, 0)),
-            pl.BlockSpec((MP, None, WIDTH, WIDTH), lambda i: (0, 1, 0, 0)),
-            pl.BlockSpec((MP, WIDTH, WIDTH), lambda i: (0, 0, 0)),
-        ],
-        out_specs=pl.BlockSpec((BALL, WIDTH), lambda i: (i, 0)),
-        compiler_params=params(),
-    )(state, gate_up, gate_up, down)
+    return total
 
 
 def project_kernel(rows_ref, w_ref, one_ref, two_ref):
@@ -713,7 +786,7 @@
 def on_device(points, mask, perm, w_qkv, w_out, w_gate_up, w_down, w_coarse, w_coarse_out):
     slot, source, codes = index(perm, mask)
     got, got_code, full_qkv, full_out, full_gate_up, full_down, full_lift = send_rows(
-        source,
+        source.reshape(SLOTS),
         points,
         codes.reshape(WIDE, 2, 128),
         [
@@ -728,30 +801,15 @@
     full_qkv = full_qkv.reshape(3, WIDTH, WIDTH)
     full_out = full_out.reshape(WIDTH, WIDTH)
     full_gate_up = full_gate_up.reshape(MP, 2, WIDTH, WIDTH)
+    landed, owned_mask, kept = inverse(got_code.reshape(WIDE, CAP))
     got_code = got_code.reshape(SLOTS)
-    owned, owned_mask = pl.pallas_call(
-        unpack_kernel,
-        out_shape=[shape((ROWS, LOCAL), BF16), shape((ROWS + 128,), I32)],
-        in_specs=[SMEM, VMEM],
-        out_specs=[VMEM, SMEM],
-        scratch_shapes=[pltpu.VMEM((SLOTS, LOCAL), F32), pltpu.VMEM((ROWS + 8, LOCAL), F32)],
-        compiler_params=params(),
-    )(got_code, got.reshape(SLOTS, LOCAL))
-    owned_mask = owned_mask[:ROWS]
-    keep_one = (jnp.sum(owned_mask.reshape(ROWS // 4, 4), 1) > 0).astype(I32)
-    keep_two = (jnp.sum(owned_mask.reshape(ROWS // 8, 8), 1) > 0).astype(I32)
-    keep = jnp.concatenate([keep_one, keep_two]).reshape(1, 12 * 128)
-    quarter_mask = lax.dynamic_slice_in_dim(
-        owned_mask.reshape(MP, QUARTER), lax.axis_index("mp"), 1, 0
-    ).reshape(QUARTER // BALL, 1, BALL)
-    x = swap(
-        owned.reshape(MP, QUARTER, LOCAL), shape((QUARTER, WIDTH), BF16), block, columns, 2
+    keep = jnp.concatenate([kept[:, :64].reshape(1, 4 * ONE), kept[:, 64:].reshape(1, 4 * TWO)], 1)
+    fed, all_pooled = fine(
+        landed.reshape(ROWS), got.reshape(SLOTS, LOCAL), owned_mask,
+        full_qkv, full_out, full_gate_up, full_down, 2,
     )
-    state, pooled = fine(x, quarter_mask, full_qkv, full_out)
-    all_pooled = swap(pooled, shape((MP,) + pooled.shape, BF16), whole, block, 3)
     one, two = project(all_pooled, w_coarse)
     mate_one, mate_two, mate_keep = exchange(one, two, keep, 4)
-    fed = forward(state, full_gate_up, full_down)
     mixed = coarse(one, two, mate_one, mate_two, keep, mate_keep)
     all_mixed = swap(mixed, shape((COARSE, WIDTH), BF16), block, columns, 5)
     returned = return_rows(got_code, fed, all_mixed, full_lift, 6)

time: 305 us -> 209 us (0.69)
  Pallas kernels: 294 us -> 196 us
  local copies, waits for them, and re-layouts: 6.57 us -> 9.7 us
    pallas_call x1, Pallas kernels: 94 us -> 55.2 us  [send_rows(): pl.pallas_call(send_kernel, out_shape=[shape((WIDE, CAP, LOCAL), BF16), s...]
    pallas_call x3 -> x1, Pallas kernels: 45.8 us -> 8.18 us  [swap(): pl.pallas_call(functools.partial(swap_kernel, pick, place), out_shape=out...]
    pallas_call x4 -> x3, Pallas kernels: 64.1 us -> 42.5 us  [the longest x1 36.3 us: fine(): pl.pallas_call(fine_kernel, out_shape=[shape((QUARTER, WIDTH), F32), shap...]
    unnamed x3 -> x9, local copies, waits for them, and re-layouts: 1.33 us -> 5.42 us
where the time goes in v3:
time: 209 us; the launch traced here: 206 us
  Pallas kernels  196 us (94%)
  local copies, waits for them, and re-layouts  9.7 us (5%)
    pallas_call x1, Pallas kernels, send_rows(): pl.pallas_call(send_kernel, out_shape=[shape((WIDE, CAP, LOCAL), BF16), s...  55.2 us
    pallas_call x1, Pallas kernels, return_rows(): pl.pallas_call(return_kernel, out_shape=shape((WIDE, CAP, LOCAL), BF16),...  49.9 us
    pallas_call x1, Pallas kernels, fine(): pl.pallas_call(fine_kernel, out_shape=[shape((QUARTER, WIDTH), F32), shap...  36.3 us
    pallas_call x1, Pallas kernels, exchange(): pl.pallas_call(exchange_kernel, out_shape=[shape((2, 4 * ONE, LOCAL), BF1...  14.8 us
    pallas_call x1, Pallas kernels, coarse(): pl.pallas_call(coarse_kernel, out_shape=shape((MP, COARSE, LOCAL), BF16),...  12.6 us
    pallas_call x1, Pallas kernels, swap(): pl.pallas_call(functools.partial(swap_kernel, pick, place), out_shape=out...  8.18 us
    pallas_call x1, Pallas kernels, on_device(): pl.pallas_call(finish_kernel, out_shape=shape((ROWS, LOCAL), F32), in_spe...  7.77 us
    unnamed x9, local copies, waits for them, and re-layouts  5.42 us

profile of v3, /device:TPU:1, one launch (start us, length us, event | category | flops | bytes accessed | tf_op | source)
XLA Modules:
  0.0 205.6 jit_solution(11550573787197842770)
XLA Ops:
  0.0 1.3 reshape.55.mask_ref
  1.3 1.3 reshape.54.perm_ref
  2.7 3.4 %shard_map.91 = (s32[16,256]{1,0:T(8,128)}, s32[32,256]{1,0:T(8,128)}, s32[32,256]{1,0:T(8,128)}) custom-call(s32[16,256]{1,0:T(8,128)} %reshape.54.perm_ref, s32[16,256]{1,0:T(8,128)} %reshape.55.mask_ref), custom_call_target="tpu_custom_call" | custom-call | tf_op jit(solution)/shard_map/pallas_call | solution.py:91
  6.0 1.3 copy.10
  7.4 1.4 copy.11
  8.7 1.4 reshape.58.codes_ref
  10.1 55.2 %shard_map.92 = (bf16[32,256,128]{2,1,0:T(8,128)(2,1)}, s32[32,2,128]{2,1,0:T(2,128)}, bf16[1536,512]{1,0:T(8,128)(2,1)}, bf16[4,128,512]{2,1,0:T(8,128)(2,1)}, ...) custom-call(s32[8192]{0:T(1024)} %bitcast.30, ...), custom_call_target="tpu_custom_call" | custom-call | tf_op jit(solution)/shard_map/pallas_call | solution.py:315
  65.4 1.4 copy.15
  66.7 2.8 %shard_map.93 = (s32[16,256]{1,0:T(8,128)}, s32[16,256]{1,0:T(8,128)}, s32[16,96]{1,0:T(8,128)}) custom-call(s32[32,256]{1,0:T(8,128)} %bitcast.31), custom_call_target="tpu_custom_call" | custom-call | tf_op jit(solution)/shard_map/pallas_call | solution.py:127
  69.5 1.3 copy.13
  70.9 0.0 copy-start.1
  70.9 36.3 %shard_map.94 = (f32[1024,512]{1,0:T(8,128)}, bf16[4,4,96,512]{3,2,1,0:T(8,128)(2,1)}) custom-call(s32[4096]{0:T(1024)} %bitcast.33, bf16[8192,128]{1,0:T(8,128)(2,1)} %bitcast.22, s32[16,256]{1,0:T(8,128)} %get-tuple-element.31.mask_ref, bf16[3,512,512]{2,1,0:T(8,128)(2,1)} %bitcast.23, bf16[512,512]{1,0:T(8,128)(2,1)} %bitcast.25, ...), custom_call_target="tpu_custom_call" | custom-call | tf_op jit(solution)/shard_map/pallas_call | solution.py:637
  107.2 0.0 copy-done.1
  107.2 0.1 reshape.69
  107.3 0.1 slice.7
  107.3 0.1 reshape.70
  107.4 0.0 copy-start
  107.4 5.0 %shard_map.95 = (bf16[3,1024,128]{2,1,0:T(8,128)(2,1)}, bf16[3,512,128]{2,1,0:T(8,128)(2,1)}) custom-call(bf16[4,4,96,512]{3,2,1,0:T(8,128)(2,1)} %get-tuple-element.37.rows_ref, bf16[2,3,512,128]{3,2,1,0:T(8,128)(2,1)} %w_ref.1), custom_call_target="tpu_custom_call" | custom-call | tf_op jit(solution)/shard_map/pallas_call | solution.py:685
  112.5 0.0 copy-done
  112.5 14.8 %shard_map.96 = (bf16[2,1024,128]{2,1,0:T(8,128)(2,1)}, bf16[3,2,512,128]{3,2,1,0:T(8,128)(2,1)}, s32[3,1,1536]{2,1,0:T(1,128)}) custom-call(bf16[3,1024,128]{2,1,0:T(8,128)(2,1)} %get-tuple-element.38.one, bf16[3,512,128]{2,1,0:T(8,128)(2,1)} %get-tuple-element.39.two, s32[1,1536]{1,0:T(1,128)} %copy-done), custom_call_target="tpu_custom_call" | custom-call | tf_op jit(solution)/shard_map/pallas_call | solution.py:732
  127.2 12.6 %shard_map.97.src = bf16[4,384,128]{2,1,0:T(8,128)(2,1)} custom-call(bf16[3,1024,128]{2,1,0:T(8,128)(2,1)} %get-tuple-element.38.one, bf16[3,512,128]{2,1,0:T(8,128)(2,1)} %get-tuple-element.39.two, bf16[2,1024,128]{2,1,0:T(8,128)(2,1)} %get-tuple-element.41.mate_one, bf16[3,2,512,128]{3,2,1,0:T(8,128)(2,1)} %get-tuple-element.42.mate_two, ...), custom_call_target="tpu_custom_call" | custom-call | tf_op jit(solution)/shard_map/pallas_call | solution.py:777
  139.8 8.2 %shard_map.98.mixed_ref = bf16[384,512]{1,0:T(8,128)(2,1)} custom-call(bf16[4,384,128]{2,1,0:T(8,128)(2,1)} %shard_map.97.src), custom_call_target="tpu_custom_call" | custom-call | tf_op jit(solution)/shard_map/pallas_call | solution.py:473
  148.0 49.9 %shard_map.99 = bf16[32,256,128]{2,1,0:T(8,128)(2,1)} custom-call(s32[8192]{0:T(1024)} %bitcast.29, f32[1024,512]{1,0:T(8,128)} %get-tuple-element.36.state_ref, bf16[384,512]{1,0:T(8,128)(2,1)} %shard_map.98.mixed_ref, bf16[4,256,512]{2,1,0:T(8,128)(2,1)} %get-tuple-element.44.w_ref), custom_call_target="tpu_custom_call" | custom-call | tf_op jit(solution)/shard_map/pallas_call | solution.py:434
  197.9 7.8 %shard_map.100 = f32[4096,128]{1,0:T(8,128)} custom-call(s32[4096]{0:T(1024)} %bitcast.32, bf16[8192,128]{1,0:T(8,128)(2,1)} %bitcast.20), custom_call_target="tpu_custom_call" | custom-call | tf_op jit(solution)/shard_map/pallas_call | solution.py:816
  (2 shorter events, 0.0 us)
Async XLA Ops:
  70.9 36.3 %copy-start.1 = (s32[16,96]{1,0:T(8,128)S(1)}, s32[16,96]{1,0:T(8,128)}, u32[]{:S(2)}) copy-start(s32[16,96]{1,0:T(8,128)} %get-tuple-element.40) | copy-start | bytes 18436
  107.4 5.0 %copy-start = (s32[1,1536]{1,0:T(1,128)}, s32[1,1536]{1,0:T(1,128)S(1)}, u32[]{:S(2)}) copy-start(s32[1,1536]{1,0:T(1,128)S(1)} %constant_dynamic-update-slice_fusion.keep) | copy-start | bytes 18436

commit v4 on v3

v4 whole, which is shorter than its diff:
```python
import functools

import jax
import jax.numpy as jnp
from jax import lax
from jax.experimental import pallas as pl
from jax.experimental.pallas import tpu as pltpu
from jax.sharding import PartitionSpec as P

BALL = 256
WIDE = 32
MP = 4
ROWS = 4096
CAP = 256
SLOTS = WIDE * CAP
QUARTER = ROWS // MP
WIDTH = 512
LOCAL = WIDTH // MP
HIDDEN = 2048
ONE = QUARTER // 4
TWO = QUARTER // 8
COARSE = ONE + TWO
F32 = jnp.float32
BF16 = jnp.bfloat16
I32 = jnp.int32
MESH = pl.DeviceIdType.MESH
ANY = pl.BlockSpec(memory_space=pl.ANY)
VMEM = pl.BlockSpec(memory_space=pltpu.VMEM)
SMEM = pl.BlockSpec(memory_space=pltpu.SMEM)
LIMIT = 56 * 1024 * 1024


def shape(dims, kind):
    return jax.ShapeDtypeStruct(dims, kind)


def params(collective=None):
    if collective is None:
        return pltpu.CompilerParams(vmem_limit_bytes=LIMIT)
    return pltpu.CompilerParams(
        vmem_limit_bytes=LIMIT, collective_id=collective, has_side_effects=True
    )


def dot(a, b):
    return jnp.dot(a, b, preferred_element_type=F32)


def dot_t(a, b):
    return lax.dot_general(a, b, (((1,), (1,)), ((), ())), preferred_element_type=F32)


def norm(values):
    return values * lax.rsqrt(jnp.mean(values * values, -1, keepdims=True) + 1e-06)


UNROLL = 16
NONE = 2 * ROWS


def index_kernel(perm_ref, mask_ref, slot_ref, source_ref, codes_ref):
    perm = perm_ref[...]
    target = perm >> 12
    code = (perm & (ROWS - 1)) * 2 + mask_ref[...]
    rows = lax.broadcasted_iota(I32, (CAP, 128), 0)
    upper = jnp.where(
        lax.broadcasted_iota(I32, (128, 128), 0) < lax.broadcasted_iota(I32, (128, 128), 1), 1.0, 0.0
    ).astype(BF16)
    which = lax.broadcasted_iota(I32, (WIDE, 128), 0)
    lane = lax.broadcasted_iota(I32, (1, 128), 1).astype(F32)
    carry = jnp.zeros((WIDE, 1), F32)
    found = jnp.zeros((5 * WIDE, CAP), F32)
    for c in range(ROWS // 128):
        row = slice(c, c + 1)
        hot = jnp.where(which == target[row, :], 1.0, 0.0)
        before = dot(hot.astype(BF16), upper) + carry
        rank = jnp.sum(hot * before, 0, keepdims=True).astype(I32)
        slot_ref[row, :] = target[row, :] * CAP + rank
        carry = carry + jnp.sum(hot, 1, keepdims=True)
        placed = jnp.where(rows == rank, 1.0, 0.0).astype(BF16)
        high = (code[row, :] >> 6).astype(F32)
        low = (code[row, :] & 63).astype(F32)
        values = jnp.concatenate([hot * lane, hot * float(c), hot * high, hot * low, hot], 0)
        found = found + dot_t(values.astype(BF16), placed)
    source = (found[:WIDE] + found[WIDE : 2 * WIDE] * 128.0).astype(I32)
    codes = (found[2 * WIDE : 3 * WIDE] * 64.0 + found[3 * WIDE : 4 * WIDE]).astype(I32)
    codes = jnp.where(found[4 * WIDE :] > 0.5, codes, NONE)
    for h in range(2):
        at = slice(h * 128, (h + 1) * 128)
        source_ref[:, h, :] = source[:, at]
        codes_ref[:, h, :] = codes[:, at]


def index(perm, mask):
    return pl.pallas_call(
        index_kernel,
        out_shape=[shape((32, 128), I32), shape((WIDE, 2, 128), I32), shape((WIDE, 2, 128), I32)],
        in_specs=[VMEM] * 2,
        out_specs=[VMEM] * 3,
        compiler_params=params(),
    )(perm.reshape(32, 128), mask.reshape(32, 128))


def run_matrix(r, c):
    hot = jnp.logical_or(
        jnp.logical_and(c < 64, r // 4 == c), jnp.logical_and(c >= 64, r // 8 == c - 64)
    )
    return jnp.where(hot, 1.0, 0.0).astype(BF16)


def inverse_kernel(codes_ref, slot_ref, mask_ref, keep_ref):
    balls = ROWS // BALL
    rows = lax.broadcasted_iota(I32, (256, 128), 0)
    which = lax.broadcasted_iota(I32, (balls, 128), 0)
    lane = lax.broadcasted_iota(I32, (1, 128), 1).astype(F32)
    found = jnp.zeros((3 * balls, 256), F32)
    for c in range(WIDE):
        for h in range(2):
            code = codes_ref[c, h : h + 1, :]
            landing = code >> 1
            hot = jnp.where(which == (landing >> 8), 1.0, 0.0)
            placed = jnp.where(rows == (landing & 255), 1.0, 0.0).astype(BF16)
            real = (code & 1).astype(F32)
            values = jnp.concatenate([hot * lane, hot * float(2 * c + h), hot * real], 0)
            found = found + dot_t(values.astype(BF16), placed)
    slots = (found[:balls] + found[balls : 2 * balls] * 128.0).astype(I32)
    for h in range(2):
        slot_ref[:, h, :] = slots[:, h * 128 : (h + 1) * 128]
    mask = found[2 * balls :]
    mask_ref[...] = mask.astype(I32)
    runs = run_matrix(
        lax.broadcasted_iota(I32, (256, 96), 0), lax.broadcasted_iota(I32, (256, 96), 1)
    )
    keep_ref[...] = jnp.where(dot(mask.astype(BF16), runs) > 0.5, 1, 0)


def inverse(codes):
    return pl.pallas_call(
        inverse_kernel,
        out_shape=[shape((16, 2, 128), I32), shape((16, 256), I32), shape((16, 96), I32)],
        in_specs=[VMEM],
        out_specs=[VMEM] * 3,
        compiler_params=params(),
    )(codes)


def widen(src, dst, rows):
    @pl.loop(0, rows // 256)
    def _(i):
        at = pl.ds(pl.multiple_of(i * 256, 256), 256)
        dst[at, :] = src[at, :].astype(dst.dtype)


def finish_kernel(slot_ref, got_ref, out_ref, wide):
    widen(got_ref, wide, SLOTS)

    @pl.loop(0, ROWS // UNROLL)
    def _(i):
        base = i * UNROLL
        lines = [wide[pl.ds(slot_ref[base + u], 1), :] for u in range(UNROLL)]
        for u in range(UNROLL):
            out_ref[pl.ds(base + u, 1), :] = lines[u]


def remote(src, dst, send, recv, device):
    return pltpu.make_async_remote_copy(
        src_ref=src, dst_ref=dst, send_sem=send, recv_sem=recv, device_id=device, device_id_type=MESH
    )


def gather_bucket(line, lookup, wide, staged, packed, peer):
    @pl.loop(0, CAP // UNROLL)
    def _(i):
        begin = i * UNROLL
        lines = [wide[pl.ds(lookup(peer * CAP + begin + u), 1), :] for u in range(UNROLL)]
        for u in range(UNROLL):
            staged[line, pl.ds(begin + u, 1), :] = lines[u]

    packed[peer] = staged[line].astype(BF16)


def send_kernel(
    source_ref, points_ref, codes_ref, qkv_ref, out_ref, gate_up_ref, down_ref, lift_ref,
    got_ref, got_codes_ref, all_qkv, all_out, all_gate_up, all_down, all_lift,
    wide, staged, packed, send, recv, own, w_send, w_recv, w_own,
):
    me = lax.axis_index("wide")
    mp = lax.axis_index("mp")
    core = lax.rem(me, 2)
    partner = me + 1 - 2 * core
    after, ahead = lax.rem(mp + 1, MP), lax.rem(mp + 2, MP)
    behind = lax.rem(mp + 3, MP)
    barrier = pltpu.get_barrier_semaphore()

    @pl.loop(1, WIDE)
    def _(k):
        pl.semaphore_signal(
            barrier, inc=1, device_id={"wide": lax.rem(me + k, WIDE)}, device_id_type=MESH
        )

    for other in (after, behind):
        pl.semaphore_signal(barrier, inc=1, device_id={"mp": other}, device_id_type=MESH)
    widen(points_ref, wide, ROWS)

    def part(first, count):
        def rows(ref, quarter):
            return pl.ds(pl.multiple_of(first * quarter, 16), count * quarter)

        def cut(j, ref, shard):
            if j == 0:
                return ref.at[rows(ref, 384), pl.ds(pl.multiple_of(shard * 128, 128), 128)]
            quarter = (0, 32, 256, 128, 64)[j]
            return ref.at[shard, rows(ref, quarter), :]

        def own_cut(j, ref):
            quarter = (384, 32, 256, 128, 64)[j]
            return ref.at[rows(ref, quarter), :]

        return cut, own_cut

    half, own_half = part(2 * core, 2)
    first, _ = part(2 * core, 1)
    second, _ = part(2 * core + 1, 1)
    every, own_every = part(0, 4)
    shards = [qkv_ref, out_ref, gate_up_ref, down_ref, lift_ref]
    full = [all_qkv, all_out, all_gate_up, all_down, all_lift]
    count = len(shards)

    def weight(j, kind, cut, src, shard, device):
        return remote(
            src, cut(j, full[j], shard), w_send.at[j, kind], w_recv.at[j, kind], device
        )

    def weight_copies(j):
        ref = full[j]
        mine = own_half(j, shards[j])
        return [
            weight(j, 0, half, mine, mp, {"mp": after}),
            weight(j, 1, half, mine, mp, {"mp": behind}),
            weight(j, 2, first, first(j, ref, behind), behind, {"mp": after}),
            weight(j, 3, second, second(j, ref, after), after, {"mp": behind}),
            weight(j, 4, half, half(j, ref, behind), behind, {"wide": partner}),
            weight(j, 5, half, half(j, ref, after), after, {"wide": partner}),
            weight(j, 6, first, first(j, ref, ahead), ahead, {"wide": partner}),
            weight(j, 7, second, second(j, ref, ahead), ahead, {"wide": partner}),
        ]

    weights = [weight_copies(j) for j in range(count)]

    def rows_copy(k):
        peer = lax.rem(me + k, WIDE)
        return remote(
            packed.at[peer], got_ref.at[me], send.at[k, 0], recv.at[k, 0], {"wide": peer}
        )

    def codes_copy(k):
        peer = lax.rem(me + k, WIDE)
        return remote(
            codes_ref.at[peer], got_codes_ref.at[me], send.at[k, 1], recv.at[k, 1], {"wide": peer}
        )

    pl.semaphore_wait(barrier, WIDE + 1)
    for j in range(count):
        weights[j][0].start()
        weights[j][1].start()

    @pl.loop(1, WIDE)
    def _(k):
        gather_bucket(0, lambda s: source_ref[s], wide, staged, packed, lax.rem(me + k, WIDE))
        rows_copy(k).start()
        codes_copy(k).start()

    gather_bucket(0, lambda s: source_ref[s], wide, staged, packed, me)
    mine = [
        pltpu.make_async_copy(packed.at[me], got_ref.at[me], own.at[0]),
        pltpu.make_async_copy(codes_ref.at[me], got_codes_ref.at[me], own.at[1]),
    ]
    for j in range(count):
        mine.append(
            pltpu.make_async_copy(own_every(j, shards[j]), every(j, full[j], mp), w_own.at[j])
        )
    for copy in mine:
        copy.start()
    for j in range(count):
        weights[j][0].wait_recv()
        weights[j][2].start()
        weights[j][4].start()
        weights[j][1].wait_recv()
        weights[j][3].start()
        weights[j][5].start()
    for j in range(count):
        weights[j][2].wait_recv()
        weights[j][6].start()
        weights[j][3].wait_recv()
        weights[j][7].start()
    for copy in mine:
        copy.wait()

    @pl.loop(1, WIDE)
    def _(k):
        rows_copy(k).wait()
        codes_copy(k).wait()

    for j in range(count):
        for kind in range(4):
            weights[j][kind].wait_send()
        for kind in range(4, 8):
            weights[j][kind].wait()


def send_rows(source, points, codes, weights, collective):
    return pl.pallas_call(
        send_kernel,
        out_shape=[
            shape((WIDE, CAP, LOCAL), BF16),
            shape((WIDE, 2, 128), I32),
            shape((3 * WIDTH, WIDTH), BF16),
            shape((MP, LOCAL, WIDTH), BF16),
            shape((MP, 2 * WIDTH, WIDTH), BF16),
            shape((MP, WIDTH, WIDTH), BF16),
            shape((MP, 2 * LOCAL, WIDTH), BF16),
        ],
        in_specs=[SMEM, VMEM, ANY] + [VMEM] * 5,
        out_specs=[ANY] * 7,
        scratch_shapes=[
            pltpu.VMEM((ROWS, LOCAL), F32),
            pltpu.VMEM((1, CAP, LOCAL), F32),
            pltpu.VMEM((WIDE, CAP, LOCAL), BF16),
            pltpu.SemaphoreType.DMA((WIDE, 2)),
            pltpu.SemaphoreType.DMA((WIDE, 2)),
            pltpu.SemaphoreType.DMA((2,)),
            pltpu.SemaphoreType.DMA((5, 8)),
            pltpu.SemaphoreType.DMA((5, 8)),
            pltpu.SemaphoreType.DMA((5,)),
        ],
        compiler_params=params(collective),
    )(source, points, codes, *weights)


def return_kernel(
    code_ref, turned_ref, lifted_ref, got_ref, wide, staged, packed, send, recv, own
):
    me = lax.axis_index("wide")
    barrier = pltpu.get_barrier_semaphore()

    @pl.loop(1, WIDE)
    def _(k):
        pl.semaphore_signal(
            barrier, inc=1, device_id={"wide": lax.rem(me + k, WIDE)}, device_id_type=MESH
        )

    runs = run_matrix(
        lax.broadcasted_iota(I32, (BALL, 96), 0), lax.broadcasted_iota(I32, (BALL, 96), 1)
    )

    @pl.loop(0, ROWS // BALL)
    def _(i):
        at = pl.ds(pl.multiple_of(i * BALL, BALL), BALL)
        wide[at, :] = turned_ref[at, :].astype(F32) + dot(runs, lifted_ref[i])

    wide[ROWS : ROWS + 8, :] = jnp.zeros((8, LOCAL), F32)
    pl.semaphore_wait(barrier, WIDE - 1)

    def rows_copy(k):
        peer = lax.rem(me + k, WIDE)
        return remote(packed.at[peer], got_ref.at[me], send.at[k], recv.at[k], {"wide": peer})

    @pl.loop(1, WIDE)
    def _(k):
        gather_bucket(0, lambda s: code_ref[s] >> 1, wide, staged, packed, lax.rem(me + k, WIDE))
        rows_copy(k).start()

    gather_bucket(0, lambda s: code_ref[s] >> 1, wide, staged, packed, me)
    last = pltpu.make_async_copy(packed.at[me], got_ref.at[me], own)
    last.start()
    last.wait()

    @pl.loop(1, WIDE)
    def _(k):
        rows_copy(k).wait()


def return_rows(codes, turned, lifted, collective):
    return pl.pallas_call(
        return_kernel,
        out_shape=shape((WIDE, CAP, LOCAL), BF16),
        in_specs=[SMEM, VMEM, VMEM],
        out_specs=ANY,
        scratch_shapes=[
            pltpu.VMEM((ROWS + 8, LOCAL), F32),
            pltpu.VMEM((1, CAP, LOCAL), F32),
            pltpu.VMEM((WIDE, CAP, LOCAL), BF16),
            pltpu.SemaphoreType.DMA((WIDE,)),
            pltpu.SemaphoreType.DMA((WIDE,)),
            pltpu.SemaphoreType.DMA,
        ],
        compiler_params=params(collective),
    )(codes, turned, lifted)


def attend_pair(queries, parts, low):
    mixed = []
    for head in range(2):
        mine = low if head == 0 else jnp.logical_not(low)
        q = jnp.where(mine, queries, jnp.zeros_like(queries))
        scores = [jnp.where(allowed, dot_t(q, keys), -1e30) for keys, _, allowed in parts]
        top = functools.reduce(jnp.maximum, [jnp.max(s, -1, keepdims=True) for s in scores])
        expo = [jnp.exp(s - top) for s in scores]
        total = sum(jnp.sum(e, -1, keepdims=True) for e in expo)
        out = sum(dot(e.astype(BF16), values) for e, (_, values, _) in zip(expo, parts))
        mixed.append(out / total)
    return jnp.where(low, mixed[0], mixed[1])


def fine_ball(x, real, qkv_ref, out_ref):
    x = x.astype(F32)
    normed = norm(x).astype(BF16)
    q = (dot(normed, qkv_ref[0]) * 0.125).astype(BF16)
    k = dot(normed, qkv_ref[1]).astype(BF16)
    v = dot(normed, qkv_ref[2]).astype(BF16)
    rows = lax.broadcasted_iota(I32, (BALL, BALL), 0)
    cols = lax.broadcasted_iota(I32, (BALL, BALL), 1)
    allowed = jnp.logical_or(real, rows == cols)
    low = lax.broadcasted_iota(I32, (BALL, 128), 1) < 64
    mixed = []
    for g in range(MP):
        at = slice(g * 128, (g + 1) * 128)
        mixed.append(attend_pair(q[:, at], [(k[:, at], v[:, at], allowed)], low).astype(BF16))
    state = x + dot(jnp.concatenate(mixed, 1), out_ref[...])
    high = state.astype(BF16)
    rest = (state - high.astype(F32)).astype(BF16)
    runs, counted = pooling(real, 4)
    pooled = (dot(runs, high) + dot(runs, rest)) / jnp.maximum(counted, 1.0)
    return state, pooled.astype(BF16)


def pooling(real, factor):
    count_rows = BALL // factor
    r = lax.broadcasted_iota(I32, (count_rows, BALL), 0)
    c = lax.broadcasted_iota(I32, (count_rows, BALL), 1)
    hot = jnp.where(jnp.logical_and(r == c // factor, real), 1.0, 0.0)
    return hot.astype(BF16), jnp.sum(hot, 1, keepdims=True)


BALLS = QUARTER // BALL


def forward_tile(state, gate_up_ref, down_ref):
    normed = norm(state).astype(BF16)
    total = state
    for c in range(MP):
        gate = dot(normed, gate_up_ref[c, 0])
        up = dot(normed, gate_up_ref[c, 1])
        activated = (gate / (1.0 + jnp.exp(-gate)) * up).astype(BF16)
        total = total + dot(activated, down_ref[c])
    return total


def relatives(me):
    low = lax.rem(me, 2)
    high = lax.rem(me // 2, 2)
    first = me + 1 - 2 * low
    second = me + 2 - 4 * high
    third = first + 2 - 4 * high
    return (first, second, third)


def middle_kernel(
    slot_ref, got_ref, mask_ref, keep_ref, qkv_hbm, out_hbm, gate_up_hbm, down_hbm, coarse_hbm,
    lift_hbm, turned_ref, lifted_ref,
    wide, staged, packed, x, state, pooled, tiles, one, two, mate_one, mate_two, mate_keep,
    mixed, all_mixed, lifted, qkv_ref, out_ref, gate_up_ref, down_ref, w_ref, lift_ref,
    x_sem, p_sem, e_sem, k_sem, m_sem, t_sem, l_sem, own, loads,
):
    me = lax.axis_index("wide")
    mp = lax.axis_index("mp")
    others = relatives(me)
    barrier = pltpu.get_barrier_semaphore()
    for k in range(1, MP):
        pl.semaphore_signal(
            barrier, inc=1, device_id={"mp": lax.rem(mp + k, MP)}, device_id_type=MESH
        )
    for other in others:
        pl.semaphore_signal(barrier, inc=1, device_id={"wide": other}, device_id_type=MESH)
    load = [
        pltpu.make_async_copy(src, dst, loads.at[j])
        for j, (src, dst) in enumerate([
            (qkv_hbm, qkv_ref),
            (out_hbm, out_ref),
            (gate_up_hbm, gate_up_ref),
            (down_hbm, down_ref),
            (coarse_hbm, w_ref),
            (lift_hbm, lift_ref),
        ])
    ]
    for copy in load:
        copy.start()
    widen(got_ref, wide, SLOTS)
    pl.semaphore_wait(barrier, MP + 2)

    def rows(t, size):
        return pl.ds(pl.multiple_of(t * size, size), size)

    def cols(g):
        return pl.ds(pl.multiple_of(g * LOCAL, LOCAL), LOCAL)

    def peer(k):
        return lax.rem(mp + k, MP)

    def to_mp(src, dst, sem, k, t):
        return remote(src, dst, sem.at[0, k, t], sem.at[1, k, t], {"mp": peer(k)})

    def turn(k, t):
        return to_mp(packed.at[peer(k) * BALLS + t], x.at[rows(t, BALL), cols(mp)], x_sem, k, t)

    def keep_turn(t):
        return pltpu.make_async_copy(
            packed.at[mp * BALLS + t], x.at[rows(t, BALL), cols(mp)], own.at[0, t]
        )

    @pl.loop(0, BALLS)
    def _(t):
        for k in (2, 1, 3):
            gather_bucket(0, lambda s: slot_ref[s], wide, staged, packed, peer(k) * BALLS + t)
            turn(k, t).start()
        gather_bucket(0, lambda s: slot_ref[s], wide, staged, packed, mp * BALLS + t)
        keep_turn(t).start()

    def flags(j):
        return remote(
            keep_ref, mate_keep.at[j], k_sem.at[0, j], k_sem.at[1, j], {"wide": others[j]}
        )

    for j in range(3):
        flags(j).start()
    load[0].wait()
    load[1].wait()

    def share(k, t):
        return to_mp(pooled.at[mp, t], pooled.at[mp, t], p_sem, k, t)

    @pl.loop(0, BALLS)
    def _(t):
        for k in (1, 3, 2):
            turn(k, t).wait_recv()
        keep_turn(t).wait()
        real = mask_ref[pl.ds(mp * BALLS + t, 1), :] > 0
        out, means = fine_ball(x[rows(t, BALL), :], real, qkv_ref, out_ref)
        state[rows(t, BALL), :] = out
        pooled[mp, t] = means
        for k in (2, 1, 3):
            share(k, t).start()

    load[2].wait()
    load[3].wait()

    def give(k, t):
        return to_mp(
            tiles.at[rows(t, BALL), cols(peer(k))],
            turned_ref.at[rows(mp * BALLS + t, BALL), :],
            t_sem,
            k,
            t,
        )

    def keep_give(t):
        return pltpu.make_async_copy(
            tiles.at[rows(t, BALL), cols(mp)],
            turned_ref.at[rows(mp * BALLS + t, BALL), :],
            own.at[1, t],
        )

    def feed(t):
        fed = forward_tile(state[rows(t, BALL), :], gate_up_ref, down_ref)
        tiles[rows(t, BALL), :] = fed.astype(BF16)
        for k in (2, 1, 3):
            give(k, t).start()
        keep_give(t).start()

    @pl.loop(0, FIRST)
    def _(t):
        feed(t)

    def pass_one(q):
        return remote(
            one.at[pl.ds(1, 2), rows(q, ONE), :],
            mate_one.at[:, rows(q, ONE), :],
            e_sem.at[0, 3, q],
            e_sem.at[1, 3, q],
            {"wide": others[0]},
        )

    def pass_two(j, q):
        return remote(
            two.at[pl.ds(1, 2), rows(q, TWO), :],
            mate_two.at[j, :, rows(q, TWO), :],
            e_sem.at[0, j, q],
            e_sem.at[1, j, q],
            {"wide": others[j]},
        )

    pair = lax.broadcasted_iota(I32, (32, 64), 0) == lax.broadcasted_iota(I32, (32, 64), 1) // 2
    pair = jnp.where(pair, 1.0, 0.0).astype(BF16)
    load[4].wait()

    def project(q):
        firsts, seconds = [], []
        for ball in range(BALLS):
            real = mask_ref[pl.ds(q * BALLS + ball, 1), :] > 0
            means = pooled[q, ball].astype(F32)
            firsts.append(norm(means).astype(BF16))
            sums = means * pooling(real, 4)[1]
            high = sums.astype(BF16)
            rest = (sums - high.astype(F32)).astype(BF16)
            counted = jnp.maximum(pooling(real, 8)[1], 1.0)
            seconds.append(norm((dot(pair, high) + dot(pair, rest)) / counted).astype(BF16))
        firsts = jnp.concatenate(firsts, 0)
        seconds = jnp.concatenate(seconds, 0)
        for t in (1, 2):
            two[t, rows(q, TWO), :] = dot(seconds, w_ref[1, t]).astype(BF16)
            one[t, rows(q, ONE), :] = dot(firsts, w_ref[0, t]).astype(BF16)
        for j in (1, 2, 0):
            pass_two(j, q).start()
        pass_one(q).start()
        two[0, rows(q, TWO), :] = (dot(seconds, w_ref[1, 0]) * 0.125).astype(BF16)
        one[0, rows(q, ONE), :] = (dot(firsts, w_ref[0, 0]) * 0.125).astype(BF16)

    project(mp)
    for k in (1, 3, 2):

        @pl.loop(0, BALLS)
        def _(t):
            share(MP - k, t).wait_recv()

        project(peer(k))

    @pl.loop(FIRST, SECOND)
    def _(t):
        feed(t)

    def hand(k, level):
        at = pl.ds(0, ONE) if level == 0 else pl.ds(ONE, TWO)
        return to_mp(mixed.at[peer(k), at, :], all_mixed.at[at, cols(mp)], m_sem, k, level)

    def keep_hand(level):
        at = pl.ds(0, ONE) if level == 0 else pl.ds(ONE, TWO)
        return pltpu.make_async_copy(
            mixed.at[mp, at, :], all_mixed.at[at, cols(mp)], own.at[2, level]
        )

    def own_keys(begin, real, count, length):
        r = lax.broadcasted_iota(I32, (count, length), 0) + begin
        c = lax.broadcasted_iota(I32, (count, length), 1)
        return jnp.logical_or(real, r == c)

    for j in range(3):
        flags(j).wait()

    @pl.loop(0, MP)
    def _(q):
        pass_one(q).wait()

    @pl.loop(1, MP + 1)
    def _(k):
        q = peer(k)
        low = lax.broadcasted_iota(I32, (ONE, 128), 1) < 64
        real = keep_ref[:, : 4 * ONE] > 0
        mate = mate_keep[0][:, : 4 * ONE] > 0
        parts = [
            (one[1], one[2], own_keys(q * ONE, real, ONE, 4 * ONE)),
            (mate_one[0], mate_one[1], mate),
        ]
        mixed[q, 0:ONE, :] = attend_pair(one[0, rows(q, ONE), :], parts, low).astype(BF16)

        @pl.when(k < MP)
        def _():
            hand(k, 0).start()

    keep_hand(0).start()

    @pl.loop(0, MP)
    def _(q):
        for j in range(3):
            pass_two(j, q).wait()

    @pl.loop(1, MP + 1)
    def _(k):
        q = peer(k)
        low = lax.broadcasted_iota(I32, (TWO, 128), 1) < 64
        real = keep_ref[:, 4 * ONE :] > 0
        parts = [(two[1], two[2], own_keys(q * TWO, real, TWO, 4 * TWO))]
        for j in range(3):
            parts.append((mate_two[j, 0], mate_two[j, 1], mate_keep[j][:, 4 * ONE :] > 0))
        mixed[q, ONE:COARSE, :] = attend_pair(two[0, rows(q, TWO), :], parts, low).astype(BF16)

        @pl.when(k < MP)
        def _():
            hand(k, 1).start()

    keep_hand(1).start()

    @pl.loop(SECOND, BALLS)
    def _(t):
        feed(t)

    load[5].wait()
    for level in range(2):
        keep_hand(level).wait()
        for k in (1, 3, 2):
            hand(k, level).wait()
    for level, begin, size in ((0, 0, 64), (1, ONE, 32)):
        span = slice(begin, begin + size * BALLS)
        total = jnp.zeros((size * BALLS, WIDTH), F32)
        for g in range(MP):
            total = total + dot(
                all_mixed[span, g * LOCAL : (g + 1) * LOCAL],
                lift_ref[g, level * LOCAL : (level + 1) * LOCAL, :],
            )
        total = total.astype(BF16)
        for ball in range(BALLS):
            at = slice(0, 64) if level == 0 else slice(64, 96)
            lifted[ball, at, :] = total[ball * size : (ball + 1) * size]

    def rise(k):
        return to_mp(lifted.at[:, :, cols(peer(k))], lifted_ref.at[mp], l_sem, k, 0)

    for k in (2, 1, 3):
        rise(k).start()
    keep_rise = pltpu.make_async_copy(lifted.at[:, :, cols(mp)], lifted_ref.at[mp], own.at[3, 0])
    keep_rise.start()

    @pl.loop(0, BALLS)
    def _(t):
        keep_give(t).wait()
        for k in (1, 3, 2):
            turn(k, t).wait_send()
            share(k, t).wait_send()
            give(k, t).wait()

    keep_rise.wait()
    for k in (1, 3, 2):
        rise(k).wait()


FIRST = 2
SECOND = 3


def middle(slots, got, mask, keep, weights, collective):
    dma = pltpu.SemaphoreType.DMA
    return pl.pallas_call(
        middle_kernel,
        out_shape=[shape((ROWS, LOCAL), BF16), shape((MP, BALLS, 96, LOCAL), BF16)],
        in_specs=[SMEM, VMEM, VMEM, VMEM] + [ANY] * 6,
        out_specs=[ANY, ANY],
        scratch_shapes=[
            pltpu.VMEM((SLOTS, LOCAL), F32),
            pltpu.VMEM((1, CAP, LOCAL), F32),
            pltpu.VMEM((MP * BALLS, BALL, LOCAL), BF16),
            pltpu.VMEM((QUARTER, WIDTH), BF16),
            pltpu.VMEM((QUARTER, WIDTH), F32),
            pltpu.VMEM((MP, BALLS, 64, WIDTH), BF16),
            pltpu.VMEM((QUARTER, WIDTH), BF16),
            pltpu.VMEM((3, 4 * ONE, LOCAL), BF16),
            pltpu.VMEM((3, 4 * TWO, LOCAL), BF16),
            pltpu.VMEM((2, 4 * ONE, LOCAL), BF16),
            pltpu.VMEM((3, 2, 4 * TWO, LOCAL), BF16),
            pltpu.VMEM((3, 1, 12 * 128), I32),
            pltpu.VMEM((MP, COARSE, LOCAL), BF16),
            pltpu.VMEM((COARSE, WIDTH), BF16),
            pltpu.VMEM((BALLS, 96, WIDTH), BF16),
            pltpu.VMEM((3, WIDTH, WIDTH), BF16),
            pltpu.VMEM((WIDTH, WIDTH), BF16),
            pltpu.VMEM((MP, 2, WIDTH, WIDTH), BF16),
            pltpu.VMEM((MP, WIDTH, WIDTH), BF16),
            pltpu.VMEM((2, 3, WIDTH, LOCAL), BF16),
            pltpu.VMEM((MP, 2 * LOCAL, WIDTH), BF16),
            dma((2, MP, BALLS)),
            dma((2, MP, BALLS)),
            dma((2, 4, MP)),
            dma((2, 3)),
            dma((2, MP, 2)),
            dma((2, MP, BALLS)),
            dma((2, MP, 1)),
            dma((4, BALLS)),
            dma((6,)),
        ],
        compiler_params=params(collective),
    )(slots, got, mask, keep, *weights)


def on_device(points, mask, perm, w_qkv, w_out, w_gate_up, w_down, w_coarse, w_coarse_out):
    slot, source, codes = index(perm, mask)
    got, got_code, full_qkv, full_out, full_gate_up, full_down, full_lift = send_rows(
        source.reshape(SLOTS),
        points,
        codes,
        [
            w_qkv.reshape(3 * WIDTH, LOCAL),
            w_out,
            w_gate_up.reshape(2 * WIDTH, WIDTH),
            w_down,
            w_coarse_out.reshape(2 * LOCAL, WIDTH),
        ],
        1,
    )
    full_qkv = full_qkv.reshape(3, WIDTH, WIDTH)
    full_out = full_out.reshape(WIDTH, WIDTH)
    full_gate_up = full_gate_up.reshape(MP, 2, WIDTH, WIDTH)
    landed, owned_mask, kept = inverse(got_code)
    keep = jnp.concatenate([kept[:, :64].reshape(1, 4 * ONE), kept[:, 64:].reshape(1, 4 * TWO)], 1)
    turned, lifted = middle(
        landed.reshape(ROWS), got.reshape(SLOTS, LOCAL), owned_mask, keep,
        [full_qkv, full_out, full_gate_up, full_down, w_coarse, full_lift], 2,
    )
    lifted = lifted.reshape(MP * BALLS, 96, LOCAL)
    returned = return_rows(got_code.reshape(SLOTS), turned, lifted, 3)
    return pl.pallas_call(
        finish_kernel,
        out_shape=shape((ROWS, LOCAL), F32),
        in_specs=[SMEM, VMEM],
        out_specs=VMEM,
        scratch_shapes=[pltpu.VMEM((SLOTS, LOCAL), F32)],
        compiler_params=params(),
    )(slot.reshape(ROWS), returned.reshape(SLOTS, LOCAL))


def solution(mesh):
    placed = (
        P("wide", "mp"),
        P("wide"),
        P("wide"),
        P(None, None, "mp"),
        P("mp", None),
        P(None, None, "mp"),
        P("mp", None),
        P(None, None, None, "mp"),
        P(None, "mp", None),
    )
    return jax.shard_map(
        on_device, mesh=mesh, in_specs=placed, out_specs=P("wide", "mp"), check_vma=False
    )
```

time: 209 us -> 171 us (0.82)
  Pallas kernels: 196 us -> 165 us
  local copies, waits for them, and re-layouts: 9.7 us -> 1.62 us
    pallas_call x7 -> x3, Pallas kernels: 83 us -> 66.5 us  [the longest x1 59.3 us: middle(): pl.pallas_call(middle_kernel, out_shape=[shape((ROWS, LOCAL), BF16), shap...]
    pallas_call x1, Pallas kernels: 49.9 us -> 35.9 us  [return_rows(): pl.pallas_call(return_kernel, out_shape=shape((WIDE, CAP, LOCAL), BF16),...]
    unnamed x9 -> x0, local copies, waits for them, and re-layouts: 5.42 us -> none
    reshape x3 -> x0, local copies, waits for them, and re-layouts: 4.04 us -> none  [the longest x1 1.39 us: on_device(): codes.reshape(WIDE, 2, 128)]
where the time goes in v4:
time: 171 us; the launch traced here: 168 us
  Pallas kernels  165 us (96%)
    pallas_call x1, Pallas kernels, middle(): pl.pallas_call(middle_kernel, out_shape=[shape((ROWS, LOCAL), BF16), shap...  59.3 us
    pallas_call x1, Pallas kernels, send_rows(): pl.pallas_call(send_kernel, out_shape=[shape((WIDE, CAP, LOCAL), BF16), s...  55.2 us
    pallas_call x1, Pallas kernels, return_rows(): pl.pallas_call(return_kernel, out_shape=shape((WIDE, CAP, LOCAL), BF16),...  35.9 us
    pallas_call x1, Pallas kernels, on_device(): pl.pallas_call(finish_kernel, out_shape=shape((ROWS, LOCAL), F32), in_spe...  7.77 us
    pallas_call x1, Pallas kernels, index(): pl.pallas_call(index_kernel, out_shape=[shape((32, 128), I32), shape((WID...  4.16 us

profile of v4, /device:TPU:1, one launch (start us, length us, event | category | flops | bytes accessed | tf_op | source)
XLA Modules:
  0.0 167.6 jit_solution(17796753337517650093)
XLA Ops:
  0.0 4.2 %shard_map.91 = (s32[32,128]{1,0:T(8,128)}, s32[32,2,128]{2,1,0:T(2,128)}, s32[32,2,128]{2,1,0:T(2,128)}) custom-call(s32[32,128]{1,0:T(8,128)} %bitcast.30, s32[32,128]{1,0:T(8,128)} %bitcast.31), custom_call_target="tpu_custom_call" | custom-call | tf_op jit(solution)/shard_map/pallas_call | solution.py:95
  4.2 55.2 %shard_map.92 = (bf16[32,256,128]{2,1,0:T(8,128)(2,1)}, s32[32,2,128]{2,1,0:T(2,128)}, bf16[1536,512]{1,0:T(8,128)(2,1)}, bf16[4,128,512]{2,1,0:T(8,128)(2,1)}, ...) custom-call(s32[8192]{0:T(1024)} %bitcast.26, ...), custom_call_target="tpu_custom_call" | custom-call | tf_op jit(solution)/shard_map/pallas_call | solution.py:312
  59.4 3.0 %shard_map.93 = (s32[16,2,128]{2,1,0:T(2,128)}, s32[16,256]{1,0:T(8,128)}, s32[16,96]{1,0:T(8,128)}) custom-call(s32[32,2,128]{2,1,0:T(2,128)} %get-tuple-element.23.codes_ref), custom_call_target="tpu_custom_call" | custom-call | tf_op jit(solution)/shard_map/pallas_call | solution.py:138
  62.4 0.8 reshape.61
  63.2 0.8 slice.7
  64.0 0.1 reshape.62
  64.0 0.6 pad_add_fusion.keep_ref
  64.6 59.3 %shard_map.94 = (bf16[4096,128]{1,0:T(8,128)(2,1)}, bf16[4,4,96,128]{3,2,1,0:T(8,128)(2,1)}) custom-call(s32[4096]{0:T(1024)} %bitcast.29, bf16[8192,128]{1,0:T(8,128)(2,1)} %bitcast.18, s32[16,256]{1,0:T(8,128)} %get-tuple-element.26.mask_ref, s32[1,1536]{1,0:T(1,128)} %pad_add_fusion.keep_ref, bf16[3,512,512]{2,1,0:T(8,128)(2,1)} %bitcast.19, ...), custom_call_target="tpu_custom_call" | custom-call | tf_op jit(solution)/shard_map/pallas_call | solution.py:751
  123.9 35.9 %shard_map.95 = bf16[32,256,128]{2,1,0:T(8,128)(2,1)} custom-call(s32[8192]{0:T(1024)} %bitcast.25, bf16[4096,128]{1,0:T(8,128)(2,1)} %get-tuple-element.33.turned_ref, bf16[16,96,128]{2,1,0:T(8,128)(2,1)} %bitcast.22), custom_call_target="tpu_custom_call" | custom-call | tf_op jit(solution)/shard_map/pallas_call | solution.py:384
  159.8 7.8 %shard_map.96 = f32[4096,128]{1,0:T(8,128)} custom-call(s32[4096]{0:T(1024)} %bitcast.28, bf16[8192,128]{1,0:T(8,128)(2,1)} %bitcast.16), custom_call_target="tpu_custom_call" | custom-call | tf_op jit(solution)/shard_map/pallas_call | solution.py:818

commit v5 on v4

--- a/solution.py
+++ b/solution.py
@@ -54,7 +54,7 @@
     return values * lax.rsqrt(jnp.mean(values * values, -1, keepdims=True) + 1e-06)
 
 
-UNROLL = 16
+UNROLL = 32
 NONE = 2 * ROWS
 
 
@@ -168,6 +168,10 @@
     )
 
 
+def turn_of(me, k):
+    return lax.rem(me + lax.rem(k * 7, WIDE), WIDE)
+
+
 def gather_bucket(line, lookup, wide, staged, packed, peer):
     @pl.loop(0, CAP // UNROLL)
     def _(i):
@@ -248,13 +252,13 @@
     weights = [weight_copies(j) for j in range(count)]
 
     def rows_copy(k):
-        peer = lax.rem(me + k, WIDE)
+        peer = turn_of(me, k)
         return remote(
             packed.at[peer], got_ref.at[me], send.at[k, 0], recv.at[k, 0], {"wide": peer}
         )
 
     def codes_copy(k):
-        peer = lax.rem(me + k, WIDE)
+        peer = turn_of(me, k)
         return remote(
             codes_ref.at[peer], got_codes_ref.at[me], send.at[k, 1], recv.at[k, 1], {"wide": peer}
         )
@@ -266,7 +270,7 @@
 
     @pl.loop(1, WIDE)
     def _(k):
-        gather_bucket(0, lambda s: source_ref[s], wide, staged, packed, lax.rem(me + k, WIDE))
+        gather_bucket(0, lambda s: source_ref[s], wide, staged, packed, turn_of(me, k))
         rows_copy(k).start()
         codes_copy(k).start()
 
@@ -362,12 +366,12 @@
     pl.semaphore_wait(barrier, WIDE - 1)
 
     def rows_copy(k):
-        peer = lax.rem(me + k, WIDE)
+        peer = turn_of(me, k)
         return remote(packed.at[peer], got_ref.at[me], send.at[k], recv.at[k], {"wide": peer})
 
     @pl.loop(1, WIDE)
     def _(k):
-        gather_bucket(0, lambda s: code_ref[s] >> 1, wide, staged, packed, lax.rem(me + k, WIDE))
+        gather_bucket(0, lambda s: code_ref[s] >> 1, wide, staged, packed, turn_of(me, k))
         rows_copy(k).start()
 
     gather_bucket(0, lambda s: code_ref[s] >> 1, wide, staged, packed, me)
@@ -398,34 +402,77 @@
     )(codes, turned, lifted)
 
 
-def attend_pair(queries, parts, low):
-    mixed = []
+SCALE = 0.125 * 1.4426950408889634
+
+
+def lanes(count):
+    return lax.broadcasted_iota(I32, (count, 128), 1)
+
+
+def columns_of(flags):
+    size = 256
+    eye = lax.broadcasted_iota(I32, (size, size), 0) == lax.broadcasted_iota(I32, (size, size), 1)
+    eye = jnp.where(eye, 1.0, 0.0).astype(BF16)
+    out = []
+    for begin in range(0, flags.shape[1], size):
+        row = jnp.where(flags[:, begin : begin + size], 1.0, 0.0)
+        out.append(dot_t(eye, jnp.broadcast_to(row, (128, size)).astype(BF16)))
+    return jnp.concatenate(out, 0)
+
+
+def augment(keys, values, columns):
+    lane = lanes(keys.shape[0])
+    low = lane < 64
+    bias = jnp.where(columns > 0.5, 0.0, -1e30)
+    keys = keys.astype(F32)
+    values = values.astype(F32)
+    return (
+        (
+            jnp.where(low, keys, jnp.where(lane == 64, bias, 0.0)).astype(BF16),
+            jnp.where(low, jnp.where(lane == 0, bias, 0.0), keys).astype(BF16),
+        ),
+        (jnp.where(low, values, 1.0).astype(BF16), jnp.where(low, 1.0, values).astype(BF16)),
+    )
+
+
+def attend_pair(queries, own_keys, own_values, masked, keys, values):
+    count = queries.shape[0]
+    lane = lanes(count)
+    low = lane < 64
+    queries = queries.astype(F32)
+    own_keys = own_keys.astype(F32)
+    own_values = own_values.astype(F32)
+    out = []
     for head in range(2):
         mine = low if head == 0 else jnp.logical_not(low)
-        q = jnp.where(mine, queries, jnp.zeros_like(queries))
-        scores = [jnp.where(allowed, dot_t(q, keys), -1e30) for keys, _, allowed in parts]
-        top = functools.reduce(jnp.maximum, [jnp.max(s, -1, keepdims=True) for s in scores])
-        expo = [jnp.exp(s - top) for s in scores]
-        total = sum(jnp.sum(e, -1, keepdims=True) for e in expo)
-        out = sum(dot(e.astype(BF16), values) for e, (_, values, _) in zip(expo, parts))
-        mixed.append(out / total)
-    return jnp.where(low, mixed[0], mixed[1])
+        spare = jnp.where(lane == (64 if head == 0 else 0), 1.0, 0.0)
+        q = jnp.where(mine, queries, spare).astype(BF16)
+        scores = dot_t(q, keys(head))
+        alone = jnp.sum(jnp.where(mine, queries * own_keys, 0.0), -1, keepdims=True)
+        top = jnp.maximum(jnp.max(scores, -1, keepdims=True), alone)
+        weights = jnp.exp2(scores - top).astype(BF16)
+        own = jnp.where(masked, jnp.exp2(alone - top), 0.0)
+        total = dot(weights, values(head))
+        out.append(total + own * jnp.where(mine, own_values, 1.0))
+    sums = pltpu.roll(jnp.where(low, out[1], out[0]), 64, 1)
+    return (jnp.where(low, out[0], out[1]) / sums).astype(BF16)
 
 
 def fine_ball(x, real, qkv_ref, out_ref):
     x = x.astype(F32)
     normed = norm(x).astype(BF16)
-    q = (dot(normed, qkv_ref[0]) * 0.125).astype(BF16)
+    q = (dot(normed, qkv_ref[0]) * SCALE).astype(BF16)
     k = dot(normed, qkv_ref[1]).astype(BF16)
     v = dot(normed, qkv_ref[2]).astype(BF16)
-    rows = lax.broadcasted_iota(I32, (BALL, BALL), 0)
-    cols = lax.broadcasted_iota(I32, (BALL, BALL), 1)
-    allowed = jnp.logical_or(real, rows == cols)
-    low = lax.broadcasted_iota(I32, (BALL, 128), 1) < 64
+    columns = columns_of(real)
+    masked = columns[:, :1] < 0.5
     mixed = []
     for g in range(MP):
         at = slice(g * 128, (g + 1) * 128)
-        mixed.append(attend_pair(q[:, at], [(k[:, at], v[:, at], allowed)], low).astype(BF16))
+        keys, values = augment(k[:, at], v[:, at], columns)
+        mixed.append(
+            attend_pair(q[:, at], k[:, at], v[:, at], masked, keys.__getitem__, values.__getitem__)
+        )
     state = x + dot(jnp.concatenate(mixed, 1), out_ref[...])
     high = state.astype(BF16)
     rest = (state - high.astype(F32)).astype(BF16)
@@ -451,7 +498,8 @@
     for c in range(MP):
         gate = dot(normed, gate_up_ref[c, 0])
         up = dot(normed, gate_up_ref[c, 1])
-        activated = (gate / (1.0 + jnp.exp(-gate)) * up).astype(BF16)
+        half = gate * 0.5
+        activated = ((half + half * jnp.tanh(half)) * up).astype(BF16)
         total = total + dot(activated, down_ref[c])
     return total
 
@@ -469,7 +517,7 @@
     slot_ref, got_ref, mask_ref, keep_ref, qkv_hbm, out_hbm, gate_up_hbm, down_hbm, coarse_hbm,
     lift_hbm, turned_ref, lifted_ref,
     wide, staged, packed, x, state, pooled, tiles, one, two, mate_one, mate_two, mate_keep,
-    mixed, all_mixed, lifted, qkv_ref, out_ref, gate_up_ref, down_ref, w_ref, lift_ref,
+    mixed, all_mixed, lifted, keys_one, values_one, keys_two, values_two, qkv_ref, out_ref, gate_up_ref, down_ref, w_ref, lift_ref,
     x_sem, p_sem, e_sem, k_sem, m_sem, t_sem, l_sem, own, loads,
 ):
     me = lax.axis_index("wide")
@@ -570,16 +618,15 @@
             own.at[1, t],
         )
 
-    def feed(t):
-        fed = forward_tile(state[rows(t, BALL), :], gate_up_ref, down_ref)
-        tiles[rows(t, BALL), :] = fed.astype(BF16)
-        for k in (2, 1, 3):
-            give(k, t).start()
-        keep_give(t).start()
-
-    @pl.loop(0, FIRST)
-    def _(t):
-        feed(t)
+    def feed(t, count):
+        at = pl.ds(t * BALL, count * BALL)
+        tiles[at, :] = forward_tile(state[at, :], gate_up_ref, down_ref).astype(BF16)
+        for u in range(t, t + count):
+            for k in (2, 1, 3):
+                give(k, u).start()
+            keep_give(u).start()
+
+    feed(0, 2)
 
     def pass_one(q):
         return remote(
@@ -622,8 +669,8 @@
         for j in (1, 2, 0):
             pass_two(j, q).start()
         pass_one(q).start()
-        two[0, rows(q, TWO), :] = (dot(seconds, w_ref[1, 0]) * 0.125).astype(BF16)
-        one[0, rows(q, ONE), :] = (dot(firsts, w_ref[0, 0]) * 0.125).astype(BF16)
+        two[0, rows(q, TWO), :] = (dot(seconds, w_ref[1, 0]) * SCALE).astype(BF16)
+        one[0, rows(q, ONE), :] = (dot(firsts, w_ref[0, 0]) * SCALE).astype(BF16)
 
     project(mp)
     for k in (1, 3, 2):
@@ -634,13 +681,14 @@
 
         project(peer(k))
 
-    @pl.loop(FIRST, SECOND)
-    def _(t):
-        feed(t)
+    feed(2, 1)
+
+    def hand_to(q, k, level):
+        at = pl.ds(0, ONE) if level == 0 else pl.ds(ONE, TWO)
+        return to_mp(mixed.at[q, at, :], all_mixed.at[at, cols(mp)], m_sem, k, level)
 
     def hand(k, level):
-        at = pl.ds(0, ONE) if level == 0 else pl.ds(ONE, TWO)
-        return to_mp(mixed.at[peer(k), at, :], all_mixed.at[at, cols(mp)], m_sem, k, level)
+        return hand_to(peer(k), k, level)
 
     def keep_hand(level):
         at = pl.ds(0, ONE) if level == 0 else pl.ds(ONE, TWO)
@@ -648,60 +696,76 @@
             mixed.at[mp, at, :], all_mixed.at[at, cols(mp)], own.at[2, level]
         )
 
-    def own_keys(begin, real, count, length):
-        r = lax.broadcasted_iota(I32, (count, length), 0) + begin
-        c = lax.broadcasted_iota(I32, (count, length), 1)
-        return jnp.logical_or(real, r == c)
-
     for j in range(3):
         flags(j).wait()
+
+    def fill(keys_ref, values_ref, begin, src, first, flag):
+        for c in range(src.shape[1] // 256):
+            at = slice(c * 256, (c + 1) * 256)
+            here = flag[:, first + c * 256 : first + (c + 1) * 256] > 0
+            keys, values = augment(src[0, at, :], src[1, at, :], columns_of(here))
+            to = slice(begin + c * 256, begin + (c + 1) * 256)
+            for head in range(2):
+                keys_ref[head, to, :] = keys[head]
+                values_ref[head, to, :] = values[head]
+
+    def masked_of(keys_ref, at):
+        spare = keys_ref[0, at, :].astype(F32)
+        return jnp.min(jnp.where(lanes(256) == 64, spare, 0.0), -1, keepdims=True) < 0.0
+
+    mine = keep_ref[...]
+    fill(keys_one, values_one, 0, one.at[1:], 0, mine)
 
     @pl.loop(0, MP)
     def _(q):
         pass_one(q).wait()
 
+    fill(keys_one, values_one, 4 * ONE, mate_one, 0, mate_keep[0])
+
     @pl.loop(1, MP + 1)
     def _(k):
         q = peer(k)
-        low = lax.broadcasted_iota(I32, (ONE, 128), 1) < 64
-        real = keep_ref[:, : 4 * ONE] > 0
-        mate = mate_keep[0][:, : 4 * ONE] > 0
-        parts = [
-            (one[1], one[2], own_keys(q * ONE, real, ONE, 4 * ONE)),
-            (mate_one[0], mate_one[1], mate),
-        ]
-        mixed[q, 0:ONE, :] = attend_pair(one[0, rows(q, ONE), :], parts, low).astype(BF16)
+        at = rows(q, ONE)
+        mixed[q, 0:ONE, :] = attend_pair(
+            one[0, at, :], one[1, at, :], one[2, at, :], masked_of(keys_one, at),
+            lambda head: keys_one[head], lambda head: values_one[head],
+        )
 
         @pl.when(k < MP)
         def _():
             hand(k, 0).start()
 
     keep_hand(0).start()
+
+    fill(keys_two, values_two, 0, two.at[1:], 4 * ONE, mine)
 
     @pl.loop(0, MP)
     def _(q):
         for j in range(3):
             pass_two(j, q).wait()
 
-    @pl.loop(1, MP + 1)
-    def _(k):
-        q = peer(k)
-        low = lax.broadcasted_iota(I32, (TWO, 128), 1) < 64
-        real = keep_ref[:, 4 * ONE :] > 0
-        parts = [(two[1], two[2], own_keys(q * TWO, real, TWO, 4 * TWO))]
-        for j in range(3):
-            parts.append((mate_two[j, 0], mate_two[j, 1], mate_keep[j][:, 4 * ONE :] > 0))
-        mixed[q, ONE:COARSE, :] = attend_pair(two[0, rows(q, TWO), :], parts, low).astype(BF16)
-
-        @pl.when(k < MP)
-        def _():
-            hand(k, 1).start()
+    for j in range(3):
+        fill(keys_two, values_two, (j + 1) * 4 * TWO, mate_two.at[j], 4 * ONE, mate_keep[j])
+
+    @pl.loop(0, 2)
+    def _(p):
+        at = rows(p, 256)
+        both = attend_pair(
+            two[0, at, :], two[1, at, :], two[2, at, :], masked_of(keys_two, at),
+            lambda head: keys_two[head], lambda head: values_two[head],
+        )
+        for h in range(2):
+            q = p * 2 + h
+            k = lax.rem(q + MP - mp, MP)
+            mixed[q, ONE:COARSE, :] = both[h * TWO : (h + 1) * TWO]
+
+            @pl.when(k > 0)
+            def _():
+                hand_to(q, k, 1).start()
 
     keep_hand(1).start()
 
-    @pl.loop(SECOND, BALLS)
-    def _(t):
-        feed(t)
+    feed(3, 1)
 
     load[5].wait()
     for level in range(2):
@@ -740,10 +804,6 @@
     keep_rise.wait()
     for k in (1, 3, 2):
         rise(k).wait()
-
-
-FIRST = 2
-SECOND = 3
 
 
 def middle(slots, got, mask, keep, weights, collective):
@@ -769,6 +829,10 @@
             pltpu.VMEM((MP, COARSE, LOCAL), BF16),
             pltpu.VMEM((COARSE, WIDTH), BF16),
             pltpu.VMEM((BALLS, 96, WIDTH), BF16),
+            pltpu.VMEM((2, 8 * ONE, LOCAL), BF16),
+            pltpu.VMEM((2, 8 * ONE, LOCAL), BF16),
+            pltpu.VMEM((2, 16 * TWO, LOCAL), BF16),
+            pltpu.VMEM((2, 16 * TWO, LOCAL), BF16),
             pltpu.VMEM((3, WIDTH, WIDTH), BF16),
             pltpu.VMEM((WIDTH, WIDTH), BF16),
             pltpu.VMEM((MP, 2, WIDTH, WIDTH), BF16),

time: 171 us -> 167 us (0.977); the launches traced: 168 us -> 166 us
    pallas_call x1, Pallas kernels: 35.9 us -> 32.5 us  [return_rows(): pl.pallas_call(return_kernel, out_shape=shape((WIDE, CAP, LOCAL), BF16),...]
    pallas_call x1, Pallas kernels: 59.3 us -> 62.1 us  [middle(): pl.pallas_call(middle_kernel, out_shape=[shape((ROWS, LOCAL), BF16), shap...]
where the time goes in v5:
time: 167 us; the launch traced here: 166 us
  Pallas kernels  164 us (98%)
    pallas_call x1, Pallas kernels, middle(): pl.pallas_call(middle_kernel, out_shape=[shape((ROWS, LOCAL), BF16), shap...  62.1 us
    pallas_call x1, Pallas kernels, send_rows(): pl.pallas_call(send_kernel, out_shape=[shape((WIDE, CAP, LOCAL), BF16), s...  55.2 us
    pallas_call x1, Pallas kernels, return_rows(): pl.pallas_call(return_kernel, out_shape=shape((WIDE, CAP, LOCAL), BF16),...  32.5 us
    pallas_call x1, Pallas kernels, on_device(): pl.pallas_call(finish_kernel, out_shape=shape((ROWS, LOCAL), F32), in_spe...  7.16 us
    pallas_call x1, Pallas kernels, index(): pl.pallas_call(index_kernel, out_shape=[shape((32, 128), I32), shape((WID...  4.16 us

profile of v5, /device:TPU:1, one launch (start us, length us, event | category | flops | bytes accessed | tf_op | source)
XLA Modules:
  0.0 166.4 jit_solution(14371132105251251048)
XLA Ops:
  0.0 4.2 %shard_map.91 = (s32[32,128]{1,0:T(8,128)}, s32[32,2,128]{2,1,0:T(2,128)}, s32[32,2,128]{2,1,0:T(2,128)}) custom-call(s32[32,128]{1,0:T(8,128)} %bitcast.30, s32[32,128]{1,0:T(8,128)} %bitcast.31), custom_call_target="tpu_custom_call" | custom-call | tf_op jit(solution)/shard_map/pallas_call | solution.py:95
  4.2 55.2 %shard_map.92 = (bf16[32,256,128]{2,1,0:T(8,128)(2,1)}, s32[32,2,128]{2,1,0:T(2,128)}, bf16[1536,512]{1,0:T(8,128)(2,1)}, bf16[4,128,512]{2,1,0:T(8,128)(2,1)}, ...) custom-call(s32[8192]{0:T(1024)} %bitcast.26, ...), custom_call_target="tpu_custom_call" | custom-call | tf_op jit(solution)/shard_map/pallas_call | solution.py:316
  59.4 3.0 %shard_map.93 = (s32[16,2,128]{2,1,0:T(2,128)}, s32[16,256]{1,0:T(8,128)}, s32[16,96]{1,0:T(8,128)}) custom-call(s32[32,2,128]{2,1,0:T(2,128)} %get-tuple-element.23.codes_ref), custom_call_target="tpu_custom_call" | custom-call | tf_op jit(solution)/shard_map/pallas_call | solution.py:138
  62.4 0.8 reshape.61
  63.2 0.8 slice.7
  64.0 0.1 reshape.62
  64.0 0.6 pad_add_fusion.keep_ref
  64.6 62.1 %shard_map.94 = (bf16[4096,128]{1,0:T(8,128)(2,1)}, bf16[4,4,96,128]{3,2,1,0:T(8,128)(2,1)}) custom-call(s32[4096]{0:T(1024)} %bitcast.29, bf16[8192,128]{1,0:T(8,128)(2,1)} %bitcast.18, s32[16,256]{1,0:T(8,128)} %get-tuple-element.26.mask_ref, s32[1,1536]{1,0:T(1,128)} %pad_add_fusion.keep_ref, bf16[3,512,512]{2,1,0:T(8,128)(2,1)} %bitcast.19, ...), custom_call_target="tpu_custom_call" | custom-call | tf_op jit(solution)/shard_map/pallas_call | solution.py:811
  126.7 32.5 %shard_map.95 = bf16[32,256,128]{2,1,0:T(8,128)(2,1)} custom-call(s32[8192]{0:T(1024)} %bitcast.25, bf16[4096,128]{1,0:T(8,128)(2,1)} %get-tuple-element.33.turned_ref, bf16[16,96,128]{2,1,0:T(8,128)(2,1)} %bitcast.22), custom_call_target="tpu_custom_call" | custom-call | tf_op jit(solution)/shard_map/pallas_call | solution.py:388
  159.3 7.2 %shard_map.96 = f32[4096,128]{1,0:T(8,128)} custom-call(s32[4096]{0:T(1024)} %bitcast.28, bf16[8192,128]{1,0:T(8,128)(2,1)} %bitcast.16), custom_call_target="tpu_custom_call" | custom-call | tf_op jit(solution)/shard_map/pallas_call | solution.py:882

commit v6 on v5

--- a/solution.py
+++ b/solution.py
@@ -101,14 +101,7 @@
     )(perm.reshape(32, 128), mask.reshape(32, 128))
 
 
-def run_matrix(r, c):
-    hot = jnp.logical_or(
-        jnp.logical_and(c < 64, r // 4 == c), jnp.logical_and(c >= 64, r // 8 == c - 64)
-    )
-    return jnp.where(hot, 1.0, 0.0).astype(BF16)
-
-
-def inverse_kernel(codes_ref, slot_ref, mask_ref, keep_ref):
+def invert(codes_ref, slot_ref, mask_ref, keep_ref):
     balls = ROWS // BALL
     rows = lax.broadcasted_iota(I32, (256, 128), 0)
     which = lax.broadcasted_iota(I32, (balls, 128), 0)
@@ -128,20 +121,27 @@
         slot_ref[:, h, :] = slots[:, h * 128 : (h + 1) * 128]
     mask = found[2 * balls :]
     mask_ref[...] = mask.astype(I32)
-    runs = run_matrix(
-        lax.broadcasted_iota(I32, (256, 96), 0), lax.broadcasted_iota(I32, (256, 96), 1)
+    mask = mask.astype(BF16)
+    for f, first in ((4, 0), (8, 8)):
+        side = f // 2
+        count = balls // side
+        total = jnp.zeros((count, 128), F32)
+        for j in range(side):
+            r = lax.broadcasted_iota(I32, (count, balls), 0)
+            c = lax.broadcasted_iota(I32, (count, balls), 1)
+            pick = jnp.where(c == r * side + j, 1.0, 0.0).astype(BF16)
+            r = lax.broadcasted_iota(I32, (256, 128), 0)
+            c = lax.broadcasted_iota(I32, (256, 128), 1)
+            runs = jnp.where(c == r // f + j * (128 // side), 1.0, 0.0).astype(BF16)
+            total = total + dot(dot(pick, mask).astype(BF16), runs)
+        keep_ref[first : first + count, :] = jnp.where(total > 0.5, 1, 0)
+
+
+def run_matrix(r, c):
+    hot = jnp.logical_or(
+        jnp.logical_and(c < 64, r // 4 == c), jnp.logical_and(c >= 64, r // 8 == c - 64)
     )
-    keep_ref[...] = jnp.where(dot(mask.astype(BF16), runs) > 0.5, 1, 0)
-
-
-def inverse(codes):
-    return pl.pallas_call(
-        inverse_kernel,
-        out_shape=[shape((16, 2, 128), I32), shape((16, 256), I32), shape((16, 96), I32)],
-        in_specs=[VMEM],
-        out_specs=[VMEM] * 3,
-        compiler_params=params(),
-    )(codes)
+    return jnp.where(hot, 1.0, 0.0).astype(BF16)
 
 
 def widen(src, dst, rows):
@@ -184,9 +184,9 @@
 
 
 def send_kernel(
-    source_ref, points_ref, codes_ref, qkv_ref, out_ref, gate_up_ref, down_ref, lift_ref,
-    got_ref, got_codes_ref, all_qkv, all_out, all_gate_up, all_down, all_lift,
-    wide, staged, packed, send, recv, own, w_send, w_recv, w_own,
+    source_ref, points_ref, codes_ref, qkv_ref, out_ref, gate_up_ref, down_ref,
+    got_ref, got_codes_out, slot_ref, mask_ref, keep_ref, all_qkv, all_out, all_gate_up, all_down,
+    got_codes_ref, wide, staged, packed, send, recv, own, w_send, w_recv, w_own,
 ):
     me = lax.axis_index("wide")
     mp = lax.axis_index("mp")
@@ -213,11 +213,11 @@
         def cut(j, ref, shard):
             if j == 0:
                 return ref.at[rows(ref, 384), pl.ds(pl.multiple_of(shard * 128, 128), 128)]
-            quarter = (0, 32, 256, 128, 64)[j]
+            quarter = (0, 32, 256, 128)[j]
             return ref.at[shard, rows(ref, quarter), :]
 
         def own_cut(j, ref):
-            quarter = (384, 32, 256, 128, 64)[j]
+            quarter = (384, 32, 256, 128)[j]
             return ref.at[rows(ref, quarter), :]
 
         return cut, own_cut
@@ -226,8 +226,8 @@
     first, _ = part(2 * core, 1)
     second, _ = part(2 * core + 1, 1)
     every, own_every = part(0, 4)
-    shards = [qkv_ref, out_ref, gate_up_ref, down_ref, lift_ref]
-    full = [all_qkv, all_out, all_gate_up, all_down, all_lift]
+    shards = [qkv_ref, out_ref, gate_up_ref, down_ref]
+    full = [all_qkv, all_out, all_gate_up, all_down]
     count = len(shards)
 
     def weight(j, kind, cut, src, shard, device):
@@ -270,9 +270,12 @@
 
     @pl.loop(1, WIDE)
     def _(k):
+        codes_copy(k).start()
+
+    @pl.loop(1, WIDE)
+    def _(k):
         gather_bucket(0, lambda s: source_ref[s], wide, staged, packed, turn_of(me, k))
         rows_copy(k).start()
-        codes_copy(k).start()
 
     gather_bucket(0, lambda s: source_ref[s], wide, staged, packed, me)
     mine = [
@@ -285,25 +288,40 @@
         )
     for copy in mine:
         copy.start()
-    for j in range(count):
+
+    def forward(j):
         weights[j][0].wait_recv()
         weights[j][2].start()
         weights[j][4].start()
         weights[j][1].wait_recv()
         weights[j][3].start()
         weights[j][5].start()
-    for j in range(count):
+
+    def forward_last(j):
         weights[j][2].wait_recv()
         weights[j][6].start()
         weights[j][3].wait_recv()
         weights[j][7].start()
+
+    forward(0)
+    forward(1)
     for copy in mine:
         copy.wait()
+
+    @pl.loop(1, WIDE)
+    def _(k):
+        codes_copy(k).wait()
+
+    invert(got_codes_ref, slot_ref, mask_ref, keep_ref)
+    got_codes_out[...] = got_codes_ref[...]
+    for j in range(2, count):
+        forward(j)
+    for j in range(count):
+        forward_last(j)
 
     @pl.loop(1, WIDE)
     def _(k):
         rows_copy(k).wait()
-        codes_copy(k).wait()
 
     for j in range(count):
         for kind in range(4):
@@ -318,24 +336,27 @@
         out_shape=[
             shape((WIDE, CAP, LOCAL), BF16),
             shape((WIDE, 2, 128), I32),
+            shape((16, 2, 128), I32),
+            shape((16, 256), I32),
+            shape((12, 128), I32),
             shape((3 * WIDTH, WIDTH), BF16),
             shape((MP, LOCAL, WIDTH), BF16),
             shape((MP, 2 * WIDTH, WIDTH), BF16),
             shape((MP, WIDTH, WIDTH), BF16),
-            shape((MP, 2 * LOCAL, WIDTH), BF16),
         ],
-        in_specs=[SMEM, VMEM, ANY] + [VMEM] * 5,
-        out_specs=[ANY] * 7,
+        in_specs=[SMEM, VMEM, ANY] + [VMEM] * 4,
+        out_specs=[ANY] + [VMEM] * 4 + [ANY] * 4,
         scratch_shapes=[
+            pltpu.VMEM((WIDE, 2, 128), I32),
             pltpu.VMEM((ROWS, LOCAL), F32),
             pltpu.VMEM((1, CAP, LOCAL), F32),
             pltpu.VMEM((WIDE, CAP, LOCAL), BF16),
             pltpu.SemaphoreType.DMA((WIDE, 2)),
             pltpu.SemaphoreType.DMA((WIDE, 2)),
             pltpu.SemaphoreType.DMA((2,)),
-            pltpu.SemaphoreType.DMA((5, 8)),
-            pltpu.SemaphoreType.DMA((5, 8)),
-            pltpu.SemaphoreType.DMA((5,)),
+            pltpu.SemaphoreType.DMA((4, 8)),
+            pltpu.SemaphoreType.DMA((4, 8)),
+            pltpu.SemaphoreType.DMA((4,)),
         ],
         compiler_params=params(collective),
     )(source, points, codes, *weights)
@@ -410,14 +431,9 @@
 
 
 def columns_of(flags):
-    size = 256
-    eye = lax.broadcasted_iota(I32, (size, size), 0) == lax.broadcasted_iota(I32, (size, size), 1)
-    eye = jnp.where(eye, 1.0, 0.0).astype(BF16)
-    out = []
-    for begin in range(0, flags.shape[1], size):
-        row = jnp.where(flags[:, begin : begin + size], 1.0, 0.0)
-        out.append(dot_t(eye, jnp.broadcast_to(row, (128, size)).astype(BF16)))
-    return jnp.concatenate(out, 0)
+    eye = lax.broadcasted_iota(I32, (128, 128), 0) == lax.broadcasted_iota(I32, (128, 128), 1)
+    row = jnp.broadcast_to(jnp.where(flags, 1.0, 0.0), (128, 128)).astype(BF16)
+    return dot_t(jnp.where(eye, 1.0, 0.0).astype(BF16), row)
 
 
 def augment(keys, values, columns):
@@ -458,21 +474,32 @@
     return (jnp.where(low, out[0], out[1]) / sums).astype(BF16)
 
 
+def attend_ball(queries, keys, values, allowed):
+    low = lanes(BALL) < 64
+    out = []
+    for head in range(2):
+        mine = low if head == 0 else jnp.logical_not(low)
+        q = jnp.where(mine, queries, jnp.zeros_like(queries))
+        scores = jnp.where(allowed, dot_t(q, keys), -1e30)
+        weights = jnp.exp2(scores - jnp.max(scores, -1, keepdims=True))
+        total = jnp.sum(weights, -1, keepdims=True)
+        out.append(dot(weights.astype(BF16), values) / total)
+    return jnp.where(low, out[0], out[1]).astype(BF16)
+
+
 def fine_ball(x, real, qkv_ref, out_ref):
     x = x.astype(F32)
     normed = norm(x).astype(BF16)
     q = (dot(normed, qkv_ref[0]) * SCALE).astype(BF16)
     k = dot(normed, qkv_ref[1]).astype(BF16)
     v = dot(normed, qkv_ref[2]).astype(BF16)
-    columns = columns_of(real)
-    masked = columns[:, :1] < 0.5
+    rows = lax.broadcasted_iota(I32, (BALL, BALL), 0)
+    cols = lax.broadcasted_iota(I32, (BALL, BALL), 1)
+    allowed = jnp.logical_or(real, rows == cols)
     mixed = []
     for g in range(MP):
         at = slice(g * 128, (g + 1) * 128)
-        keys, values = augment(k[:, at], v[:, at], columns)
-        mixed.append(
-            attend_pair(q[:, at], k[:, at], v[:, at], masked, keys.__getitem__, values.__getitem__)
-        )
+        mixed.append(attend_ball(q[:, at], k[:, at], v[:, at], allowed))
     state = x + dot(jnp.concatenate(mixed, 1), out_ref[...])
     high = state.astype(BF16)
     rest = (state - high.astype(F32)).astype(BF16)
@@ -518,7 +545,7 @@
     lift_hbm, turned_ref, lifted_ref,
     wide, staged, packed, x, state, pooled, tiles, one, two, mate_one, mate_two, mate_keep,
     mixed, all_mixed, lifted, keys_one, values_one, keys_two, values_two, qkv_ref, out_ref, gate_up_ref, down_ref, w_ref, lift_ref,
-    x_sem, p_sem, e_sem, k_sem, m_sem, t_sem, l_sem, own, loads,
+    x_sem, p_sem, e_sem, k_sem, m_sem, t_sem, l_sem, w_sem, own, loads,
 ):
     me = lax.axis_index("wide")
     mp = lax.axis_index("mp")
@@ -538,7 +565,7 @@
             (gate_up_hbm, gate_up_ref),
             (down_hbm, down_ref),
             (coarse_hbm, w_ref),
-            (lift_hbm, lift_ref),
+            (lift_hbm, lift_ref.at[mp]),
         ])
     ]
     for copy in load:
@@ -599,6 +626,20 @@
         for k in (2, 1, 3):
             share(k, t).start()
 
+    core = lax.rem(me, 2)
+    lift_half = pl.ds(pl.multiple_of(core * LOCAL, LOCAL), LOCAL)
+
+    def weigh(k):
+        part = lift_ref.at[mp, lift_half, :]
+        return to_mp(part, part, w_sem, k, 0)
+
+    def weigh_on(k):
+        part = lift_ref.at[peer(MP - k), lift_half, :]
+        return remote(part, part, w_sem.at[0, k, 1], w_sem.at[1, k, 1], {"wide": others[0]})
+
+    load[5].wait()
+    for k in (1, 3, 2):
+        weigh(k).start()
     load[2].wait()
     load[3].wait()
 
@@ -682,6 +723,9 @@
         project(peer(k))
 
     feed(2, 1)
+    for k in (1, 3, 2):
+        weigh(k).wait_recv()
+        weigh_on(k).start()
 
     def hand_to(q, k, level):
         at = pl.ds(0, ONE) if level == 0 else pl.ds(ONE, TWO)
@@ -700,11 +744,11 @@
         flags(j).wait()
 
     def fill(keys_ref, values_ref, begin, src, first, flag):
-        for c in range(src.shape[1] // 256):
-            at = slice(c * 256, (c + 1) * 256)
-            here = flag[:, first + c * 256 : first + (c + 1) * 256] > 0
+        for c in range(src.shape[1] // 128):
+            at = slice(c * 128, (c + 1) * 128)
+            here = flag[first + c : first + c + 1, :] > 0
             keys, values = augment(src[0, at, :], src[1, at, :], columns_of(here))
-            to = slice(begin + c * 256, begin + (c + 1) * 256)
+            to = slice(begin + c * 128, begin + (c + 1) * 128)
             for head in range(2):
                 keys_ref[head, to, :] = keys[head]
                 values_ref[head, to, :] = values[head]
@@ -737,7 +781,7 @@
 
     keep_hand(0).start()
 
-    fill(keys_two, values_two, 0, two.at[1:], 4 * ONE, mine)
+    fill(keys_two, values_two, 0, two.at[1:], 8, mine)
 
     @pl.loop(0, MP)
     def _(q):
@@ -745,7 +789,7 @@
             pass_two(j, q).wait()
 
     for j in range(3):
-        fill(keys_two, values_two, (j + 1) * 4 * TWO, mate_two.at[j], 4 * ONE, mate_keep[j])
+        fill(keys_two, values_two, (j + 1) * 4 * TWO, mate_two.at[j], 8, mate_keep[j])
 
     @pl.loop(0, 2)
     def _(p):
@@ -767,7 +811,9 @@
 
     feed(3, 1)
 
-    load[5].wait()
+    for k in (1, 3, 2):
+        weigh(k).wait_send()
+        weigh_on(k).wait()
     for level in range(2):
         keep_hand(level).wait()
         for k in (1, 3, 2):
@@ -825,7 +871,7 @@
             pltpu.VMEM((3, 4 * TWO, LOCAL), BF16),
             pltpu.VMEM((2, 4 * ONE, LOCAL), BF16),
             pltpu.VMEM((3, 2, 4 * TWO, LOCAL), BF16),
-            pltpu.VMEM((3, 1, 12 * 128), I32),
+            pltpu.VMEM((3, 12, 128), I32),
             pltpu.VMEM((MP, COARSE, LOCAL), BF16),
             pltpu.VMEM((COARSE, WIDTH), BF16),
             pltpu.VMEM((BALLS, 96, WIDTH), BF16),
@@ -846,6 +892,7 @@
             dma((2, MP, 2)),
             dma((2, MP, BALLS)),
             dma((2, MP, 1)),
+            dma((2, MP, 2)),
             dma((4, BALLS)),
             dma((6,)),
         ],
@@ -855,7 +902,7 @@
 
 def on_device(points, mask, perm, w_qkv, w_out, w_gate_up, w_down, w_coarse, w_coarse_out):
     slot, source, codes = index(perm, mask)
-    got, got_code, full_qkv, full_out, full_gate_up, full_down, full_lift = send_rows(
+    got, got_code, landed, owned_mask, keep, full_qkv, full_out, full_gate_up, full_down = send_rows(
         source.reshape(SLOTS),
         points,
         codes,
@@ -864,18 +911,16 @@
             w_out,
             w_gate_up.reshape(2 * WIDTH, WIDTH),
             w_down,
-            w_coarse_out.reshape(2 * LOCAL, WIDTH),
         ],
         1,
     )
     full_qkv = full_qkv.reshape(3, WIDTH, WIDTH)
     full_out = full_out.reshape(WIDTH, WIDTH)
     full_gate_up = full_gate_up.reshape(MP, 2, WIDTH, WIDTH)
-    landed, owned_mask, kept = inverse(got_code)
-    keep = jnp.concatenate([kept[:, :64].reshape(1, 4 * ONE), kept[:, 64:].reshape(1, 4 * TWO)], 1)
+    own_lift = w_coarse_out.reshape(2 * LOCAL, WIDTH)
     turned, lifted = middle(
         landed.reshape(ROWS), got.reshape(SLOTS, LOCAL), owned_mask, keep,
-        [full_qkv, full_out, full_gate_up, full_down, w_coarse, full_lift], 2,
+        [full_qkv, full_out, full_gate_up, full_down, w_coarse, own_lift], 2,
     )
     lifted = lifted.reshape(MP * BALLS, 96, LOCAL)
     returned = return_rows(got_code.reshape(SLOTS), turned, lifted, 3)

time: 167 us -> 155 us (0.928)
  Pallas kernels: 164 us -> 155 us
    pallas_call x1, Pallas kernels: 55.2 us -> 51.6 us  [send_rows(): pl.pallas_call(send_kernel, out_shape=[shape((WIDE, CAP, LOCAL), BF16), s...]
    pallas_call x1 -> x0, Pallas kernels: 3.03 us -> none  [inverse(): pl.pallas_call(inverse_kernel, out_shape=[shape((16, 2, 128), I32), shape...]
    pallas_call x1, Pallas kernels: 62.1 us -> 59.1 us  [middle(): pl.pallas_call(middle_kernel, out_shape=[shape((ROWS, LOCAL), BF16), shap...]
where the time goes in v6:
time: 155 us
  Pallas kernels  155 us (100%)
    pallas_call x1, Pallas kernels, middle(): pl.pallas_call(middle_kernel, out_shape=[shape((ROWS, LOCAL), BF16), shap...  59.1 us
    pallas_call x1, Pallas kernels, send_rows(): pl.pallas_call(send_kernel, out_shape=[shape((WIDE, CAP, LOCAL), BF16), s...  51.6 us
    pallas_call x1, Pallas kernels, return_rows(): pl.pallas_call(return_kernel, out_shape=shape((WIDE, CAP, LOCAL), BF16),...  32.6 us
    pallas_call x1, Pallas kernels, on_device(): pl.pallas_call(finish_kernel, out_shape=shape((ROWS, LOCAL), F32), in_spe...  7.16 us
    pallas_call x1, Pallas kernels, index(): pl.pallas_call(index_kernel, out_shape=[shape((32, 128), I32), shape((WID...  4.16 us

profile of v6, /device:TPU:1, one launch (start us, length us, event | category | flops | bytes accessed | tf_op | source)
XLA Modules:
  0.0 154.6 jit_solution(9541961756283172241)
XLA Ops:
  0.0 4.2 %shard_map.91 = (s32[32,128]{1,0:T(8,128)}, s32[32,2,128]{2,1,0:T(2,128)}, s32[32,2,128]{2,1,0:T(2,128)}) custom-call(s32[32,128]{1,0:T(8,128)} %bitcast.28, s32[32,128]{1,0:T(8,128)} %bitcast.29), custom_call_target="tpu_custom_call" | custom-call | tf_op jit(solution)/shard_map/pallas_call | solution.py:95
  4.2 51.6 %shard_map.92 = (bf16[32,256,128]{2,1,0:T(8,128)(2,1)}, s32[32,2,128]{2,1,0:T(2,128)}, s32[16,2,128]{2,1,0:T(2,128)}, s32[16,256]{1,0:T(8,128)}, s32[12,128]{1,0...) custom-call(s32[8192]{0:T(1024)} %bitcast.25, ...), custom_call_target="tpu_custom_call" | custom-call | tf_op jit(solution)/shard_map/pallas_call | solution.py:334
  55.8 59.1 %shard_map.93 = (bf16[4096,128]{1,0:T(8,128)(2,1)}, bf16[4,4,96,128]{3,2,1,0:T(8,128)(2,1)}) custom-call(s32[4096]{0:T(1024)} %bitcast.27, bf16[8192,128]{1,0:T(8,128)(2,1)} %bitcast.17, s32[16,256]{1,0:T(8,128)} %get-tuple-element.25.mask_ref, s32[12,128]{1,0:T(8,128)} %get-tuple-element.26.keep_ref, bf16[3,512,512]{2,1,0:T(8,128)(2,1)} %bitcast.18, ...), custom_call_target="tpu_custom_call" | custom-call | tf_op jit(solution)/shard_map/pallas_call | solution.py:857
  114.9 32.6 %shard_map.94 = bf16[32,256,128]{2,1,0:T(8,128)(2,1)} custom-call(s32[8192]{0:T(1024)} %bitcast.24, bf16[4096,128]{1,0:T(8,128)(2,1)} %get-tuple-element.31.turned_ref, bf16[16,96,128]{2,1,0:T(8,128)(2,1)} %bitcast.22), custom_call_target="tpu_custom_call" | custom-call | tf_op jit(solution)/shard_map/pallas_call | solution.py:409
  147.5 7.2 %shard_map.95 = f32[4096,128]{1,0:T(8,128)} custom-call(s32[4096]{0:T(1024)} %bitcast.26, bf16[8192,128]{1,0:T(8,128)(2,1)} %bitcast.15), custom_call_target="tpu_custom_call" | custom-call | tf_op jit(solution)/shard_map/pallas_call | solution.py:927

commit v7 on v6

--- a/solution.py
+++ b/solution.py
@@ -184,8 +184,8 @@
 
 
 def send_kernel(
-    source_ref, points_ref, codes_ref, qkv_ref, out_ref, gate_up_ref, down_ref,
-    got_ref, got_codes_out, slot_ref, mask_ref, keep_ref, all_qkv, all_out, all_gate_up, all_down,
+    source_ref, points_ref, codes_ref, qkv_ref, out_ref, lift_ref, down_ref,
+    got_ref, got_codes_out, slot_ref, mask_ref, keep_ref, all_qkv, all_out, all_lift, all_down,
     got_codes_ref, wide, staged, packed, send, recv, own, w_send, w_recv, w_own,
 ):
     me = lax.axis_index("wide")
@@ -213,11 +213,11 @@
         def cut(j, ref, shard):
             if j == 0:
                 return ref.at[rows(ref, 384), pl.ds(pl.multiple_of(shard * 128, 128), 128)]
-            quarter = (0, 32, 256, 128)[j]
+            quarter = (0, 32, 64, 128)[j]
             return ref.at[shard, rows(ref, quarter), :]
 
         def own_cut(j, ref):
-            quarter = (384, 32, 256, 128)[j]
+            quarter = (384, 32, 64, 128)[j]
             return ref.at[rows(ref, quarter), :]
 
         return cut, own_cut
@@ -226,8 +226,8 @@
     first, _ = part(2 * core, 1)
     second, _ = part(2 * core + 1, 1)
     every, own_every = part(0, 4)
-    shards = [qkv_ref, out_ref, gate_up_ref, down_ref]
-    full = [all_qkv, all_out, all_gate_up, all_down]
+    shards = [qkv_ref, out_ref, lift_ref, down_ref]
+    full = [all_qkv, all_out, all_lift, all_down]
     count = len(shards)
 
     def weight(j, kind, cut, src, shard, device):
@@ -341,7 +341,7 @@
             shape((12, 128), I32),
             shape((3 * WIDTH, WIDTH), BF16),
             shape((MP, LOCAL, WIDTH), BF16),
-            shape((MP, 2 * WIDTH, WIDTH), BF16),
+            shape((MP, 2 * LOCAL, WIDTH), BF16),
             shape((MP, WIDTH, WIDTH), BF16),
         ],
         in_specs=[SMEM, VMEM, ANY] + [VMEM] * 4,
@@ -519,15 +519,14 @@
 BALLS = QUARTER // BALL
 
 
-def forward_tile(state, gate_up_ref, down_ref):
+def forward_tile(state, mp, gate_up_ref, down_ref):
     normed = norm(state).astype(BF16)
     total = state
     for c in range(MP):
-        gate = dot(normed, gate_up_ref[c, 0])
-        up = dot(normed, gate_up_ref[c, 1])
-        half = gate * 0.5
+        half = dot(normed, gate_up_ref[c, :WIDTH, :]) * 0.5
+        up = dot(normed, gate_up_ref[c, WIDTH:, :])
         activated = ((half + half * jnp.tanh(half)) * up).astype(BF16)
-        total = total + dot(activated, down_ref[c])
+        total = total + dot(activated, down_ref[lax.rem(mp + c, MP)])
     return total
 
 
@@ -545,7 +544,7 @@
     lift_hbm, turned_ref, lifted_ref,
     wide, staged, packed, x, state, pooled, tiles, one, two, mate_one, mate_two, mate_keep,
     mixed, all_mixed, lifted, keys_one, values_one, keys_two, values_two, qkv_ref, out_ref, gate_up_ref, down_ref, w_ref, lift_ref,
-    x_sem, p_sem, e_sem, k_sem, m_sem, t_sem, l_sem, w_sem, own, loads,
+    x_sem, p_sem, e_sem, k_sem, m_sem, t_sem, l_sem, g_sem, b_sem, f_sem, own, loads,
 ):
     me = lax.axis_index("wide")
     mp = lax.axis_index("mp")
@@ -555,23 +554,33 @@
         pl.semaphore_signal(
             barrier, inc=1, device_id={"mp": lax.rem(mp + k, MP)}, device_id_type=MESH
         )
-    for other in others:
+    for other in (others[0], others[2]):
         pl.semaphore_signal(barrier, inc=1, device_id={"wide": other}, device_id_type=MESH)
+
+    def chip(i):
+        return 2 * lax.rem(i * 7, WIDE // 2)
+
+    @pl.loop(1, WIDE // 2)
+    def _(i):
+        pl.semaphore_signal(
+            barrier, inc=1, device_id={"wide": lax.rem(me + chip(i), WIDE)}, device_id_type=MESH
+        )
+
     load = [
         pltpu.make_async_copy(src, dst, loads.at[j])
         for j, (src, dst) in enumerate([
             (qkv_hbm, qkv_ref),
             (out_hbm, out_ref),
-            (gate_up_hbm, gate_up_ref),
+            (gate_up_hbm, gate_up_ref.at[0]),
             (down_hbm, down_ref),
             (coarse_hbm, w_ref),
-            (lift_hbm, lift_ref.at[mp]),
+            (lift_hbm, lift_ref),
         ])
     ]
     for copy in load:
         copy.start()
     widen(got_ref, wide, SLOTS)
-    pl.semaphore_wait(barrier, MP + 2)
+    pl.semaphore_wait(barrier, MP - 1 + 2 + WIDE // 2 - 1)
 
     def rows(t, size):
         return pl.ds(pl.multiple_of(t * size, size), size)
@@ -584,6 +593,25 @@
 
     def to_mp(src, dst, sem, k, t):
         return remote(src, dst, sem.at[0, k, t], sem.at[1, k, t], {"mp": peer(k)})
+
+    def piece(shards, owner):
+        return gate_up_ref.at[shards, pl.ds(pl.multiple_of(owner * 32, 32), 32), :]
+
+    def fetch(k):
+        src = gate_up_hbm.at[pl.ds(pl.multiple_of(me * 32, 32), 32), :]
+        return to_mp(src, piece(MP - k, me), g_sem, k, 0)
+
+    def broadcast(i):
+        part = piece(pl.ds(1, 3), me)
+        to = {"wide": lax.rem(me + chip(i), WIDE)}
+        return remote(part, part, b_sem.at[0, i], b_sem.at[1, i], to)
+
+    def pass_on(i):
+        part = piece(pl.ds(1, 3), lax.rem(me + WIDE - chip(i), WIDE))
+        return remote(part, part, f_sem.at[0, i], f_sem.at[1, i], {"wide": others[0]})
+
+    for k in (2, 1, 3):
+        fetch(k).start()
 
     def turn(k, t):
         return to_mp(packed.at[peer(k) * BALLS + t], x.at[rows(t, BALL), cols(mp)], x_sem, k, t)
@@ -608,6 +636,14 @@
 
     for j in range(3):
         flags(j).start()
+    for k in (1, 3, 2):
+        fetch(k).wait_recv()
+
+    @pl.loop(1, WIDE // 2)
+    def _(i):
+        broadcast(i).start()
+
+    pass_on(0).start()
     load[0].wait()
     load[1].wait()
 
@@ -626,20 +662,6 @@
         for k in (2, 1, 3):
             share(k, t).start()
 
-    core = lax.rem(me, 2)
-    lift_half = pl.ds(pl.multiple_of(core * LOCAL, LOCAL), LOCAL)
-
-    def weigh(k):
-        part = lift_ref.at[mp, lift_half, :]
-        return to_mp(part, part, w_sem, k, 0)
-
-    def weigh_on(k):
-        part = lift_ref.at[peer(MP - k), lift_half, :]
-        return remote(part, part, w_sem.at[0, k, 1], w_sem.at[1, k, 1], {"wide": others[0]})
-
-    load[5].wait()
-    for k in (1, 3, 2):
-        weigh(k).start()
     load[2].wait()
     load[3].wait()
 
@@ -661,13 +683,16 @@
 
     def feed(t, count):
         at = pl.ds(t * BALL, count * BALL)
-        tiles[at, :] = forward_tile(state[at, :], gate_up_ref, down_ref).astype(BF16)
+        tiles[at, :] = forward_tile(state[at, :], mp, gate_up_ref, down_ref).astype(BF16)
         for u in range(t, t + count):
             for k in (2, 1, 3):
                 give(k, u).start()
             keep_give(u).start()
 
-    feed(0, 2)
+    @pl.loop(1, WIDE // 2)
+    def _(i):
+        broadcast(i).wait_recv()
+        pass_on(i).start()
 
     def pass_one(q):
         return remote(
@@ -722,10 +747,12 @@
 
         project(peer(k))
 
+    @pl.loop(0, WIDE // 2)
+    def _(i):
+        pass_on(i).wait_recv()
+
+    feed(0, 2)
     feed(2, 1)
-    for k in (1, 3, 2):
-        weigh(k).wait_recv()
-        weigh_on(k).start()
 
     def hand_to(q, k, level):
         at = pl.ds(0, ONE) if level == 0 else pl.ds(ONE, TWO)
@@ -811,9 +838,7 @@
 
     feed(3, 1)
 
-    for k in (1, 3, 2):
-        weigh(k).wait_send()
-        weigh_on(k).wait()
+    load[5].wait()
     for level in range(2):
         keep_hand(level).wait()
         for k in (1, 3, 2):
@@ -847,6 +872,16 @@
             share(k, t).wait_send()
             give(k, t).wait()
 
+    @pl.loop(1, WIDE // 2)
+    def _(i):
+        broadcast(i).wait_send()
+
+    @pl.loop(0, WIDE // 2)
+    def _(i):
+        pass_on(i).wait_send()
+
+    for k in (1, 3, 2):
+        fetch(k).wait_send()
     keep_rise.wait()
     for k in (1, 3, 2):
         rise(k).wait()
@@ -881,7 +916,7 @@
             pltpu.VMEM((2, 16 * TWO, LOCAL), BF16),
             pltpu.VMEM((3, WIDTH, WIDTH), BF16),
             pltpu.VMEM((WIDTH, WIDTH), BF16),
-            pltpu.VMEM((MP, 2, WIDTH, WIDTH), BF16),
+            pltpu.VMEM((MP, 2 * WIDTH, WIDTH), BF16),
             pltpu.VMEM((MP, WIDTH, WIDTH), BF16),
             pltpu.VMEM((2, 3, WIDTH, LOCAL), BF16),
             pltpu.VMEM((MP, 2 * LOCAL, WIDTH), BF16),
@@ -892,7 +927,9 @@
             dma((2, MP, 2)),
             dma((2, MP, BALLS)),
             dma((2, MP, 1)),
-            dma((2, MP, 2)),
+            dma((2, MP, 1)),
+            dma((2, WIDE // 2)),
+            dma((2, WIDE // 2)),
             dma((4, BALLS)),
             dma((6,)),
         ],
@@ -902,25 +939,24 @@
 
 def on_device(points, mask, perm, w_qkv, w_out, w_gate_up, w_down, w_coarse, w_coarse_out):
     slot, source, codes = index(perm, mask)
-    got, got_code, landed, owned_mask, keep, full_qkv, full_out, full_gate_up, full_down = send_rows(
+    got, got_code, landed, owned_mask, keep, full_qkv, full_out, full_lift, full_down = send_rows(
         source.reshape(SLOTS),
         points,
         codes,
         [
             w_qkv.reshape(3 * WIDTH, LOCAL),
             w_out,
-            w_gate_up.reshape(2 * WIDTH, WIDTH),
+            w_coarse_out.reshape(2 * LOCAL, WIDTH),
             w_down,
         ],
         1,
     )
     full_qkv = full_qkv.reshape(3, WIDTH, WIDTH)
     full_out = full_out.reshape(WIDTH, WIDTH)
-    full_gate_up = full_gate_up.reshape(MP, 2, WIDTH, WIDTH)
-    own_lift = w_coarse_out.reshape(2 * LOCAL, WIDTH)
+    own_gate_up = w_gate_up.reshape(2 * WIDTH, WIDTH)
     turned, lifted = middle(
         landed.reshape(ROWS), got.reshape(SLOTS, LOCAL), owned_mask, keep,
-        [full_qkv, full_out, full_gate_up, full_down, w_coarse, own_lift], 2,
+        [full_qkv, full_out, own_gate_up, full_down, w_coarse, full_lift], 2,
     )
     lifted = lifted.reshape(MP * BALLS, 96, LOCAL)
     returned = return_rows(got_code.reshape(SLOTS), turned, lifted, 3)

time: 155 us -> 150 us (0.968)
  Pallas kernels: 155 us -> 149 us
    pallas_call x1, Pallas kernels: 51.6 us -> 38.8 us  [send_rows(): pl.pallas_call(send_kernel, out_shape=[shape((WIDE, CAP, LOCAL), BF16), s...]
    pallas_call x1, Pallas kernels: 59.1 us -> 65.2 us  [middle(): pl.pallas_call(middle_kernel, out_shape=[shape((ROWS, LOCAL), BF16), shap...]
where the time goes in v7:
time: 150 us; the launch traced here: 149 us
  Pallas kernels  149 us (99%)
    pallas_call x1, Pallas kernels, middle(): pl.pallas_call(middle_kernel, out_shape=[shape((ROWS, LOCAL), BF16), shap...  65.2 us
    pallas_call x1, Pallas kernels, send_rows(): pl.pallas_call(send_kernel, out_shape=[shape((WIDE, CAP, LOCAL), BF16), s...  38.8 us
    pallas_call x1, Pallas kernels, return_rows(): pl.pallas_call(return_kernel, out_shape=shape((WIDE, CAP, LOCAL), BF16),...  34 us
    pallas_call x1, Pallas kernels, on_device(): pl.pallas_call(finish_kernel, out_shape=shape((ROWS, LOCAL), F32), in_spe...  7.16 us
    pallas_call x1, Pallas kernels, index(): pl.pallas_call(index_kernel, out_shape=[shape((32, 128), I32), shape((WID...  4.17 us

profile of v7, /device:TPU:1, one launch (start us, length us, event | category | flops | bytes accessed | tf_op | source)
XLA Modules:
  0.0 149.3 jit_solution(3787647165086679926)
XLA Ops:
  0.0 4.2 %shard_map.91 = (s32[32,128]{1,0:T(8,128)}, s32[32,2,128]{2,1,0:T(2,128)}, s32[32,2,128]{2,1,0:T(2,128)}) custom-call(s32[32,128]{1,0:T(8,128)} %bitcast.26, s32[32,128]{1,0:T(8,128)} %bitcast.27), custom_call_target="tpu_custom_call" | custom-call | tf_op jit(solution)/shard_map/pallas_call | solution.py:95
  4.2 38.8 %shard_map.92 = (bf16[32,256,128]{2,1,0:T(8,128)(2,1)}, s32[32,2,128]{2,1,0:T(2,128)}, s32[16,2,128]{2,1,0:T(2,128)}, s32[16,256]{1,0:T(8,128)}, s32[12,128]{1,0...) custom-call(s32[8192]{0:T(1024)} %bitcast.23, ...), custom_call_target="tpu_custom_call" | custom-call | tf_op jit(solution)/shard_map/pallas_call | solution.py:334
  43.0 65.2 %shard_map.93 = (bf16[4096,128]{1,0:T(8,128)(2,1)}, bf16[4,4,96,128]{3,2,1,0:T(8,128)(2,1)}) custom-call(s32[4096]{0:T(1024)} %bitcast.25, bf16[8192,128]{1,0:T(8,128)(2,1)} %bitcast.15, s32[16,256]{1,0:T(8,128)} %get-tuple-element.25.mask_ref, s32[12,128]{1,0:T(8,128)} %get-tuple-element.26.keep_ref, bf16[3,512,512]{2,1,0:T(8,128)(2,1)} %bitcast.16, ...), custom_call_target="tpu_custom_call" | custom-call | tf_op jit(solution)/shard_map/pallas_call | solution.py:892
  108.1 34.0 %shard_map.94 = bf16[32,256,128]{2,1,0:T(8,128)(2,1)} custom-call(s32[8192]{0:T(1024)} %bitcast.22, bf16[4096,128]{1,0:T(8,128)(2,1)} %get-tuple-element.31.turned_ref, bf16[16,96,128]{2,1,0:T(8,128)(2,1)} %bitcast.20), custom_call_target="tpu_custom_call" | custom-call | tf_op jit(solution)/shard_map/pallas_call | solution.py:409
  142.2 7.2 %shard_map.95 = f32[4096,128]{1,0:T(8,128)} custom-call(s32[4096]{0:T(1024)} %bitcast.24, bf16[8192,128]{1,0:T(8,128)(2,1)} %bitcast.14), custom_call_target="tpu_custom_call" | custom-call | tf_op jit(solution)/shard_map/pallas_call | solution.py:963

commit v8 on v7

--- a/solution.py
+++ b/solution.py
@@ -151,15 +151,36 @@
         dst[at, :] = src[at, :].astype(dst.dtype)
 
 
-def finish_kernel(slot_ref, got_ref, out_ref, wide):
-    widen(got_ref, wide, SLOTS)
-
-    @pl.loop(0, ROWS // UNROLL)
+def finish_kernel(slot_ref, got_ref, out_ref, narrow, wide, done, in_sem, out_sem):
+    def chunk(ref, i, size):
+        return ref.at[pl.ds(pl.multiple_of(i * size, size), size), :]
+
+    def load(i):
+        return pltpu.make_async_copy(chunk(got_ref, i, 1024), chunk(narrow, i, 1024), in_sem.at[i])
+
+    def store(i):
+        return pltpu.make_async_copy(chunk(done, i, 512), chunk(out_ref, i, 512), out_sem.at[i])
+
+    for i in range(SLOTS // 1024):
+        load(i).start()
+    for i in range(SLOTS // 1024):
+        load(i).wait()
+        widen(chunk(narrow, i, 1024), chunk(wide, i, 1024), 1024)
+
+    @pl.loop(0, ROWS // 512)
     def _(i):
-        base = i * UNROLL
-        lines = [wide[pl.ds(slot_ref[base + u], 1), :] for u in range(UNROLL)]
-        for u in range(UNROLL):
-            out_ref[pl.ds(base + u, 1), :] = lines[u]
+        @pl.loop(0, 512 // UNROLL)
+        def _(j):
+            base = i * 512 + j * UNROLL
+            lines = [wide[pl.ds(slot_ref[base + u], 1), :] for u in range(UNROLL)]
+            for u in range(UNROLL):
+                done[pl.ds(base + u, 1), :] = lines[u]
+
+        store(i).start()
+
+    @pl.loop(0, ROWS // 512)
+    def _(i):
+        store(i).wait()
 
 
 def remote(src, dst, send, recv, device):
@@ -362,67 +383,6 @@
     )(source, points, codes, *weights)
 
 
-def return_kernel(
-    code_ref, turned_ref, lifted_ref, got_ref, wide, staged, packed, send, recv, own
-):
-    me = lax.axis_index("wide")
-    barrier = pltpu.get_barrier_semaphore()
-
-    @pl.loop(1, WIDE)
-    def _(k):
-        pl.semaphore_signal(
-            barrier, inc=1, device_id={"wide": lax.rem(me + k, WIDE)}, device_id_type=MESH
-        )
-
-    runs = run_matrix(
-        lax.broadcasted_iota(I32, (BALL, 96), 0), lax.broadcasted_iota(I32, (BALL, 96), 1)
-    )
-
-    @pl.loop(0, ROWS // BALL)
-    def _(i):
-        at = pl.ds(pl.multiple_of(i * BALL, BALL), BALL)
-        wide[at, :] = turned_ref[at, :].astype(F32) + dot(runs, lifted_ref[i])
-
-    wide[ROWS : ROWS + 8, :] = jnp.zeros((8, LOCAL), F32)
-    pl.semaphore_wait(barrier, WIDE - 1)
-
-    def rows_copy(k):
-        peer = turn_of(me, k)
-        return remote(packed.at[peer], got_ref.at[me], send.at[k], recv.at[k], {"wide": peer})
-
-    @pl.loop(1, WIDE)
-    def _(k):
-        gather_bucket(0, lambda s: code_ref[s] >> 1, wide, staged, packed, turn_of(me, k))
-        rows_copy(k).start()
-
-    gather_bucket(0, lambda s: code_ref[s] >> 1, wide, staged, packed, me)
-    last = pltpu.make_async_copy(packed.at[me], got_ref.at[me], own)
-    last.start()
-    last.wait()
-
-    @pl.loop(1, WIDE)
-    def _(k):
-        rows_copy(k).wait()
-
-
-def return_rows(codes, turned, lifted, collective):
-    return pl.pallas_call(
-        return_kernel,
-        out_shape=shape((WIDE, CAP, LOCAL), BF16),
-        in_specs=[SMEM, VMEM, VMEM],
-        out_specs=ANY,
-        scratch_shapes=[
-            pltpu.VMEM((ROWS + 8, LOCAL), F32),
-            pltpu.VMEM((1, CAP, LOCAL), F32),
-            pltpu.VMEM((WIDE, CAP, LOCAL), BF16),
-            pltpu.SemaphoreType.DMA((WIDE,)),
-            pltpu.SemaphoreType.DMA((WIDE,)),
-            pltpu.SemaphoreType.DMA,
-        ],
-        compiler_params=params(collective),
-    )(codes, turned, lifted)
-
-
 SCALE = 0.125 * 1.4426950408889634
 
 
@@ -540,8 +500,9 @@
 
 
 def middle_kernel(
-    slot_ref, got_ref, mask_ref, keep_ref, qkv_hbm, out_hbm, gate_up_hbm, down_hbm, coarse_hbm,
-    lift_hbm, turned_ref, lifted_ref,
+    slot_ref, code_ref, got_ref, mask_ref, keep_ref, qkv_hbm, out_hbm, gate_up_hbm, down_hbm, coarse_hbm,
+    lift_hbm, back_ref,
+    turned_ref, lifted_ref, outgoing, r_sem,
     wide, staged, packed, x, state, pooled, tiles, one, two, mate_one, mate_two, mate_keep,
     mixed, all_mixed, lifted, keys_one, values_one, keys_two, values_two, qkv_ref, out_ref, gate_up_ref, down_ref, w_ref, lift_ref,
     x_sem, p_sem, e_sem, k_sem, m_sem, t_sem, l_sem, g_sem, b_sem, f_sem, own, loads,
@@ -554,17 +515,15 @@
         pl.semaphore_signal(
             barrier, inc=1, device_id={"mp": lax.rem(mp + k, MP)}, device_id_type=MESH
         )
-    for other in (others[0], others[2]):
-        pl.semaphore_signal(barrier, inc=1, device_id={"wide": other}, device_id_type=MESH)
+
+    @pl.loop(1, WIDE)
+    def _(k):
+        pl.semaphore_signal(
+            barrier, inc=1, device_id={"wide": lax.rem(me + k, WIDE)}, device_id_type=MESH
+        )
 
     def chip(i):
         return 2 * lax.rem(i * 7, WIDE // 2)
-
-    @pl.loop(1, WIDE // 2)
-    def _(i):
-        pl.semaphore_signal(
-            barrier, inc=1, device_id={"wide": lax.rem(me + chip(i), WIDE)}, device_id_type=MESH
-        )
 
     load = [
         pltpu.make_async_copy(src, dst, loads.at[j])
@@ -580,7 +539,7 @@
     for copy in load:
         copy.start()
     widen(got_ref, wide, SLOTS)
-    pl.semaphore_wait(barrier, MP - 1 + 2 + WIDE // 2 - 1)
+    pl.semaphore_wait(barrier, MP - 1 + WIDE - 1)
 
     def rows(t, size):
         return pl.ds(pl.multiple_of(t * size, size), size)
@@ -621,14 +580,27 @@
             packed.at[mp * BALLS + t], x.at[rows(t, BALL), cols(mp)], own.at[0, t]
         )
 
-    @pl.loop(0, BALLS)
-    def _(t):
+    def send_ball(t):
         for k in (2, 1, 3):
             gather_bucket(0, lambda s: slot_ref[s], wide, staged, packed, peer(k) * BALLS + t)
             turn(k, t).start()
         gather_bucket(0, lambda s: slot_ref[s], wide, staged, packed, mp * BALLS + t)
         keep_turn(t).start()
 
+    send_ball(0)
+    for k in (1, 3, 2):
+        fetch(k).wait_recv()
+
+    @pl.loop(1, WIDE // 2)
+    def _(i):
+        broadcast(i).start()
+
+    pass_on(0).start()
+
+    @pl.loop(1, BALLS)
+    def _(t):
+        send_ball(t)
+
     def flags(j):
         return remote(
             keep_ref, mate_keep.at[j], k_sem.at[0, j], k_sem.at[1, j], {"wide": others[j]}
@@ -636,14 +608,6 @@
 
     for j in range(3):
         flags(j).start()
-    for k in (1, 3, 2):
-        fetch(k).wait_recv()
-
-    @pl.loop(1, WIDE // 2)
-    def _(i):
-        broadcast(i).start()
-
-    pass_on(0).start()
     load[0].wait()
     load[1].wait()
 
@@ -857,11 +821,13 @@
             lifted[ball, at, :] = total[ball * size : (ball + 1) * size]
 
     def rise(k):
-        return to_mp(lifted.at[:, :, cols(peer(k))], lifted_ref.at[mp], l_sem, k, 0)
+        return to_mp(lifted.at[:, :, cols(peer(k))], lifted_ref.at[pl.ds(mp * BALLS, BALLS)], l_sem, k, 0)
 
     for k in (2, 1, 3):
         rise(k).start()
-    keep_rise = pltpu.make_async_copy(lifted.at[:, :, cols(mp)], lifted_ref.at[mp], own.at[3, 0])
+    keep_rise = pltpu.make_async_copy(
+        lifted.at[:, :, cols(mp)], lifted_ref.at[pl.ds(mp * BALLS, BALLS)], own.at[3, 0]
+    )
     keep_rise.start()
 
     @pl.loop(0, BALLS)
@@ -886,15 +852,50 @@
     for k in (1, 3, 2):
         rise(k).wait()
 
-
-def middle(slots, got, mask, keep, weights, collective):
+    runs = run_matrix(
+        lax.broadcasted_iota(I32, (BALL, 96), 0), lax.broadcasted_iota(I32, (BALL, 96), 1)
+    )
+
+    @pl.loop(0, ROWS // BALL)
+    def _(i):
+        at = rows(i, BALL)
+        wide[at, :] = turned_ref[at, :].astype(F32) + dot(runs, lifted_ref[i])
+
+    wide[ROWS : ROWS + 8, :] = jnp.zeros((8, LOCAL), F32)
+
+    def rows_copy(k):
+        to = turn_of(me, k)
+        return remote(
+            outgoing.at[to], back_ref.at[me], r_sem.at[0, k], r_sem.at[1, k], {"wide": to}
+        )
+
+    @pl.loop(1, WIDE)
+    def _(k):
+        gather_bucket(0, lambda s: code_ref[s] >> 1, wide, staged, outgoing, turn_of(me, k))
+        rows_copy(k).start()
+
+    gather_bucket(0, lambda s: code_ref[s] >> 1, wide, staged, outgoing, me)
+    last = pltpu.make_async_copy(outgoing.at[me], back_ref.at[me], own.at[3, 1])
+    last.start()
+    last.wait()
+
+    @pl.loop(1, WIDE)
+    def _(k):
+        rows_copy(k).wait()
+
+
+def middle(slots, codes, got, mask, keep, weights, collective):
     dma = pltpu.SemaphoreType.DMA
     return pl.pallas_call(
         middle_kernel,
-        out_shape=[shape((ROWS, LOCAL), BF16), shape((MP, BALLS, 96, LOCAL), BF16)],
-        in_specs=[SMEM, VMEM, VMEM, VMEM] + [ANY] * 6,
-        out_specs=[ANY, ANY],
+        out_shape=shape((WIDE, CAP, LOCAL), BF16),
+        in_specs=[SMEM, SMEM, VMEM, VMEM, VMEM] + [ANY] * 6,
+        out_specs=ANY,
         scratch_shapes=[
+            pltpu.VMEM((ROWS, LOCAL), BF16),
+            pltpu.VMEM((MP * BALLS, 96, LOCAL), BF16),
+            pltpu.VMEM((WIDE, CAP, LOCAL), BF16),
+            dma((2, WIDE)),
             pltpu.VMEM((SLOTS, LOCAL), F32),
             pltpu.VMEM((1, CAP, LOCAL), F32),
             pltpu.VMEM((MP * BALLS, BALL, LOCAL), BF16),
@@ -934,7 +935,7 @@
             dma((6,)),
         ],
         compiler_params=params(collective),
-    )(slots, got, mask, keep, *weights)
+    )(slots, codes, got, mask, keep, *weights)
 
 
 def on_device(points, mask, perm, w_qkv, w_out, w_gate_up, w_down, w_coarse, w_coarse_out):
@@ -954,18 +955,22 @@
     full_qkv = full_qkv.reshape(3, WIDTH, WIDTH)
     full_out = full_out.reshape(WIDTH, WIDTH)
     own_gate_up = w_gate_up.reshape(2 * WIDTH, WIDTH)
-    turned, lifted = middle(
-        landed.reshape(ROWS), got.reshape(SLOTS, LOCAL), owned_mask, keep,
+    returned = middle(
+        landed.reshape(ROWS), got_code.reshape(SLOTS), got.reshape(SLOTS, LOCAL), owned_mask, keep,
         [full_qkv, full_out, own_gate_up, full_down, w_coarse, full_lift], 2,
     )
-    lifted = lifted.reshape(MP * BALLS, 96, LOCAL)
-    returned = return_rows(got_code.reshape(SLOTS), turned, lifted, 3)
     return pl.pallas_call(
         finish_kernel,
         out_shape=shape((ROWS, LOCAL), F32),
-        in_specs=[SMEM, VMEM],
-        out_specs=VMEM,
-        scratch_shapes=[pltpu.VMEM((SLOTS, LOCAL), F32)],
+        in_specs=[SMEM, ANY],
+        out_specs=ANY,
+        scratch_shapes=[
+            pltpu.VMEM((SLOTS, LOCAL), BF16),
+            pltpu.VMEM((SLOTS, LOCAL), F32),
+            pltpu.VMEM((ROWS, LOCAL), F32),
+            pltpu.SemaphoreType.DMA((SLOTS // 1024,)),
+            pltpu.SemaphoreType.DMA((ROWS // 512,)),
+        ],
         compiler_params=params(),
     )(slot.reshape(ROWS), returned.reshape(SLOTS, LOCAL))
 

time: 150 us -> 148 us (0.987)
  Pallas kernels: 149 us -> 147 us
    pallas_call x2 -> x1, Pallas kernels: 99.2 us -> 96.9 us  [middle(): pl.pallas_call(middle_kernel, out_shape=shape((WIDE, CAP, LOCAL), BF16),...]
where the time goes in v8:
time: 148 us; the launch traced here: 147 us
  Pallas kernels  147 us (99%)
    pallas_call x1, Pallas kernels, middle(): pl.pallas_call(middle_kernel, out_shape=shape((WIDE, CAP, LOCAL), BF16),...  96.9 us
    pallas_call x1, Pallas kernels, send_rows(): pl.pallas_call(send_kernel, out_shape=[shape((WIDE, CAP, LOCAL), BF16), s...  38.8 us
    pallas_call x1, Pallas kernels, on_device(): pl.pallas_call(finish_kernel, out_shape=shape((ROWS, LOCAL), F32), in_spe...  7.25 us
    pallas_call x1, Pallas kernels, index(): pl.pallas_call(index_kernel, out_shape=[shape((32, 128), I32), shape((WID...  4.17 us

profile of v8, /device:TPU:1, one launch (start us, length us, event | category | flops | bytes accessed | tf_op | source)
XLA Modules:
  0.0 147.3 jit_solution(16232734597232469171)
XLA Ops:
  0.0 4.2 %shard_map.91 = (s32[32,128]{1,0:T(8,128)}, s32[32,2,128]{2,1,0:T(2,128)}, s32[32,2,128]{2,1,0:T(2,128)}) custom-call(s32[32,128]{1,0:T(8,128)} %bitcast.24, s32[32,128]{1,0:T(8,128)} %bitcast.25), custom_call_target="tpu_custom_call" | custom-call | tf_op jit(solution)/shard_map/pallas_call | solution.py:95
  4.2 38.8 %shard_map.92 = (bf16[32,256,128]{2,1,0:T(8,128)(2,1)}, s32[32,2,128]{2,1,0:T(2,128)}, s32[16,2,128]{2,1,0:T(2,128)}, s32[16,256]{1,0:T(8,128)}, s32[12,128]{1,0...) custom-call(s32[8192]{0:T(1024)} %bitcast.20, ...), custom_call_target="tpu_custom_call" | custom-call | tf_op jit(solution)/shard_map/pallas_call | solution.py:355
  43.0 96.9 %shard_map.93 = bf16[32,256,128]{2,1,0:T(8,128)(2,1)} custom-call(s32[4096]{0:T(1024)} %bitcast.23, s32[8192]{0:T(1024)} %bitcast.21, bf16[8192,128]{1,0:T(8,128)(2,1)} %bitcast.14, s32[16,256]{1,0:T(8,128)} %get-tuple-element.23.mask_ref, s32[12,128]{1,0:T(8,128)} %get-tuple-element.24.keep_ref, bf16[3,512,512]{2,1,0:T(8,128)(2,1)} %bitcast.15, ...), custom_call_target="tpu_custom_call" | custom-call | tf_op jit(solution)/shard_map/pallas_call | solution.py:889
  139.9 7.2 %shard_map.94 = f32[4096,128]{1,0:T(8,128)} custom-call(s32[4096]{0:T(1024)} %bitcast.22, bf16[8192,128]{1,0:T(8,128)(2,1)} %bitcast.13), custom_call_target="tpu_custom_call" | custom-call | tf_op jit(solution)/shard_map/pallas_call | solution.py:962

commit v9 on v8

--- a/solution.py
+++ b/solution.py
@@ -205,8 +205,9 @@
 
 
 def send_kernel(
-    source_ref, points_ref, codes_ref, qkv_ref, out_ref, lift_ref, down_ref,
+    source_ref, points_ref, codes_ref, qkv_ref, out_ref, lift_ref, down_ref, gate_ref,
     got_ref, got_codes_out, slot_ref, mask_ref, keep_ref, all_qkv, all_out, all_lift, all_down,
+    all_gate,
     got_codes_ref, wide, staged, packed, send, recv, own, w_send, w_recv, w_own,
 ):
     me = lax.axis_index("wide")
@@ -234,11 +235,11 @@
         def cut(j, ref, shard):
             if j == 0:
                 return ref.at[rows(ref, 384), pl.ds(pl.multiple_of(shard * 128, 128), 128)]
-            quarter = (0, 32, 64, 128)[j]
+            quarter = (0, 32, 64, 128, 128)[j]
             return ref.at[shard, rows(ref, quarter), :]
 
         def own_cut(j, ref):
-            quarter = (384, 32, 64, 128)[j]
+            quarter = (384, 32, 64, 128, 128)[j]
             return ref.at[rows(ref, quarter), :]
 
         return cut, own_cut
@@ -247,8 +248,8 @@
     first, _ = part(2 * core, 1)
     second, _ = part(2 * core + 1, 1)
     every, own_every = part(0, 4)
-    shards = [qkv_ref, out_ref, lift_ref, down_ref]
-    full = [all_qkv, all_out, all_lift, all_down]
+    shards = [qkv_ref, out_ref, lift_ref, down_ref, gate_ref]
+    full = [all_qkv, all_out, all_lift, all_down, all_gate]
     count = len(shards)
 
     def weight(j, kind, cut, src, shard, device):
@@ -364,9 +365,10 @@
             shape((MP, LOCAL, WIDTH), BF16),
             shape((MP, 2 * LOCAL, WIDTH), BF16),
             shape((MP, WIDTH, WIDTH), BF16),
+            shape((MP, WIDTH, WIDTH), BF16),
         ],
-        in_specs=[SMEM, VMEM, ANY] + [VMEM] * 4,
-        out_specs=[ANY] + [VMEM] * 4 + [ANY] * 4,
+        in_specs=[SMEM, VMEM, ANY] + [VMEM] * 5,
+        out_specs=[ANY] + [VMEM] * 4 + [ANY] * 5,
         scratch_shapes=[
             pltpu.VMEM((WIDE, 2, 128), I32),
             pltpu.VMEM((ROWS, LOCAL), F32),
@@ -375,9 +377,9 @@
             pltpu.SemaphoreType.DMA((WIDE, 2)),
             pltpu.SemaphoreType.DMA((WIDE, 2)),
             pltpu.SemaphoreType.DMA((2,)),
-            pltpu.SemaphoreType.DMA((4, 8)),
-            pltpu.SemaphoreType.DMA((4, 8)),
-            pltpu.SemaphoreType.DMA((4,)),
+            pltpu.SemaphoreType.DMA((5, 8)),
+            pltpu.SemaphoreType.DMA((5, 8)),
+            pltpu.SemaphoreType.DMA((5,)),
         ],
         compiler_params=params(collective),
     )(source, points, codes, *weights)
@@ -479,14 +481,15 @@
 BALLS = QUARTER // BALL
 
 
-def forward_tile(state, mp, gate_up_ref, down_ref):
+def forward_tile(state, mp, gate_ref, up_ref, down_ref):
     normed = norm(state).astype(BF16)
     total = state
     for c in range(MP):
-        half = dot(normed, gate_up_ref[c, :WIDTH, :]) * 0.5
-        up = dot(normed, gate_up_ref[c, WIDTH:, :])
+        shard = lax.rem(mp + c, MP)
+        half = dot(normed, gate_ref[shard]) * 0.5
+        up = dot(normed, up_ref[c])
         activated = ((half + half * jnp.tanh(half)) * up).astype(BF16)
-        total = total + dot(activated, down_ref[lax.rem(mp + c, MP)])
+        total = total + dot(activated, down_ref[shard])
     return total
 
 
@@ -500,11 +503,11 @@
 
 
 def middle_kernel(
-    slot_ref, code_ref, got_ref, mask_ref, keep_ref, qkv_hbm, out_hbm, gate_up_hbm, down_hbm, coarse_hbm,
+    slot_ref, code_ref, got_ref, mask_ref, keep_ref, qkv_hbm, out_hbm, gate_up_hbm, gate_hbm, down_hbm, coarse_hbm,
     lift_hbm, back_ref,
     turned_ref, lifted_ref, outgoing, r_sem,
     wide, staged, packed, x, state, pooled, tiles, one, two, mate_one, mate_two, mate_keep,
-    mixed, all_mixed, lifted, keys_one, values_one, keys_two, values_two, qkv_ref, out_ref, gate_up_ref, down_ref, w_ref, lift_ref,
+    mixed, all_mixed, lifted, keys_one, values_one, keys_two, values_two, qkv_ref, out_ref, gate_ref, up_ref, down_ref, w_ref, lift_ref,
     x_sem, p_sem, e_sem, k_sem, m_sem, t_sem, l_sem, g_sem, b_sem, f_sem, own, loads,
 ):
     me = lax.axis_index("wide")
@@ -530,10 +533,11 @@
         for j, (src, dst) in enumerate([
             (qkv_hbm, qkv_ref),
             (out_hbm, out_ref),
-            (gate_up_hbm, gate_up_ref.at[0]),
+            (gate_up_hbm.at[pl.ds(WIDTH, WIDTH), :], up_ref.at[0]),
             (down_hbm, down_ref),
             (coarse_hbm, w_ref),
             (lift_hbm, lift_ref),
+            (gate_hbm, gate_ref),
         ])
     ]
     for copy in load:
@@ -554,10 +558,10 @@
         return remote(src, dst, sem.at[0, k, t], sem.at[1, k, t], {"mp": peer(k)})
 
     def piece(shards, owner):
-        return gate_up_ref.at[shards, pl.ds(pl.multiple_of(owner * 32, 32), 32), :]
+        return up_ref.at[shards, pl.ds(pl.multiple_of(owner * 16, 16), 16), :]
 
     def fetch(k):
-        src = gate_up_hbm.at[pl.ds(pl.multiple_of(me * 32, 32), 32), :]
+        src = gate_up_hbm.at[pl.ds(pl.multiple_of(WIDTH + me * 16, 16), 16), :]
         return to_mp(src, piece(MP - k, me), g_sem, k, 0)
 
     def broadcast(i):
@@ -628,6 +632,7 @@
 
     load[2].wait()
     load[3].wait()
+    load[6].wait()
 
     def give(k, t):
         return to_mp(
@@ -647,7 +652,7 @@
 
     def feed(t, count):
         at = pl.ds(t * BALL, count * BALL)
-        tiles[at, :] = forward_tile(state[at, :], mp, gate_up_ref, down_ref).astype(BF16)
+        tiles[at, :] = forward_tile(state[at, :], mp, gate_ref, up_ref, down_ref).astype(BF16)
         for u in range(t, t + count):
             for k in (2, 1, 3):
                 give(k, u).start()
@@ -657,6 +662,12 @@
     def _(i):
         broadcast(i).wait_recv()
         pass_on(i).start()
+
+    @pl.loop(0, WIDE // 2)
+    def _(i):
+        pass_on(i).wait_recv()
+
+    feed(0, 2)
 
     def pass_one(q):
         return remote(
@@ -711,11 +722,6 @@
 
         project(peer(k))
 
-    @pl.loop(0, WIDE // 2)
-    def _(i):
-        pass_on(i).wait_recv()
-
-    feed(0, 2)
     feed(2, 1)
 
     def hand_to(q, k, level):
@@ -889,7 +895,7 @@
     return pl.pallas_call(
         middle_kernel,
         out_shape=shape((WIDE, CAP, LOCAL), BF16),
-        in_specs=[SMEM, SMEM, VMEM, VMEM, VMEM] + [ANY] * 6,
+        in_specs=[SMEM, SMEM, VMEM, VMEM, VMEM] + [ANY] * 7,
         out_specs=ANY,
         scratch_shapes=[
             pltpu.VMEM((ROWS, LOCAL), BF16),
@@ -917,7 +923,8 @@
             pltpu.VMEM((2, 16 * TWO, LOCAL), BF16),
             pltpu.VMEM((3, WIDTH, WIDTH), BF16),
             pltpu.VMEM((WIDTH, WIDTH), BF16),
-            pltpu.VMEM((MP, 2 * WIDTH, WIDTH), BF16),
+            pltpu.VMEM((MP, WIDTH, WIDTH), BF16),
+            pltpu.VMEM((MP, WIDTH, WIDTH), BF16),
             pltpu.VMEM((MP, WIDTH, WIDTH), BF16),
             pltpu.VMEM((2, 3, WIDTH, LOCAL), BF16),
             pltpu.VMEM((MP, 2 * LOCAL, WIDTH), BF16),
@@ -932,7 +939,7 @@
             dma((2, WIDE // 2)),
             dma((2, WIDE // 2)),
             dma((4, BALLS)),
-            dma((6,)),
+            dma((7,)),
         ],
         compiler_params=params(collective),
     )(slots, codes, got, mask, keep, *weights)
@@ -940,24 +947,27 @@
 
 def on_device(points, mask, perm, w_qkv, w_out, w_gate_up, w_down, w_coarse, w_coarse_out):
     slot, source, codes = index(perm, mask)
-    got, got_code, landed, owned_mask, keep, full_qkv, full_out, full_lift, full_down = send_rows(
-        source.reshape(SLOTS),
-        points,
-        codes,
-        [
-            w_qkv.reshape(3 * WIDTH, LOCAL),
-            w_out,
-            w_coarse_out.reshape(2 * LOCAL, WIDTH),
-            w_down,
-        ],
-        1,
+    own_gate_up = w_gate_up.reshape(2 * WIDTH, WIDTH)
+    got, got_code, landed, owned_mask, keep, full_qkv, full_out, full_lift, full_down, full_gate = (
+        send_rows(
+            source.reshape(SLOTS),
+            points,
+            codes,
+            [
+                w_qkv.reshape(3 * WIDTH, LOCAL),
+                w_out,
+                w_coarse_out.reshape(2 * LOCAL, WIDTH),
+                w_down,
+                own_gate_up,
+            ],
+            1,
+        )
     )
     full_qkv = full_qkv.reshape(3, WIDTH, WIDTH)
     full_out = full_out.reshape(WIDTH, WIDTH)
-    own_gate_up = w_gate_up.reshape(2 * WIDTH, WIDTH)
     returned = middle(
         landed.reshape(ROWS), got_code.reshape(SLOTS), got.reshape(SLOTS, LOCAL), owned_mask, keep,
-        [full_qkv, full_out, own_gate_up, full_down, w_coarse, full_lift], 2,
+        [full_qkv, full_out, own_gate_up, full_gate, full_down, w_coarse, full_lift], 2,
     )
     return pl.pallas_call(
         finish_kernel,

time: 148 us -> 151 us (1.020)
  Pallas kernels: 147 us -> 150 us
    pallas_call x1, Pallas kernels: 38.8 us -> 47.7 us  [send_rows(): pl.pallas_call(send_kernel, out_shape=[shape((WIDE, CAP, LOCAL), BF16), s...]
    pallas_call x1, Pallas kernels: 96.9 us -> 91.3 us  [middle(): pl.pallas_call(middle_kernel, out_shape=shape((WIDE, CAP, LOCAL), BF16),...]
where the time goes in v9:
time: 151 us
  Pallas kernels  150 us (99%)
    pallas_call x1, Pallas kernels, middle(): pl.pallas_call(middle_kernel, out_shape=shape((WIDE, CAP, LOCAL), BF16),...  91.3 us
    pallas_call x1, Pallas kernels, send_rows(): pl.pallas_call(send_kernel, out_shape=[shape((WIDE, CAP, LOCAL), BF16), s...  47.7 us
    pallas_call x1, Pallas kernels, on_device(): pl.pallas_call(finish_kernel, out_shape=shape((ROWS, LOCAL), F32), in_spe...  7.25 us
    pallas_call x1, Pallas kernels, index(): pl.pallas_call(index_kernel, out_shape=[shape((32, 128), I32), shape((WID...  4.16 us

profile of v9, /device:TPU:1, one launch (start us, length us, event | category | flops | bytes accessed | tf_op | source)
XLA Modules:
  0.0 150.5 jit_solution(15265287131372084698)
XLA Ops:
  0.0 4.2 %shard_map.91 = (s32[32,128]{1,0:T(8,128)}, s32[32,2,128]{2,1,0:T(2,128)}, s32[32,2,128]{2,1,0:T(2,128)}) custom-call(s32[32,128]{1,0:T(8,128)} %bitcast.25, s32[32,128]{1,0:T(8,128)} %bitcast.26), custom_call_target="tpu_custom_call" | custom-call | tf_op jit(solution)/shard_map/pallas_call | solution.py:95
  4.2 47.7 %shard_map.92 = (bf16[32,256,128]{2,1,0:T(8,128)(2,1)}, s32[32,2,128]{2,1,0:T(2,128)}, s32[16,2,128]{2,1,0:T(2,128)}, s32[16,256]{1,0:T(8,128)}, s32[12,128]{1,0...) custom-call(s32[8192]{0:T(1024)} %bitcast.21, ...), custom_call_target="tpu_custom_call" | custom-call | tf_op jit(solution)/shard_map/pallas_call | solution.py:356
  51.8 91.3 %shard_map.93 = bf16[32,256,128]{2,1,0:T(8,128)(2,1)} custom-call(s32[4096]{0:T(1024)} %bitcast.24, s32[8192]{0:T(1024)} %bitcast.22, bf16[8192,128]{1,0:T(8,128)(2,1)} %bitcast.16, s32[16,256]{1,0:T(8,128)} %get-tuple-element.24.mask_ref, s32[12,128]{1,0:T(8,128)} %get-tuple-element.25.keep_ref, bf16[3,512,512]{2,1,0:T(8,128)(2,1)} %bitcast.17, ...), custom_call_target="tpu_custom_call" | custom-call | tf_op jit(solution)/shard_map/pallas_call | solution.py:895
  143.1 7.2 %shard_map.94 = f32[4096,128]{1,0:T(8,128)} custom-call(s32[4096]{0:T(1024)} %bitcast.23, bf16[8192,128]{1,0:T(8,128)(2,1)} %bitcast.13), custom_call_target="tpu_custom_call" | custom-call | tf_op jit(solution)/shard_map/pallas_call | solution.py:972

commit v10 on v9

--- a/solution.py
+++ b/solution.py
@@ -205,9 +205,8 @@
 
 
 def send_kernel(
-    source_ref, points_ref, codes_ref, qkv_ref, out_ref, lift_ref, down_ref, gate_ref,
-    got_ref, got_codes_out, slot_ref, mask_ref, keep_ref, all_qkv, all_out, all_lift, all_down,
-    all_gate,
+    source_ref, points_ref, codes_ref, qkv_ref, out_ref, down_ref, gate_ref,
+    got_ref, got_codes_out, slot_ref, mask_ref, keep_ref, all_qkv, all_out, all_down, all_gate,
     got_codes_ref, wide, staged, packed, send, recv, own, w_send, w_recv, w_own,
 ):
     me = lax.axis_index("wide")
@@ -235,11 +234,11 @@
         def cut(j, ref, shard):
             if j == 0:
                 return ref.at[rows(ref, 384), pl.ds(pl.multiple_of(shard * 128, 128), 128)]
-            quarter = (0, 32, 64, 128, 128)[j]
+            quarter = (0, 32, 128, 128)[j]
             return ref.at[shard, rows(ref, quarter), :]
 
         def own_cut(j, ref):
-            quarter = (384, 32, 64, 128, 128)[j]
+            quarter = (384, 32, 128, 128)[j]
             return ref.at[rows(ref, quarter), :]
 
         return cut, own_cut
@@ -248,8 +247,8 @@
     first, _ = part(2 * core, 1)
     second, _ = part(2 * core + 1, 1)
     every, own_every = part(0, 4)
-    shards = [qkv_ref, out_ref, lift_ref, down_ref, gate_ref]
-    full = [all_qkv, all_out, all_lift, all_down, all_gate]
+    shards = [qkv_ref, out_ref, down_ref, gate_ref]
+    full = [all_qkv, all_out, all_down, all_gate]
     count = len(shards)
 
     def weight(j, kind, cut, src, shard, device):
@@ -325,8 +324,8 @@
         weights[j][3].wait_recv()
         weights[j][7].start()
 
-    forward(0)
-    forward(1)
+    for j in range(count):
+        forward(j)
     for copy in mine:
         copy.wait()
 
@@ -336,8 +335,6 @@
 
     invert(got_codes_ref, slot_ref, mask_ref, keep_ref)
     got_codes_out[...] = got_codes_ref[...]
-    for j in range(2, count):
-        forward(j)
     for j in range(count):
         forward_last(j)
 
@@ -363,12 +360,11 @@
             shape((12, 128), I32),
             shape((3 * WIDTH, WIDTH), BF16),
             shape((MP, LOCAL, WIDTH), BF16),
-            shape((MP, 2 * LOCAL, WIDTH), BF16),
             shape((MP, WIDTH, WIDTH), BF16),
             shape((MP, WIDTH, WIDTH), BF16),
         ],
-        in_specs=[SMEM, VMEM, ANY] + [VMEM] * 5,
-        out_specs=[ANY] + [VMEM] * 4 + [ANY] * 5,
+        in_specs=[SMEM, VMEM, ANY] + [VMEM] * 4,
+        out_specs=[ANY] + [VMEM] * 4 + [ANY] * 4,
         scratch_shapes=[
             pltpu.VMEM((WIDE, 2, 128), I32),
             pltpu.VMEM((ROWS, LOCAL), F32),
@@ -377,9 +373,9 @@
             pltpu.SemaphoreType.DMA((WIDE, 2)),
             pltpu.SemaphoreType.DMA((WIDE, 2)),
             pltpu.SemaphoreType.DMA((2,)),
-            pltpu.SemaphoreType.DMA((5, 8)),
-            pltpu.SemaphoreType.DMA((5, 8)),
-            pltpu.SemaphoreType.DMA((5,)),
+            pltpu.SemaphoreType.DMA((4, 8)),
+            pltpu.SemaphoreType.DMA((4, 8)),
+            pltpu.SemaphoreType.DMA((4,)),
         ],
         compiler_params=params(collective),
     )(source, points, codes, *weights)
@@ -536,7 +532,7 @@
             (gate_up_hbm.at[pl.ds(WIDTH, WIDTH), :], up_ref.at[0]),
             (down_hbm, down_ref),
             (coarse_hbm, w_ref),
-            (lift_hbm, lift_ref),
+            (lift_hbm, lift_ref.at[0]),
             (gate_hbm, gate_ref),
         ])
     ]
@@ -560,21 +556,45 @@
     def piece(shards, owner):
         return up_ref.at[shards, pl.ds(pl.multiple_of(owner * 16, 16), 16), :]
 
+    def lift_rows(owner):
+        return pl.ds(pl.multiple_of(owner // 2 * 16, 16), 16)
+
+    def lift_cols(owner):
+        return pl.ds(pl.multiple_of(lax.rem(owner, 2) * 256, 256), 256)
+
+    def lift_piece(shards, owner):
+        return lift_ref.at[shards, lift_rows(owner), lift_cols(owner)]
+
     def fetch(k):
         src = gate_up_hbm.at[pl.ds(pl.multiple_of(WIDTH + me * 16, 16), 16), :]
         return to_mp(src, piece(MP - k, me), g_sem, k, 0)
 
+    def fetch_lift(k):
+        src = lift_hbm.at[lift_rows(me), lift_cols(me)]
+        return to_mp(src, lift_piece(MP - k, me), g_sem, k, 1)
+
+    def spread_to(part, i, t):
+        to = {"wide": lax.rem(me + chip(i), WIDE)}
+        return remote(part, part, b_sem.at[0, i, t], b_sem.at[1, i, t], to)
+
     def broadcast(i):
-        part = piece(pl.ds(1, 3), me)
-        to = {"wide": lax.rem(me + chip(i), WIDE)}
-        return remote(part, part, b_sem.at[0, i], b_sem.at[1, i], to)
+        return spread_to(piece(pl.ds(1, 3), me), i, 0)
+
+    def broadcast_lift(i):
+        return spread_to(lift_piece(pl.ds(1, 3), me), i, 1)
+
+    def hand_over(part, i, t):
+        return remote(part, part, f_sem.at[0, i, t], f_sem.at[1, i, t], {"wide": others[0]})
 
     def pass_on(i):
-        part = piece(pl.ds(1, 3), lax.rem(me + WIDE - chip(i), WIDE))
-        return remote(part, part, f_sem.at[0, i], f_sem.at[1, i], {"wide": others[0]})
+        return hand_over(piece(pl.ds(1, 3), lax.rem(me + WIDE - chip(i), WIDE)), i, 0)
+
+    def pass_on_lift(i):
+        return hand_over(lift_piece(pl.ds(1, 3), lax.rem(me + WIDE - chip(i), WIDE)), i, 1)
 
     for k in (2, 1, 3):
         fetch(k).start()
+        fetch_lift(k).start()
 
     def turn(k, t):
         return to_mp(packed.at[peer(k) * BALLS + t], x.at[rows(t, BALL), cols(mp)], x_sem, k, t)
@@ -594,6 +614,7 @@
     send_ball(0)
     for k in (1, 3, 2):
         fetch(k).wait_recv()
+        fetch_lift(k).wait_recv()
 
     @pl.loop(1, WIDE // 2)
     def _(i):
@@ -604,6 +625,12 @@
     @pl.loop(1, BALLS)
     def _(t):
         send_ball(t)
+
+    @pl.loop(1, WIDE // 2)
+    def _(i):
+        broadcast_lift(i).start()
+
+    pass_on_lift(0).start()
 
     def flags(j):
         return remote(
@@ -724,6 +751,12 @@
 
     feed(2, 1)
 
+    @pl.loop(1, WIDE // 2)
+    def _(i):
+        broadcast_lift(i).wait_recv()
+        pass_on_lift(i).start()
+
+
     def hand_to(q, k, level):
         at = pl.ds(0, ONE) if level == 0 else pl.ds(ONE, TWO)
         return to_mp(mixed.at[q, at, :], all_mixed.at[at, cols(mp)], m_sem, k, level)
@@ -809,6 +842,11 @@
     feed(3, 1)
 
     load[5].wait()
+
+    @pl.loop(0, WIDE // 2)
+    def _(i):
+        pass_on_lift(i).wait_recv()
+
     for level in range(2):
         keep_hand(level).wait()
         for k in (1, 3, 2):
@@ -818,7 +856,7 @@
         total = jnp.zeros((size * BALLS, WIDTH), F32)
         for g in range(MP):
             total = total + dot(
-                all_mixed[span, g * LOCAL : (g + 1) * LOCAL],
+                all_mixed[span, cols(peer(g))],
                 lift_ref[g, level * LOCAL : (level + 1) * LOCAL, :],
             )
         total = total.astype(BF16)
@@ -847,13 +885,16 @@
     @pl.loop(1, WIDE // 2)
     def _(i):
         broadcast(i).wait_send()
+        broadcast_lift(i).wait_send()
 
     @pl.loop(0, WIDE // 2)
     def _(i):
         pass_on(i).wait_send()
+        pass_on_lift(i).wait_send()
 
     for k in (1, 3, 2):
         fetch(k).wait_send()
+        fetch_lift(k).wait_send()
     keep_rise.wait()
     for k in (1, 3, 2):
         rise(k).wait()
@@ -935,9 +976,9 @@
             dma((2, MP, 2)),
             dma((2, MP, BALLS)),
             dma((2, MP, 1)),
-            dma((2, MP, 1)),
-            dma((2, WIDE // 2)),
-            dma((2, WIDE // 2)),
+            dma((2, MP, 2)),
+            dma((2, WIDE // 2, 2)),
+            dma((2, WIDE // 2, 2)),
             dma((4, BALLS)),
             dma((7,)),
         ],
@@ -948,7 +989,8 @@
 def on_device(points, mask, perm, w_qkv, w_out, w_gate_up, w_down, w_coarse, w_coarse_out):
     slot, source, codes = index(perm, mask)
     own_gate_up = w_gate_up.reshape(2 * WIDTH, WIDTH)
-    got, got_code, landed, owned_mask, keep, full_qkv, full_out, full_lift, full_down, full_gate = (
+    own_lift = w_coarse_out.reshape(2 * LOCAL, WIDTH)
+    got, got_code, landed, owned_mask, keep, full_qkv, full_out, full_down, full_gate = (
         send_rows(
             source.reshape(SLOTS),
             points,
@@ -956,7 +998,6 @@
             [
                 w_qkv.reshape(3 * WIDTH, LOCAL),
                 w_out,
-                w_coarse_out.reshape(2 * LOCAL, WIDTH),
                 w_down,
                 own_gate_up,
             ],
@@ -967,7 +1008,7 @@
     full_out = full_out.reshape(WIDTH, WIDTH)
     returned = middle(
         landed.reshape(ROWS), got_code.reshape(SLOTS), got.reshape(SLOTS, LOCAL), owned_mask, keep,
-        [full_qkv, full_out, own_gate_up, full_gate, full_down, w_coarse, full_lift], 2,
+        [full_qkv, full_out, own_gate_up, full_gate, full_down, w_coarse, own_lift], 2,
     )
     return pl.pallas_call(
         finish_kernel,

time: 151 us -> 148 us (0.980)
  Pallas kernels: 150 us -> 148 us
    pallas_call x1, Pallas kernels: 47.7 us -> 43.2 us  [send_rows(): pl.pallas_call(send_kernel, out_shape=[shape((WIDE, CAP, LOCAL), BF16), s...]
    pallas_call x1, Pallas kernels: 91.3 us -> 93 us  [middle(): pl.pallas_call(middle_kernel, out_shape=shape((WIDE, CAP, LOCAL), BF16),...]
where the time goes in v10:
time: 148 us
  Pallas kernels  148 us (100%)
    pallas_call x1, Pallas kernels, middle(): pl.pallas_call(middle_kernel, out_shape=shape((WIDE, CAP, LOCAL), BF16),...  93 us
    pallas_call x1, Pallas kernels, send_rows(): pl.pallas_call(send_kernel, out_shape=[shape((WIDE, CAP, LOCAL), BF16), s...  43.2 us
    pallas_call x1, Pallas kernels, on_device(): pl.pallas_call(finish_kernel, out_shape=shape((ROWS, LOCAL), F32), in_spe...  7.25 us
    pallas_call x1, Pallas kernels, index(): pl.pallas_call(index_kernel, out_shape=[shape((32, 128), I32), shape((WID...  4.16 us

profile of v10, /device:TPU:1, one launch (start us, length us, event | category | flops | bytes accessed | tf_op | source)
XLA Modules:
  0.0 147.8 jit_solution(9714776170273308160)
XLA Ops:
  0.0 4.2 %shard_map.91 = (s32[32,128]{1,0:T(8,128)}, s32[32,2,128]{2,1,0:T(2,128)}, s32[32,2,128]{2,1,0:T(2,128)}) custom-call(s32[32,128]{1,0:T(8,128)} %bitcast.25, s32[32,128]{1,0:T(8,128)} %bitcast.26), custom_call_target="tpu_custom_call" | custom-call | tf_op jit(solution)/shard_map/pallas_call | solution.py:95
  4.2 43.2 %shard_map.92 = (bf16[32,256,128]{2,1,0:T(8,128)(2,1)}, s32[32,2,128]{2,1,0:T(2,128)}, s32[16,2,128]{2,1,0:T(2,128)}, s32[16,256]{1,0:T(8,128)}, s32[12,128]{1,0...) custom-call(s32[8192]{0:T(1024)} %bitcast.21, ...), custom_call_target="tpu_custom_call" | custom-call | tf_op jit(solution)/shard_map/pallas_call | solution.py:353
  47.4 93.0 %shard_map.93 = bf16[32,256,128]{2,1,0:T(8,128)(2,1)} custom-call(s32[4096]{0:T(1024)} %bitcast.24, s32[8192]{0:T(1024)} %bitcast.22, bf16[8192,128]{1,0:T(8,128)(2,1)} %bitcast.16, s32[16,256]{1,0:T(8,128)} %get-tuple-element.23.mask_ref, s32[12,128]{1,0:T(8,128)} %get-tuple-element.24.keep_ref, bf16[3,512,512]{2,1,0:T(8,128)(2,1)} %bitcast.17, ...), custom_call_target="tpu_custom_call" | custom-call | tf_op jit(solution)/shard_map/pallas_call | solution.py:936
  140.4 7.2 %shard_map.94 = f32[4096,128]{1,0:T(8,128)} custom-call(s32[4096]{0:T(1024)} %bitcast.23, bf16[8192,128]{1,0:T(8,128)(2,1)} %bitcast.13), custom_call_target="tpu_custom_call" | custom-call | tf_op jit(solution)/shard_map/pallas_call | solution.py:1013

commit v11 on v10

--- a/solution.py
+++ b/solution.py
@@ -878,36 +878,24 @@
     def _(t):
         keep_give(t).wait()
         for k in (1, 3, 2):
-            turn(k, t).wait_send()
-            share(k, t).wait_send()
-            give(k, t).wait()
-
-    @pl.loop(1, WIDE // 2)
-    def _(i):
-        broadcast(i).wait_send()
-        broadcast_lift(i).wait_send()
-
-    @pl.loop(0, WIDE // 2)
-    def _(i):
-        pass_on(i).wait_send()
-        pass_on_lift(i).wait_send()
-
-    for k in (1, 3, 2):
-        fetch(k).wait_send()
-        fetch_lift(k).wait_send()
-    keep_rise.wait()
-    for k in (1, 3, 2):
-        rise(k).wait()
+            give(k, t).wait_recv()
 
     runs = run_matrix(
         lax.broadcasted_iota(I32, (BALL, 96), 0), lax.broadcasted_iota(I32, (BALL, 96), 1)
     )
 
-    @pl.loop(0, ROWS // BALL)
-    def _(i):
-        at = rows(i, BALL)
-        wide[at, :] = turned_ref[at, :].astype(F32) + dot(runs, lifted_ref[i])
-
+    def update(q):
+        @pl.loop(0, BALLS)
+        def _(t):
+            i = q * BALLS + t
+            at = rows(i, BALL)
+            wide[at, :] = turned_ref[at, :].astype(F32) + dot(runs, lifted_ref[i])
+
+    keep_rise.wait()
+    update(mp)
+    for k in (1, 3, 2):
+        rise(k).wait_recv()
+        update(peer(MP - k))
     wide[ROWS : ROWS + 8, :] = jnp.zeros((8, LOCAL), F32)
 
     def rows_copy(k):
@@ -924,6 +912,28 @@
     gather_bucket(0, lambda s: code_ref[s] >> 1, wide, staged, outgoing, me)
     last = pltpu.make_async_copy(outgoing.at[me], back_ref.at[me], own.at[3, 1])
     last.start()
+
+    @pl.loop(0, BALLS)
+    def _(t):
+        for k in (1, 3, 2):
+            turn(k, t).wait_send()
+            share(k, t).wait_send()
+            give(k, t).wait_send()
+
+    @pl.loop(1, WIDE // 2)
+    def _(i):
+        broadcast(i).wait_send()
+        broadcast_lift(i).wait_send()
+
+    @pl.loop(0, WIDE // 2)
+    def _(i):
+        pass_on(i).wait_send()
+        pass_on_lift(i).wait_send()
+
+    for k in (1, 3, 2):
+        fetch(k).wait_send()
+        fetch_lift(k).wait_send()
+        rise(k).wait_send()
     last.wait()
 
     @pl.loop(1, WIDE)

time: 148 us -> 147 us (level)
  no operation moved by 1% of the time
where the time goes in v11:
time: 147 us
  Pallas kernels  147 us (100%)
    pallas_call x1, Pallas kernels, middle(): pl.pallas_call(middle_kernel, out_shape=shape((WIDE, CAP, LOCAL), BF16),...  92.2 us
    pallas_call x1, Pallas kernels, send_rows(): pl.pallas_call(send_kernel, out_shape=[shape((WIDE, CAP, LOCAL), BF16), s...  43.2 us
    pallas_call x1, Pallas kernels, on_device(): pl.pallas_call(finish_kernel, out_shape=shape((ROWS, LOCAL), F32), in_spe...  7.25 us
    pallas_call x1, Pallas kernels, index(): pl.pallas_call(index_kernel, out_shape=[shape((32, 128), I32), shape((WID...  4.16 us

profile of v11, /device:TPU:1, one launch (start us, length us, event | category | flops | bytes accessed | tf_op | source)
XLA Modules:
  0.0 147.0 jit_solution(17200391446585583406)
XLA Ops:
  0.0 4.2 %shard_map.91 = (s32[32,128]{1,0:T(8,128)}, s32[32,2,128]{2,1,0:T(2,128)}, s32[32,2,128]{2,1,0:T(2,128)}) custom-call(s32[32,128]{1,0:T(8,128)} %bitcast.25, s32[32,128]{1,0:T(8,128)} %bitcast.26), custom_call_target="tpu_custom_call" | custom-call | tf_op jit(solution)/shard_map/pallas_call | solution.py:95
  4.2 43.2 %shard_map.92 = (bf16[32,256,128]{2,1,0:T(8,128)(2,1)}, s32[32,2,128]{2,1,0:T(2,128)}, s32[16,2,128]{2,1,0:T(2,128)}, s32[16,256]{1,0:T(8,128)}, s32[12,128]{1,0...) custom-call(s32[8192]{0:T(1024)} %bitcast.21, ...), custom_call_target="tpu_custom_call" | custom-call | tf_op jit(solution)/shard_map/pallas_call | solution.py:353
  47.4 92.2 %shard_map.93 = bf16[32,256,128]{2,1,0:T(8,128)(2,1)} custom-call(s32[4096]{0:T(1024)} %bitcast.24, s32[8192]{0:T(1024)} %bitcast.22, bf16[8192,128]{1,0:T(8,128)(2,1)} %bitcast.16, s32[16,256]{1,0:T(8,128)} %get-tuple-element.23.mask_ref, s32[12,128]{1,0:T(8,128)} %get-tuple-element.24.keep_ref, bf16[3,512,512]{2,1,0:T(8,128)(2,1)} %bitcast.17, ...), custom_call_target="tpu_custom_call" | custom-call | tf_op jit(solution)/shard_map/pallas_call | solution.py:946
  139.6 7.2 %shard_map.94 = f32[4096,128]{1,0:T(8,128)} custom-call(s32[4096]{0:T(1024)} %bitcast.23, bf16[8192,128]{1,0:T(8,128)(2,1)} %bitcast.13), custom_call_target="tpu_custom_call" | custom-call | tf_op jit(solution)/shard_map/pallas_call | solution.py:1023

commit v12 on v11

--- a/solution.py
+++ b/solution.py
@@ -62,27 +62,29 @@
     perm = perm_ref[...]
     target = perm >> 12
     code = (perm & (ROWS - 1)) * 2 + mask_ref[...]
-    rows = lax.broadcasted_iota(I32, (CAP, 128), 0)
-    upper = jnp.where(
-        lax.broadcasted_iota(I32, (128, 128), 0) < lax.broadcasted_iota(I32, (128, 128), 1), 1.0, 0.0
-    ).astype(BF16)
-    which = lax.broadcasted_iota(I32, (WIDE, 128), 0)
-    lane = lax.broadcasted_iota(I32, (1, 128), 1).astype(F32)
+    rows = lax.broadcasted_iota(I32, (CAP, 256), 0)
+    upper = jnp.where(rows < lax.broadcasted_iota(I32, (256, 256), 1), 1.0, 0.0).astype(BF16)
+    which = lax.broadcasted_iota(I32, (WIDE, 256), 0)
+    lane = lax.broadcasted_iota(I32, (1, 256), 1).astype(F32)
     carry = jnp.zeros((WIDE, 1), F32)
     found = jnp.zeros((5 * WIDE, CAP), F32)
-    for c in range(ROWS // 128):
-        row = slice(c, c + 1)
-        hot = jnp.where(which == target[row, :], 1.0, 0.0)
+    for c in range(ROWS // 256):
+        first, second = slice(2 * c, 2 * c + 1), slice(2 * c + 1, 2 * c + 2)
+        goal = jnp.concatenate([target[first, :], target[second, :]], 1)
+        both = jnp.concatenate([code[first, :], code[second, :]], 1)
+        hot = jnp.where(which == goal, 1.0, 0.0)
         before = dot(hot.astype(BF16), upper) + carry
         rank = jnp.sum(hot * before, 0, keepdims=True).astype(I32)
-        slot_ref[row, :] = target[row, :] * CAP + rank
+        slot = goal * CAP + rank
+        slot_ref[first, :] = slot[:, :128]
+        slot_ref[second, :] = slot[:, 128:]
         carry = carry + jnp.sum(hot, 1, keepdims=True)
         placed = jnp.where(rows == rank, 1.0, 0.0).astype(BF16)
-        high = (code[row, :] >> 6).astype(F32)
-        low = (code[row, :] & 63).astype(F32)
+        high = (both >> 6).astype(F32)
+        low = (both & 63).astype(F32)
         values = jnp.concatenate([hot * lane, hot * float(c), hot * high, hot * low, hot], 0)
         found = found + dot_t(values.astype(BF16), placed)
-    source = (found[:WIDE] + found[WIDE : 2 * WIDE] * 128.0).astype(I32)
+    source = (found[:WIDE] + found[WIDE : 2 * WIDE] * 256.0).astype(I32)
     codes = (found[2 * WIDE : 3 * WIDE] * 64.0 + found[3 * WIDE : 4 * WIDE]).astype(I32)
     codes = jnp.where(found[4 * WIDE :] > 0.5, codes, NONE)
     for h in range(2):

time: 147 us -> 147 us (level)
  no operation moved by 1% of the time
where the time goes in v12:
time: 147 us; the launch traced here: 146 us
  Pallas kernels  146 us (99%)
    pallas_call x1, Pallas kernels, middle(): pl.pallas_call(middle_kernel, out_shape=shape((WIDE, CAP, LOCAL), BF16),...  92.2 us
    pallas_call x1, Pallas kernels, send_rows(): pl.pallas_call(send_kernel, out_shape=[shape((WIDE, CAP, LOCAL), BF16), s...  43.2 us
    pallas_call x1, Pallas kernels, on_device(): pl.pallas_call(finish_kernel, out_shape=shape((ROWS, LOCAL), F32), in_spe...  7.25 us
    pallas_call x1, Pallas kernels, index(): pl.pallas_call(index_kernel, out_shape=[shape((32, 128), I32), shape((WID...  3.41 us

profile of v12, /device:TPU:1, one launch (start us, length us, event | category | flops | bytes accessed | tf_op | source)
XLA Modules:
  0.0 146.3 jit_solution(2556808669745550942)
XLA Ops:
  0.0 3.4 %shard_map.91 = (s32[32,128]{1,0:T(8,128)}, s32[32,2,128]{2,1,0:T(2,128)}, s32[32,2,128]{2,1,0:T(2,128)}) custom-call(s32[32,128]{1,0:T(8,128)} %bitcast.25, s32[32,128]{1,0:T(8,128)} %bitcast.26), custom_call_target="tpu_custom_call" | custom-call | tf_op jit(solution)/shard_map/pallas_call | solution.py:97
  3.4 43.2 %shard_map.92 = (bf16[32,256,128]{2,1,0:T(8,128)(2,1)}, s32[32,2,128]{2,1,0:T(2,128)}, s32[16,2,128]{2,1,0:T(2,128)}, s32[16,256]{1,0:T(8,128)}, s32[12,128]{1,0...) custom-call(s32[8192]{0:T(1024)} %bitcast.21, ...), custom_call_target="tpu_custom_call" | custom-call | tf_op jit(solution)/shard_map/pallas_call | solution.py:355
  46.6 92.2 %shard_map.93 = bf16[32,256,128]{2,1,0:T(8,128)(2,1)} custom-call(s32[4096]{0:T(1024)} %bitcast.24, s32[8192]{0:T(1024)} %bitcast.22, bf16[8192,128]{1,0:T(8,128)(2,1)} %bitcast.16, s32[16,256]{1,0:T(8,128)} %get-tuple-element.23.mask_ref, s32[12,128]{1,0:T(8,128)} %get-tuple-element.24.keep_ref, bf16[3,512,512]{2,1,0:T(8,128)(2,1)} %bitcast.17, ...), custom_call_target="tpu_custom_call" | custom-call | tf_op jit(solution)/shard_map/pallas_call | solution.py:948
  138.9 7.2 %shard_map.94 = f32[4096,128]{1,0:T(8,128)} custom-call(s32[4096]{0:T(1024)} %bitcast.23, bf16[8192,128]{1,0:T(8,128)(2,1)} %bitcast.13), custom_call_target="tpu_custom_call" | custom-call | tf_op jit(solution)/shard_map/pallas_call | solution.py:1025
